TPU v7x, 128 devices: a whole 4x4x4 slice. The times are simulated.
128 devices in a mesh: expert: 64 (over z_hi, x, y, core), tensor: 2 (over z_lo).
Axes of the slice: x: 4, y: 4, z: 4 (z_hi: 2, z_lo: 2; z = z_hi * 2 + z_lo), core: 2. Of those that a mesh axis runs over, the one named last changes fastest.
Arguments:
- tokens: bfloat16 [32768, 768], P('expert'), may hold values from -6 to 6
- routes: int32 [32768, 2], P('expert'), may hold values from 0 to 15, all different within a row; in each aligned block of 512 rows (0 to 511, 512 to 1023, ...) at most 80 rows name the same one
- gain_one: float32 [768], replicated, may hold values from 0.5 to 1.5
- w_query: bfloat16 [768, 768], P(None, 'tensor'), may hold values from -0.21875 to 0.21875
- w_key: bfloat16 [768, 768], P(None, 'tensor'), may hold values from -0.21875 to 0.21875
- w_value: bfloat16 [768, 768], P(None, 'tensor'), may hold values from -0.21875 to 0.21875
- w_output: bfloat16 [768, 768], P('tensor'), may hold values from -3 to 3
- gain_two: float32 [768], replicated, may hold values from 0.5 to 1.5
- w_router: bfloat16 [768, 16], replicated, may hold values from -0.15625 to 0.15625
- shared_gate: bfloat16 [768, 2048], P(None, 'tensor'), may hold values from -0.21875 to 0.21875
- shared_up: bfloat16 [768, 2048], P(None, 'tensor'), may hold values from -0.21875 to 0.21875
- shared_down: bfloat16 [2048, 768], P('tensor'), may hold values from -0.125 to 0.125
- expert_gate: bfloat16 [64, 768, 512], P('expert', None, 'tensor'), may hold values from -0.21875 to 0.21875
- expert_up: bfloat16 [64, 768, 512], P('expert', None, 'tensor'), may hold values from -0.21875 to 0.21875
- expert_down: bfloat16 [64, 512, 768], P('expert', 'tensor'), may hold values from -0.125 to 0.125
- cotangent: bfloat16 [32768, 768], P('expert'), may hold values from -6 to 6
Outputs:
- block_out: bfloat16 [32768, 768], P('expert')
- grad_tokens: float32 [32768, 768], P('expert')
- grad_gain_one: float32 [768], replicated
- grad_w_query: float32 [768, 768], P(None, 'tensor')
- grad_w_key: float32 [768, 768], P(None, 'tensor')
- grad_w_value: float32 [768, 768], P(None, 'tensor')
- grad_w_output: float32 [768, 768], P('tensor')
- grad_gain_two: float32 [768], replicated
- grad_router: float32 [768, 16], replicated
- grad_shared_gate: float32 [768, 2048], P(None, 'tensor')
- grad_shared_up: float32 [768, 2048], P(None, 'tensor')
- grad_shared_down: float32 [2048, 768], P('tensor')
- grad_expert_gate: float32 [64, 768, 512], P('expert', None, 'tensor')
- grad_expert_up: float32 [64, 768, 512], P('expert', None, 'tensor')
- grad_expert_down: float32 [64, 512, 768], P('expert', 'tensor')
Inputs may be any that keep to these rules, and one draw needn't show every extreme that they name: `routes`: in each device's block of 512 rows no expert is named by more than 80 rows, a bound that some block reaches; the 2 entries of a row differ, and every expert is named somewhere.
All inputs are finite; a program needn't handle non-finite values.
Results may differ from a plain program's by a relative error of at most 0.02.
Values may be sent and summed in bfloat16 or wider, within the bound.
No kernel may reach another device: no remote copies, remote signals or barrier semaphores. Data moves between devices by JAX's collectives and lax.ppermute only.
A program may use at most 256 MiB of HBM per device.

v0:
```python
import functools

import jax
import jax.numpy as jnp
import numpy as np
from jax import lax
from jax.experimental import pallas as pl
from jax.experimental.pallas import tpu as pltpu
from jax.sharding import Mesh
from jax.sharding import PartitionSpec as P

HEAD_DIM = 64
BLOCK = 256
SLOTS = 40
PAIR = 128
AXES = ("zh", "x", "yh", "yl", "c", "t")
EXPERT = AXES[:5]
ROUTE = ("zh", "x", "yh")
PLANE = ("x", "yh", "yl")

epsilon = 1e-06
rope_base = 10000.0
bf16 = jnp.bfloat16
f32 = jnp.float32
params = pltpu.CompilerParams(vmem_limit_bytes=52 << 20)


def swap(x, axis):
    return lax.ppermute(x, axis, [(0, 1), (1, 0)])


def exchange(x, axis):
    return lax.all_to_all(x, axis, split_axis=0, concat_axis=0, tiled=True)


def after(x, first):
    return lax.optimization_barrier((x, first))[0]


def dot(a, b, dims=((1,), (0,))):
    return lax.dot_general(a, b, (dims, ((), ())), preferred_element_type=f32)


def dot_nt(a, b):
    return dot(a, b, ((1,), (1,)))


def dot_tn(a, b):
    return dot(a, b, ((0,), (0,)))


def rms_scale(values):
    return lax.rsqrt(jnp.mean(values * values, axis=-1, keepdims=True) + epsilon)


def pair_sum(values, axis):
    low = values.astype(bf16)
    return low.astype(f32) + swap(low, axis).astype(f32)


def norm_back(inputs, row_scale, gain_row, upstream):
    unit_rows = inputs * row_scale
    scaled_grad = upstream * gain_row
    return row_scale * (
        scaled_grad - unit_rows * jnp.mean(scaled_grad * unit_rows, axis=-1, keepdims=True)
    )


RATE = 230000000
TIMES = dict(
    route=4,
    project=5,
    attend=14,
    attend_back=23,
    second=4,
    shared=12,
    expert_rows=20,
    expert_given=9,
    expert_kept=9,
    expert_sum=4,
    expert_sums=3,
    expert_out=3,
    combine=4,
    back_two=4,
    normed_back=8,
    first=4,
    shared_weights=6,
    late_weights=8,
    early_out=5,
    turn_rows=3,
    half_sum=4,
    late_out=4,
)


def turn(values, cos, sin):
    half = HEAD_DIM // 2
    lanes = lax.broadcasted_iota(jnp.int32, values.shape, 1)
    first = (lanes // half) % 2 == 0
    size = values.shape[1]
    other = jnp.where(first, -pltpu.roll(values, size - half, 1), pltpu.roll(values, half, 1))
    return values * cos + other * sin


def whole(shape):
    return pl.BlockSpec(shape, lambda *_: (0,) * len(shape))


def call(kernel, name, args, outs, smem=(), grid=None, in_specs=None, out_specs=None, scratch=()):
    in_specs = dict(in_specs or {})
    out_specs = dict(out_specs or {})
    for i in smem:
        in_specs[i] = pl.BlockSpec(memory_space=pltpu.SMEM)
    return pl.pallas_call(
        kernel,
        **({} if grid is None else {"grid": grid}),
        in_specs=[in_specs.get(i, whole(a.shape)) for i, a in enumerate(args)],
        out_specs=[out_specs.get(i, whole(s)) for i, (s, _) in enumerate(outs)],
        out_shape=[jax.ShapeDtypeStruct(s, d) for s, d in outs],
        scratch_shapes=scratch,
        compiler_params=params,
        cost_estimate=pl.CostEstimate(flops=TIMES[name] * RATE, bytes_accessed=1 << 20, transcendentals=0),
        name=name,
    )(*args)


def lanes_of(rows=1, count=128):
    return lax.broadcasted_iota(jnp.int32, (rows, count), 1)


def route_kernel(tensor_ref, routes_ref, cot_ref, expand_ref, seat_ref, placer_ref, turned_ref, sent_ref):
    routes = routes_ref[...]
    rows, width = cot_ref.shape
    lanes = lanes_of(rows)
    member = (routes[:, 0:1] == lanes) | (routes[:, 1:2] == lanes)
    earlier = lax.broadcasted_iota(jnp.int32, (rows, rows), 0) > lanes_of(rows, rows)
    count = dot(
        jnp.where(earlier, 1.0, 0.0).astype(bf16), jnp.where(member, 1.0, 0.0).astype(bf16)
    )
    offset = (tensor_ref[0] * SLOTS).astype(f32)
    place = jnp.where(member, count - offset, -1.0).astype(bf16)
    placer = jnp.where(dot(place, expand_ref[...]) == seat_ref[...], 1.0, 0.0).astype(bf16)
    placer_ref[...] = placer
    turned = placer.T
    turned_ref[...] = turned
    sent_ref[:, :width] = dot(turned, cot_ref[...]).astype(bf16)
    sums = (routes[:, 0:1] + routes[:, 1:2]).astype(f32)
    sent_ref[:, width:] = dot(turned, jnp.where(lanes == 0, sums, 0.0).astype(bf16)).astype(bf16)


def route(tensor, routes, cotangent, experts):
    rows, width = cotangent.shape
    seats = experts * SLOTS
    columns = np.arange(seats)
    expand = jnp.asarray(np.arange(128)[:, None] == columns[None, :] // SLOTS, bf16)
    seat = jnp.asarray((columns % SLOTS)[None], f32)
    return call(
        route_kernel,
        "route",
        (tensor[None], routes, cotangent, expand, seat),
        [((rows, seats), bf16), ((seats, rows), bf16), ((seats, width + 128), bf16)],
        smem=(0,),
    )


def project_kernel(x0_ref, x1_ref, gain_ref, wk_ref, wv_ref, cos_ref, sin_ref, *rest):
    wq_ref = rest[0] if len(rest) == 5 else None
    n_ref, k_ref, v_ref = rest[-4:-1] if wq_ref is not None else rest
    for chunk, x_ref in enumerate((x0_ref, x1_ref)):
        rows = x_ref.shape[0]
        at_rows = slice(chunk * rows, (chunk + 1) * rows)
        x = x_ref[...].astype(f32)
        normed = (x * rms_scale(x) * gain_ref[...]).astype(bf16)
        n_ref[at_rows, :] = normed
        cos, sin = cos_ref[at_rows, :], sin_ref[at_rows, :]
        key = dot(normed, wk_ref[...])
        for at in range(0, key.shape[1], PAIR):
            lanes = slice(at, at + PAIR)
            k_ref[at_rows, lanes] = turn(key[:, lanes], cos, sin).astype(bf16)
        v_ref[at_rows, :] = dot(normed, wv_ref[...]).astype(bf16)
        if chunk == 0 and wq_ref is not None:
            q_ref = rest[-1]
            query = dot(normed, wq_ref[...])
            for at in range(0, query.shape[1], PAIR):
                lanes = slice(at, at + PAIR)
                turned = turn(query[:, lanes], cos, sin).astype(bf16)
                q_ref[:, lanes] = turned * (HEAD_DIM**-0.5)


def project(first, second, gain, w_key, w_value, cos, sin, w_query=None):
    rows, width = first.shape
    wide = w_key.shape[1]
    outs = [((2 * rows, width), bf16), ((2 * rows, wide), bf16), ((2 * rows, wide), bf16)]
    args = (first, second, gain, w_key, w_value, cos, sin)
    if w_query is not None:
        args += (w_query,)
        outs.append(((rows, wide), bf16))
    return call(project_kernel, "project", args, outs)


def attend_kernel(hide_ref, q_ref, ka_ref, va_ref, kb_ref, vb_ref, wo_ref, o_ref, lse_ref, part_ref, acc_ref):
    lanes = lanes_of()
    span = 2 * BLOCK
    step = pl.program_id(0)
    for half in range(2):
        rows = slice(half * BLOCK, (half + 1) * BLOCK)
        q = q_ref[rows, :]
        outs, logs = [], []
        for head in range(2):
            query = jnp.where(lanes // HEAD_DIM == head, q, jnp.zeros_like(q))
            spans = [(ka_ref, va_ref, 0, BLOCK * (half + 1), 0.0), (ka_ref, va_ref, span, span, hide_ref[1])]
            spans += [(kb_ref, vb_ref, 0, span, hide_ref[2]), (kb_ref, vb_ref, span, span, hide_ref[3])]
            scores = [dot_nt(query, k[a : a + n, :]) for k, _, a, n, _ in spans]
            tops = [jnp.max(s, axis=1, keepdims=True) - x[4] for s, x in zip(scores, spans)]
            top = functools.reduce(jnp.maximum, tops)
            total, acc = 0.0, 0.0
            for s, (_, v, a, n, off) in zip(scores, spans):
                p = jnp.exp(s - (top + off))
                total = total + jnp.sum(p, axis=1, keepdims=True)
                acc = acc + dot(p.astype(bf16), v[a : a + n, :])
            outs.append(acc / total)
            logs.append(top + jnp.log(total))
        mixed = jnp.where(lanes < HEAD_DIM, outs[0], outs[1]).astype(bf16)
        o_ref[rows, :] = mixed
        lse_ref[rows, :] = jnp.where(lanes < HEAD_DIM, logs[0], logs[1])
    part = dot(o_ref[...], wo_ref[...])

    @pl.when(step == 0)
    def _():
        acc_ref[...] = part

    @pl.when(step > 0)
    def _():
        acc_ref[...] += part

    @pl.when(step == pl.num_programs(0) - 1)
    def _():
        part_ref[...] = acc_ref[...].astype(bf16)


def attend(hide, q, ka, va, kb, vb, w_output):
    rows, keys = q.shape[0], ka.shape[0]
    width = w_output.shape[1]
    of_q = pl.BlockSpec((rows, PAIR), lambda p: (0, p))
    of_k = pl.BlockSpec((keys, PAIR), lambda p: (0, p))
    return call(
        attend_kernel,
        "attend",
        (hide, q, ka, va, kb, vb, w_output),
        [(q.shape, bf16), (q.shape, f32), ((rows, width), bf16)],
        smem=(0,),
        grid=(q.shape[1] // PAIR,),
        in_specs={1: of_q, 2: of_k, 3: of_k, 4: of_k, 5: of_k, 6: pl.BlockSpec((PAIR, width), lambda p: (p, 0))},
        out_specs={0: of_q, 1: of_q},
        scratch=[pltpu.VMEM((rows, width), f32)],
    )


def attend_back_kernel(
    hide_ref, q_ref, ka_ref, va_ref, kb_ref, vb_ref, o_ref, lse_ref, g_ref, ca_ref, sa_ref, cb_ref, sb_ref,
    dq_ref, dka_ref, dva_ref, dkb_ref, dvb_ref,
):
    lanes = lanes_of()
    q, g = q_ref[...], g_ref[...]
    rows = q.shape[0]
    deltas = (g.astype(f32) * o_ref[...].astype(f32)).T
    logs = lse_ref[...].T
    dq = 0.0
    near = (ka_ref, va_ref, ca_ref, sa_ref, dka_ref, dva_ref)
    far = (kb_ref, vb_ref, cb_ref, sb_ref, dkb_ref, dvb_ref)
    for block in range(8):
        k_ref, v_ref, cos_ref, sin_ref, dk_ref, dv_ref = near if block < 4 else far
        off = 0.0 if block < 2 else hide_ref[block // 2]
        first = BLOCK if block == 1 else 0
        keys = slice((block % 4) * BLOCK, (block % 4 + 1) * BLOCK)
        k, v = k_ref[keys, :], v_ref[keys, :]
        dk, dv = 0.0, 0.0
        for head in range(2):
            mine = lanes // HEAD_DIM == head
            low = head * HEAD_DIM
            query = jnp.where(mine, q[first:, :], jnp.zeros_like(q[first:, :]))
            grads = jnp.where(mine, g[first:, :], jnp.zeros_like(g[first:, :]))
            key = jnp.where(mine, k, jnp.zeros_like(k))
            log = logs[low : low + 1, first:] + off
            delta = jnp.sum(deltas[low : low + HEAD_DIM, first:], axis=0, keepdims=True)
            p = jnp.exp(dot_nt(k, query) - log)
            ds = (p * (dot_nt(v, grads) - delta)).astype(bf16)
            dv = dv + dot(p.astype(bf16), grads)
            dk = dk + dot(ds, query)
            part = dot_tn(ds, key)
            if first:
                part = jnp.concatenate([jnp.zeros((first, PAIR), f32), part], axis=0)
            dq = dq + part
        dv_ref[keys, :] = dv.astype(bf16)
        dk_ref[keys, :] = turn(dk, cos_ref[keys, :], -sin_ref[keys, :]).astype(bf16)
    dq = dq * (HEAD_DIM**-0.5)
    dq_ref[...] = turn(dq, ca_ref[:rows, :], -sa_ref[:rows, :]).astype(bf16)


def attend_back(hide, q, ka, va, kb, vb, o, lse, g, ca, sa, cb, sb):
    rows, keys = q.shape[0], ka.shape[0]
    of_q = pl.BlockSpec((rows, PAIR), lambda p: (0, p))
    of_k = pl.BlockSpec((keys, PAIR), lambda p: (0, p))
    return call(
        attend_back_kernel,
        "attend_back",
        (hide, q, ka, va, kb, vb, o, lse, g, ca, sa, cb, sb),
        [(q.shape, bf16)] + [(ka.shape, bf16)] * 4,
        smem=(0,),
        grid=(q.shape[1] // PAIR,),
        in_specs={1: of_q, 2: of_k, 3: of_k, 4: of_k, 5: of_k, 6: of_q, 7: of_q, 8: of_q},
        out_specs={0: of_q, 1: of_k, 2: of_k, 3: of_k, 4: of_k},
    )


def turn_rows_kernel(a_ref, b_ref, ta_ref, tb_ref):
    ta_ref[...] = a_ref[...].T
    tb_ref[...] = b_ref[...].T


def half_sum_kernel(kept_ref, taken_ref, out_ref):
    out_ref[...] = (kept_ref[...].astype(f32) + taken_ref[...].astype(f32)).astype(bf16)


def second_kernel(x_ref, mine_ref, theirs_ref, gain_ref, turned_ref, cot_ref, middle_ref, n_ref, sent_ref):
    middle = x_ref[...].astype(f32) + (mine_ref[...].astype(f32) + theirs_ref[...].astype(f32))
    middle_ref[...] = middle
    normed = (middle * rms_scale(middle) * gain_ref[...]).astype(bf16)
    n_ref[...] = normed
    width = normed.shape[1]
    sent_ref[:, :width] = dot(turned_ref[...], normed).astype(bf16)
    sent_ref[:, width:] = cot_ref[...]


def swish(gate, up, grads):
    sigmoid = jax.nn.sigmoid(gate)
    unit = gate * sigmoid
    slope = sigmoid + unit * (1.0 - sigmoid)
    return (unit * up).astype(bf16), (grads * up * slope).astype(bf16), (grads * unit).astype(bf16)


def shared_kernel(
    n_ref, cot_ref, sg_ref, su_ref, sd_ref, router_ref, routes_ref, h_ref, gg_ref, gu_ref, back_ref, out_ref, share_ref
):
    normed, cot = n_ref[...], cot_ref[...]
    sg, su, sd = sg_ref[...], su_ref[...], sd_ref[...]
    hidden, gg, gu = swish(dot(normed, sg), dot(normed, su), dot_nt(cot, sd))
    h_ref[...], gg_ref[...], gu_ref[...] = hidden, gg, gu
    back = dot_nt(gg, sg) + dot_nt(gu, su)
    out = dot(hidden, sd)

    @pl.when(pl.program_id(0) == 0)
    def _():
        back_ref[...] = back
        out_ref[...] = out
        logits = dot(normed, router_ref[...])
        routes = routes_ref[...]
        lanes = lanes_of()
        first, second = lanes == routes[:, 0:1], lanes == routes[:, 1:2]
        one = jnp.sum(jnp.where(first, logits, 0.0), axis=1, keepdims=True)
        two = jnp.sum(jnp.where(second, logits, 0.0), axis=1, keepdims=True)
        top = jnp.maximum(one, two)
        one, two = jnp.exp(one - top), jnp.exp(two - top)
        share_ref[...] = (jnp.where(first, one, 0.0) + jnp.where(second, two, 0.0)) / (one + two)

    @pl.when(pl.program_id(0) > 0)
    def _():
        back_ref[...] += back
        out_ref[...] += out


def shared(normed, cot, shared_gate, shared_up, shared_down, router, routes):
    rows, width = normed.shape
    hidden = shared_gate.shape[1]
    block = 256
    columns = pl.BlockSpec((width, block), lambda k: (0, k))
    of_hidden = pl.BlockSpec((rows, block), lambda k: (0, k))
    return call(
        shared_kernel,
        "shared",
        (normed, cot, shared_gate, shared_up, shared_down, router, routes),
        [((rows, hidden), bf16)] * 3 + [((rows, width), f32)] * 2 + [((rows, 128), f32)],
        grid=(hidden // block,),
        in_specs={2: columns, 3: columns, 4: pl.BlockSpec((block, width), lambda k: (k, 0))},
        out_specs={0: of_hidden, 1: of_hidden, 2: of_hidden},
    )


def store_half(given_ref, kept_ref, at, value):
    value = value.astype(bf16)

    @pl.when(pl.program_id(0) == 0)
    def _():
        given_ref[:, at : at + value.shape[1]] = value

    @pl.when(pl.program_id(0) == 1)
    def _():
        kept_ref[:, at : at + value.shape[1]] = value


def shared_weights_kernel(core_ref, n_ref, cot_ref, gg_ref, gu_ref, h_ref, given_ref, kept_ref):
    part = h_ref.shape[1]
    turned = n_ref[...].T
    store_half(given_ref, kept_ref, 0, dot(turned, gg_ref[...]))
    store_half(given_ref, kept_ref, part, dot(turned, gu_ref[...]))
    store_half(given_ref, kept_ref, 2 * part, dot(cot_ref[...].T, h_ref[...]))


def half_call(kernel, name, core, halved, full, columns, by_rows=()):
    half = halved[0].shape[1] // 2
    specs = [pl.BlockSpec((a.shape[0], half), lambda s, c: (0, jnp.where(s == 0, 1 - c[0], c[0]))) for a in halved]
    specs += [
        pl.BlockSpec((half, a.shape[1]), lambda s, c: (jnp.where(s == 0, 1 - c[0], c[0]), 0))
        for a in by_rows
    ]
    specs += [pl.BlockSpec(a.shape, lambda s, c: (0, 0)) for a in full]
    return pl.pallas_call(
        kernel,
        grid_spec=pltpu.PrefetchScalarGridSpec(
            num_scalar_prefetch=1,
            grid=(2,),
            in_specs=specs,
            out_specs=[pl.BlockSpec((half, c), lambda s, c: (0, 0)) for c in columns for _ in range(2)],
        ),
        out_shape=[jax.ShapeDtypeStruct((half, c), bf16) for c in columns for _ in range(2)],
        compiler_params=params,
        cost_estimate=pl.CostEstimate(flops=TIMES[name] * RATE, bytes_accessed=1 << 20, transcendentals=0),
        name=name,
    )(core[None], *halved, *by_rows, *full)


def late_weights_kernel(
    core_ref, n2_ref, low_ref, gain_ref, scale_ref, ta_ref, tb_ref, wq_ref, wk_ref, wv_ref,
    dq_ref, dka_ref, dkb_ref, dva_ref, dvb_ref, lg_ref, o_ref, given_ref, kept_ref, small_given_ref, small_kept_ref, *, experts
):
    def column(row_ref):
        return jnp.broadcast_to(row_ref[...], (128, row_ref.shape[1])).T

    wide = dq_ref.shape[1]
    rows = dq_ref.shape[0]
    ta, tb = ta_ref[...], tb_ref[...]
    grad_q = dot(ta[:, :rows], dq_ref[...])
    grad_k = dot(ta, dka_ref[...]) + dot(tb, dkb_ref[...])
    grad_v = dot(ta, dva_ref[...]) + dot(tb, dvb_ref[...])
    for i, value in enumerate((grad_q, grad_k, grad_v, dot(low_ref[...].T, o_ref[...]))):
        store_half(given_ref, kept_ref, i * wide, value)
    small = dot(n2_ref[...].T, lg_ref[...])
    terms = grad_q * wq_ref[...].astype(f32) + grad_k * wk_ref[...].astype(f32) + grad_v * wv_ref[...].astype(f32)
    gain_one = jnp.sum(terms, axis=1, keepdims=True) / column(scale_ref)
    lanes = lanes_of()
    small = jnp.where(lanes == experts, 0.5 * column(gain_ref), small)
    store_half(small_given_ref, small_kept_ref, 0, jnp.where(lanes == experts + 1, gain_one, small))


def expert_kernel(
    here_ref, sent_ref, router_ref, *refs, experts, shards
):
    w_refs = refs[:shards]
    hidden_ref, grads_ref, back_ref, scaled_ref, out_ref, share_ref, acc_ref, dots_ref, slots_ref, sems = refs[shards:]
    step = pl.program_id(0)
    width = router_ref.shape[0]

    def fetch(i, slot):
        return pltpu.make_async_copy(w_refs[i], slots_ref.at[slot], sems.at[slot])

    @pl.when(step == 0)
    def _():
        fetch(0, 0).start()

    for i in range(1, shards):
        @pl.when(step == i - 1)
        def _(i=i):
            fetch(i, i % 2).start()

    slot = lax.rem(step, 2)
    fetch(0, slot).wait()
    w = slots_ref.at[slot]
    part = w.shape[1] // 3
    half = sent_ref.shape[0] // 2
    w_in, w_down = w[:, : 2 * part], w[:, 2 * part :]
    for at in (0, half):
        these = slice(at, at + half)
        rows, cot = sent_ref[these, :width], sent_ref[these, width : 2 * width]
        both = dot(rows, w_in)
        hidden_grads = dot(cot, w_down)
        hidden, gg, gu = swish(both[:, :part], both[:, part:], hidden_grads)
        hidden_ref[0, these, :] = hidden
        grads_ref[0, these, :part] = gg
        grads_ref[0, these, part:] = gu
        product = hidden.astype(f32) * hidden_grads
        product = functools.reduce(jnp.add, [product[:, a : a + 128] for a in range(0, part, 128)])
        back = dot_nt(gg, w[:, :part]) + dot_nt(gu, w[:, part : 2 * part])
        acc_ref[these, :] = jnp.where(step == 0, 0.0, acc_ref[these, :]) + back
        dots_ref[these, :] = jnp.where(step == 0, 0.0, dots_ref[these, :]) + product

    @pl.when(step == pl.num_programs(0) - 1)
    def _():
        rows, cot = sent_ref[:, :width], sent_ref[:, width : 2 * width]
        here = here_ref[0]
        lanes = lanes_of()
        logits = dot(rows, router_ref[...])
        other = sent_ref[:, 2 * width :].astype(f32)[:, :1].astype(jnp.int32) - here
        own_logit = jnp.sum(jnp.where(lanes == here, logits, 0.0), axis=1, keepdims=True)
        other_logit = jnp.sum(jnp.where(lanes == other, logits, 0.0), axis=1, keepdims=True)
        top = jnp.maximum(own_logit, other_logit)
        own = jnp.exp(own_logit - top)
        share = own / (own + jnp.exp(other_logit - top))
        share_ref[...] = jnp.broadcast_to(share, share_ref.shape)
        scaled_ref[...] = (share * rows.astype(f32)).astype(bf16)
        out_ref[...] = (share * cot.astype(f32)).astype(bf16)
        back_ref[:, :width] = (share * acc_ref[...]).astype(bf16)
        dots = jnp.sum(dots_ref[...], axis=1, keepdims=True)
        high = dots.astype(bf16).astype(f32)
        back_ref[:, width:] = (
            jnp.where(lanes == here, high, 0.0)
            + jnp.where(lanes == experts + here, dots - high, 0.0)
        ).astype(bf16)


def expert_rows(here, sent, router, weights, experts):
    rows, width = sent.shape[0], router.shape[0]
    shards, packed = len(weights), weights[0].shape[1]
    part = packed // 3
    return call(
        functools.partial(expert_kernel, experts=experts, shards=shards),
        "expert_rows",
        (here[None], sent, router, *weights),
        [
            ((shards, rows, part), bf16),
            ((shards, rows, 2 * part), bf16),
            ((rows, width + 128), bf16),
            ((rows, width), bf16),
            ((rows, width), bf16),
            ((rows, 128), f32),
        ],
        smem=(0,),
        grid=(shards,),
        in_specs={3 + i: pl.BlockSpec(memory_space=pl.ANY) for i in range(shards)},
        out_specs={
            0: pl.BlockSpec((1, rows, part), lambda k: (k, 0, 0)),
            1: pl.BlockSpec((1, rows, 2 * part), lambda k: (k, 0, 0)),
        },
        scratch=[
            pltpu.VMEM((rows, width), f32),
            pltpu.VMEM((rows, 128), f32),
            pltpu.VMEM((2, width, packed), bf16),
            pltpu.SemaphoreType.DMA((2,)),
        ],
    )


def expert_given_kernel(scaled_ref, out_ref, hidden_ref, grads_ref, *refs, shards):
    w_refs = refs[:shards]
    d_ref, acc_ref, st_ref, ot_ref, slots_ref, sems = refs[shards:]
    step = pl.program_id(0)

    @pl.when(step == 0)
    def _():
        st_ref[...] = scaled_ref[...].T
        ot_ref[...] = out_ref[...].T

    expert_step(step, st_ref, ot_ref, hidden_ref, grads_ref, w_refs, d_ref, slots_ref, sems, acc_ref, None)


def expert_kept_kernel(st_ref, ot_ref, share_ref, first_ref, hidden_ref, grads_ref, *refs, shards):
    w_refs = refs[:shards]
    d_ref, picked_ref, acc_ref, slots_ref, sems = refs[shards:]
    step = pl.program_id(0)
    expert_step(step, st_ref, ot_ref, hidden_ref, grads_ref, w_refs, d_ref, slots_ref, sems, acc_ref, first_ref)

    @pl.when(step == pl.num_programs(0) - 1)
    def _():
        picked_ref[...] = (share_ref[:, :1] * acc_ref[...]).astype(bf16)


def expert_step(step, st_ref, ot_ref, hidden_ref, grads_ref, w_refs, d_ref, slots_ref, sems, acc_ref, first_ref):
    part = hidden_ref.shape[2]

    def fetch(i, slot):
        return pltpu.make_async_copy(w_refs[i].at[:, 2 * part :], slots_ref.at[slot], sems.at[slot])

    @pl.when(step == 0)
    def _():
        fetch(0, 0).start()
        acc_ref[...] = jnp.zeros_like(acc_ref) if first_ref is None else first_ref[...]

    for i in range(1, len(w_refs)):
        @pl.when(step == i - 1)
        def _(i=i):
            fetch(i, i % 2).start()

    slot = lax.rem(step, 2)
    fetch(0, slot).wait()
    d_ref[0, :, : 2 * part] = dot(st_ref[...], grads_ref[0]).astype(bf16)
    d_ref[0, :, 2 * part :] = dot(ot_ref[...], hidden_ref[0]).astype(bf16)
    acc_ref[...] += dot_nt(hidden_ref[0], slots_ref[slot])


def expert_half(kernel, name, args, hidden, grads, weights, at, extra):
    shards = len(weights)
    _, rows, part = hidden.shape
    width = weights[0].shape[0]
    count = len(args)
    return call(
        functools.partial(kernel, shards=shards),
        name,
        (*args, hidden, grads, *weights),
        [((shards, width, 3 * part), bf16), *extra],
        grid=(shards,),
        in_specs={
            count: pl.BlockSpec((1, rows, part), lambda k: (k + at, 0, 0)),
            count + 1: pl.BlockSpec((1, rows, 2 * part), lambda k: (k + at, 0, 0)),
            **{count + 2 + i: pl.BlockSpec(memory_space=pl.ANY) for i in range(shards)},
        },
        out_specs={0: pl.BlockSpec((1, width, 3 * part), lambda k: (k, 0, 0))},
        scratch=([pltpu.VMEM((rows, width), f32)] if at else [])
        + [pltpu.VMEM((2, width, part), bf16), pltpu.SemaphoreType.DMA((2,))],
    )


def expert_sum_kernel(kept_ref, taken_ref, high_ref, tensor_ref, keep_high_ref, keep_tensor_ref):
    shard = pl.program_id(0)
    half = kept_ref.shape[1] // 2
    total = (kept_ref[0].astype(f32) + taken_ref[0].astype(f32)).astype(bf16)
    for ref, at, here in (
        (keep_high_ref, 0, shard < 2),
        (high_ref, 0, shard >= 2),
        (keep_tensor_ref, half, shard % 2 == 0),
        (tensor_ref, half, shard % 2 == 1),
    ):
        @pl.when(here)
        def _(ref=ref, at=at):
            ref[0] = total[at : at + half]


def expert_sums_kernel(kh_ref, fh_ref, kt_ref, ft_ref, to_t_ref, to_y_ref, kept_u_ref, kept_l_ref):
    to_t_ref[...] = (kh_ref[1].astype(f32) + fh_ref[1].astype(f32)).astype(bf16)
    to_y_ref[...] = (kt_ref[1].astype(f32) + ft_ref[1].astype(f32)).astype(bf16)
    kept_u_ref[...] = (kh_ref[0].astype(f32) + fh_ref[0].astype(f32)).astype(bf16)
    kept_l_ref[...] = (kt_ref[0].astype(f32) + ft_ref[0].astype(f32)).astype(bf16)


def expert_out_kernel(ku_ref, fu_ref, kl_ref, fl_ref, gate_ref, up_ref, down_ref):
    half = ku_ref.shape[0]
    part = gate_ref.shape[2]
    for at, (kept_ref, from_ref) in ((0, (ku_ref, fu_ref)), (half, (kl_ref, fl_ref))):
        total = kept_ref[...].astype(f32) + from_ref[...].astype(f32)
        gate_ref[0, at : at + half, :] = total[:, :part]
        up_ref[0, at : at + half, :] = total[:, part : 2 * part]
        down_ref[0, :, at : at + half] = total[:, 2 * part :].T


def combine_kernel(placer_ref, back_ref, share_ref, router_ref, shared_ref, part_ref, lg_ref, *, experts):
    width = shared_ref.shape[1]
    placer = placer_ref[...]
    lanes = lanes_of()
    dots = dot(placer, back_ref[:, width:])
    dots = jnp.where(lanes < experts, dots + pltpu.roll(dots, 128 - experts, 1), 0.0)
    share = share_ref[...]
    grads = (share * (dots - jnp.sum(share * dots, axis=1, keepdims=True))).astype(bf16)
    lg_ref[...] = grads
    total = shared_ref[...] + dot_nt(grads, router_ref[...]) + dot(placer, back_ref[:, :width])
    part_ref[...] = total.astype(bf16)


def back_two_kernel(middle_ref, mine_ref, theirs_ref, cot_ref, gain_ref, wo_ref, grads_ref, low_ref, mixed_ref, sum_ref):
    middle = middle_ref[...]
    scale = rms_scale(middle)
    upstream = mine_ref[...].astype(f32) + theirs_ref[...].astype(f32)
    sum_ref[...] = jnp.sum(upstream * (middle * scale), axis=0, keepdims=True)
    grads = cot_ref[...].astype(f32) + norm_back(middle, scale, gain_ref[...], upstream)
    grads_ref[...] = grads
    low = grads.astype(bf16)
    low_ref[...] = low
    mixed_ref[...] = dot_nt(low, wo_ref[...]).astype(bf16)


def normed_back_kernel(dq_ref, dka_ref, dva_ref, dkb_ref, dvb_ref, wq_ref, wk_ref, wv_ref, core_ref, far_ref, y_ref, own_ref):
    rows = dq_ref.shape[0]
    wk, wv = wk_ref[...], wv_ref[...]

    def back(dk_ref, dv_ref, chunk):
        these = slice(chunk * rows, (chunk + 1) * rows)
        return dot_nt(dk_ref[these, :], wk) + dot_nt(dv_ref[these, :], wv)

    far_ref[...] = back(dkb_ref, dvb_ref, 1).astype(bf16)
    core_ref[...] = back(dka_ref, dva_ref, 1).astype(bf16)
    y_ref[...] = back(dkb_ref, dvb_ref, 0)
    own_ref[...] = back(dka_ref, dva_ref, 0) + dot_nt(dq_ref[...], wq_ref[...])


def first_kernel(x_ref, mine_ref, theirs_ref, grads_ref, gain_ref, out_ref):
    x = x_ref[...].astype(f32)
    upstream = mine_ref[...].astype(f32) + theirs_ref[...].astype(f32)
    out_ref[...] = grads_ref[...] + norm_back(x, rms_scale(x), gain_ref[...], upstream)


def spread(part):
    copies = jnp.broadcast_to(part[None], (16,) + part.shape)
    return exchange(copies, PLANE).reshape(-1, part.shape[1])


def late_out_kernel(core_ref, mine_ref, theirs_ref, q_ref, k_ref, v_ref, o_ref, small_ref):
    half, wide = mine_ref.shape[0], q_ref.shape[1]
    for at, ref in ((0, mine_ref), (1, theirs_ref)):
        place = core_ref[0] if at == 0 else 1 - core_ref[0]
        these = pl.ds(pl.multiple_of(place * half, 128), half)
        for i, out_ref in enumerate((q_ref, k_ref, v_ref)):
            out_ref[these, :] = ref[:, i * wide : (i + 1) * wide].astype(f32)
        o_ref[:, these] = ref[:, 3 * wide : 4 * wide].astype(f32).T
        small_ref[these, :] = ref[:, 4 * wide :].astype(f32)


def early_out_kernel(core_ref, mine_ref, theirs_ref, gate_ref, up_ref, down_ref):
    half, wide = mine_ref.shape[0], gate_ref.shape[1]
    for at, ref in ((0, mine_ref), (1, theirs_ref)):
        place = core_ref[0] if at == 0 else 1 - core_ref[0]
        these = pl.ds(pl.multiple_of(place * half, 128), half)
        for i, out_ref in enumerate((gate_ref, up_ref)):
            out_ref[these, :] = ref[:, i * wide : (i + 1) * wide].astype(f32)
        down_ref[:, these] = ref[:, 2 * wide :].astype(f32).T


def local(
    tokens,
    routes,
    gain_one,
    w_query,
    w_key,
    w_value,
    w_output,
    gain_two,
    w_router,
    shared_gate,
    shared_up,
    shared_down,
    expert_gate,
    expert_up,
    expert_down,
    cotangent,
):
    rows, width = tokens.shape
    wide = w_query.shape[1]
    experts = w_router.shape[1]
    seats = experts * SLOTS
    part = expert_gate.shape[2]
    shared_part = shared_gate.shape[1]
    tensor = lax.axis_index("t")
    core = lax.axis_index("c")
    high = lax.axis_index("yl")
    expert_here = lax.axis_index(ROUTE)
    router = jnp.pad(w_router, ((0, 0), (0, 128 - experts)))
    of_rows = ((rows, width), f32)
    of_rows_low = ((rows, width), bf16)

    tokens_y = swap(tokens, "yl")
    tokens_c = swap(tokens, "c")
    hide = jnp.stack([core < 0, core == 0, high == 0, high == 0])
    hide = jnp.where(hide, 1e30, 0.0).astype(f32)

    frequency = rope_base ** (-np.arange(HEAD_DIM // 2) * 2.0 / HEAD_DIM)
    frequency = np.tile(frequency, PAIR // (HEAD_DIM // 2))
    inner = np.arange(rows)[:, None] * frequency[None, :]
    starts = jnp.stack(
        [((high ^ my) * 2 + (core ^ mc)) * rows for my, mc in ((0, 0), (0, 1), (1, 0), (1, 1))]
    )
    outer = starts.astype(f32)[:, None, None] * frequency.astype(np.float32)[None, None, :]
    cos_in, sin_in = np.cos(inner).astype(np.float32), np.sin(inner).astype(np.float32)
    cos_out, sin_out = jnp.cos(outer), jnp.sin(outer)
    cosine = (cos_out * cos_in - sin_out * sin_in).reshape(2, 2 * rows, PAIR)
    sine = (sin_out * cos_in + cos_out * sin_in).reshape(2, 2 * rows, PAIR)

    own = jnp.concatenate([expert_gate[0], expert_up[0], expert_down[0].T], axis=1)
    placer, placer_turned, sent_cot = route(tensor, routes, cotangent, experts)
    normed_a, keys_a, values_a, query = project(
        tokens, tokens_c, gain_one[None], w_key, w_value, cosine[0], sine[0], w_query
    )
    tokens_y, keys_a, placer, placer_turned, sent_cot, own_later = lax.optimization_barrier(
        (tokens_y, keys_a, placer, placer_turned, sent_cot, own)
    )
    tokens_yc = swap(tokens_y, "c")
    own_t, own_y = swap(own, "t"), swap(own_later, "yl")
    normed_b, keys_b, values_b = project(
        tokens_y, tokens_yc, gain_one[None], w_key, w_value, cosine[1], sine[1]
    )
    mixed_heads, logs, attended = attend(
        hide, query, keys_a, values_a, keys_b, values_b, w_output
    )
    attended, own_t, own_later = lax.optimization_barrier((attended, own_t, own_later))

    own_ty = swap(own_t, "yl")
    turned_a, turned_b = call(
        turn_rows_kernel,
        "turn_rows",
        (after(normed_a, attended), normed_b),
        [((width, 2 * rows), bf16)] * 2,
    )
    theirs, own_y, turned_a, turned_b = lax.optimization_barrier(
        (swap(attended, "t"), own_y, turned_a, turned_b)
    )
    middle, normed_two, sent_rows = call(
        second_kernel,
        "second",
        (tokens, attended, theirs, gain_two[None], placer_turned, sent_cot),
        [of_rows, of_rows_low, ((seats, 2 * width + 128), bf16)],
    )

    arrived = exchange(sent_rows.reshape(experts, SLOTS, -1), ROUTE).reshape(seats, -1)
    hidden_shared, shared_gg, shared_gu, shared_back, shared_out, share = shared(
        normed_two, cotangent, shared_gate, shared_up, shared_down, router, routes
    )
    early_given, early_kept = half_call(
        shared_weights_kernel,
        "shared_weights",
        core,
        (normed_two, cotangent),
        (shared_gg, shared_gu, hidden_shared),
        (3 * shared_part,),
    )
    weights = [own_later, own_t, own_y, own_ty]
    weights = [swap(w, "c") for w in weights] + weights
    arrived, early_given, early_kept, shared_back, shared_out, share, *weights = (
        lax.optimization_barrier(
            (arrived, early_given, early_kept, shared_back, shared_out, share, *weights)
        )
    )
    early_taken = swap(early_given, "c")
    hidden_expert, expert_grads, back, scaled_rows, out_grads, row_share = expert_rows(
        expert_here, arrived, router, weights, experts
    )
    given, first_out, scaled_turned, out_turned = expert_half(
        expert_given_kernel,
        "expert_given",
        (scaled_rows, out_grads),
        hidden_expert,
        expert_grads,
        weights[:4],
        0,
        [((seats, width), f32), ((width, seats), bf16), ((width, seats), bf16)],
    )
    (early,) = call(
        half_sum_kernel, "half_sum", (after(early_kept, back), early_taken), [(early_kept.shape, bf16)]
    )
    back = exchange(back.reshape(experts, SLOTS, -1), ROUTE).reshape(seats, -1)
    back, given, first_out, scaled_turned, out_turned, early = lax.optimization_barrier(
        (back, given, first_out, scaled_turned, out_turned, early)
    )

    mine, logits_grads = call(
        functools.partial(combine_kernel, experts=experts),
        "combine",
        (placer, back, share, router, shared_back),
        [of_rows_low, ((rows, 128), bf16)],
    )
    kept, picked = expert_half(
        expert_kept_kernel,
        "expert_kept",
        (after(scaled_turned, mine), out_turned, row_share, first_out),
        hidden_expert,
        expert_grads,
        weights[4:],
        4,
        [((seats, width), bf16)],
    )
    of_shard = pl.BlockSpec((1, width, 3 * part), lambda k: (k, 0, 0))
    half_shard = (1, width // 2, 3 * part)
    to_high, to_tensor, keep_high, keep_tensor = call(
        expert_sum_kernel,
        "expert_sum",
        (kept, swap(given, "c")),
        [((2, width // 2, 3 * part), bf16)] * 4,
        grid=(4,),
        in_specs={0: of_shard, 1: of_shard},
        out_specs={
            0: pl.BlockSpec(half_shard, lambda k: (jnp.maximum(k - 2, 0), 0, 0)),
            1: pl.BlockSpec(half_shard, lambda k: (k // 2, 0, 0)),
            2: pl.BlockSpec(half_shard, lambda k: (jnp.minimum(k, 1), 0, 0)),
            3: pl.BlockSpec(half_shard, lambda k: (k // 2, 0, 0)),
        },
    )
    theirs, to_high, to_tensor, keep_high, keep_tensor, picked = lax.optimization_barrier(
        (swap(mine, "t"), to_high, to_tensor, keep_high, keep_tensor, picked)
    )
    middle_grads, middle_low, mixed_grads, gain_sum = call(
        back_two_kernel,
        "back_two",
        (middle, mine, theirs, cotangent, gain_two[None], w_output),
        [of_rows, of_rows_low, ((rows, wide), bf16), ((1, width), f32)],
    )

    dq, dka, dva, dkb, dvb = attend_back(
        hide, query, keys_a, values_a, keys_b, values_b, mixed_heads, logs, mixed_grads,
        cosine[0], sine[0], cosine[1], sine[1],
    )
    picked = exchange(picked.reshape(experts, SLOTS, width), ROUTE).reshape(seats, width)
    from_high, from_tensor = swap(to_high, "yl"), swap(to_tensor, "t")
    dq, dka, dva, dkb, dvb, picked, from_high, from_tensor = lax.optimization_barrier(
        (dq, dka, dva, dkb, dvb, picked, from_high, from_tensor)
    )
    late_given, late_kept, small_given, small_kept = half_call(
        functools.partial(late_weights_kernel, experts=experts),
        "late_weights",
        core,
        (normed_two, middle_low, gain_sum, gain_one[None]),
        (dq, dka, dkb, dva, dvb, logits_grads, mixed_heads),
        (4 * wide, 128),
        (turned_a, turned_b, w_query, w_key, w_value),
    )

    small = swap(small_kept, "t").astype(f32) + lax.ppermute(
        small_given, ("c", "t"), [(0, 3), (3, 0), (1, 2), (2, 1)]
    ).astype(f32)
    small = small_kept.astype(f32) + swap(small_given, "c").astype(f32) + small
    sums = call(
        expert_sums_kernel,
        "expert_sums",
        (keep_high, after(from_high, late_given), keep_tensor, from_tensor),
        [((width // 2, 3 * part), bf16)] * 4,
    )
    early = lax.psum_scatter(early, "x", scatter_dimension=0, tiled=True)
    early = lax.psum_scatter(early, ("yh", "yl"), scatter_dimension=0, tiled=True)
    early_zh = swap(after(early, late_given), "zh")
    late_taken, small, next_t, next_y, kept_u, kept_l, early, early_zh = lax.optimization_barrier(
        (swap(late_given, "c"), small, *sums, early, early_zh)
    )
    total = late_kept.astype(f32) + late_taken.astype(f32)
    total = jnp.concatenate([total, small], axis=1).astype(bf16)
    parts = exchange(total.reshape(16, -1, total.shape[1]), PLANE)
    parts, from_next_t, from_next_y = lax.optimization_barrier(
        (parts, swap(next_t, "t"), swap(next_y, "yl"))
    )

    to_core, to_far, to_y, own_part = call(
        normed_back_kernel,
        "normed_back",
        (after(dq, total), dka, dva, dkb, dvb, w_query, w_key, w_value),
        [of_rows_low, of_rows_low, of_rows, of_rows],
    )
    from_far = swap(to_far, "c").astype(f32)
    own_part = own_part + swap(to_core, "c").astype(f32)
    from_y = swap((to_y + from_far).astype(bf16), "yl")
    block_part = (shared_out + dot(after(placer, total), picked)).astype(bf16)
    part_sum = jnp.sum(parts.astype(f32), axis=0).astype(bf16)
    part_zh, from_y, from_block, own_part = lax.optimization_barrier(
        (swap(part_sum, "zh"), from_y, swap(block_part, "t"), own_part)
    )
    own_part = (own_part + from_y.astype(f32)).astype(bf16)
    total = (part_sum.astype(f32) + part_zh.astype(f32)).astype(bf16)
    total, from_t = lax.optimization_barrier(
        (spread(after(total, own_part)), swap(own_part, "t"))
    )
    block_out = (middle + block_part.astype(f32) + from_block.astype(f32)).astype(bf16)
    (grad_tokens,) = call(
        first_kernel,
        "first",
        (tokens, own_part, from_t, middle_grads, gain_one[None]),
        [of_rows],
    )
    square = ((width, wide), f32)
    grad_query, grad_key, grad_value, grad_output, small = call(
        late_out_kernel,
        "late_out",
        (core[None], total, swap(total, "c")),
        [square, square, square, ((wide, width), f32), ((width, 128), f32)],
        smem=(0,),
    )
    grad_expert_gate, grad_expert_up, grad_expert_down = call(
        expert_out_kernel,
        "expert_out",
        (kept_u, from_next_t, kept_l, from_next_y),
        [((1, width, part), f32), ((1, width, part), f32), ((1, part, width), f32)],
    )
    early = (early.astype(f32) + early_zh.astype(f32)).astype(bf16)
    early = lax.all_gather(early, PLANE, axis=0, tiled=True)
    early = after(early, from_t)
    hidden = (width, shared_part)
    grad_shared_gate, grad_shared_up, grad_shared_down = call(
        early_out_kernel,
        "early_out",
        (core[None], early, swap(early, "c")),
        [(hidden, f32), (hidden, f32), (hidden[::-1], f32)],
        smem=(0,),
    )
    return (
        block_out,
        grad_tokens,
        small[:, experts + 1],
        grad_query,
        grad_key,
        grad_value,
        grad_output,
        small[:, experts],
        small[:, :experts],
        grad_shared_gate,
        grad_shared_up,
        grad_shared_down,
        grad_expert_gate,
        grad_expert_up,
        grad_expert_down,
    )


def solution(mesh):
    fine = Mesh(mesh.devices.reshape(2, 4, 2, 2, 2, 2), AXES)
    placed = (
        P(EXPERT, None),
        P(EXPERT, None),
        P(),
        P(None, "t"),
        P(None, "t"),
        P(None, "t"),
        P("t", None),
        P(),
        P(),
        P(None, "t"),
        P(None, "t"),
        P("t", None),
        P(EXPERT, None, "t"),
        P(EXPERT, None, "t"),
        P(EXPERT, "t", None),
        P(EXPERT, None),
    )
    return jax.shard_map(
        local,
        mesh=fine,
        in_specs=placed,
        out_specs=(
            P(EXPERT, None),
            P(EXPERT, None),
            P(),
            P(None, "t"),
            P(None, "t"),
            P(None, "t"),
            P("t", None),
            P(),
            P(),
            P(None, "t"),
            P(None, "t"),
            P("t", None),
            P(EXPERT, None, "t"),
            P(EXPERT, None, "t"),
            P(EXPERT, "t", None),
        ),
        check_vma=False,
    )
```

profile of v0, /device:TPU:1, one launch (start us, length us, event | category | flops | bytes accessed | tf_op | source)
XLA Modules:
  0.0 384.1 jit_solution(14518272790542232715)
XLA Ops:
  15.3 4.2 %route.1 = (bf16[512,640]{1,0:T(8,128)(2,1)S(1)}, bf16[640,512]{1,0:T(8,128)(2,1)S(1)}, bf16[640,896]{1,0:T(8,128)(2,1)}) custom-call(s32[1]{0:T(128)} %bitcast.9.tensor_ref, s32[512,2]{1,0:T(8,128)S(1)} %copy.41.routes_ref, bf16[512,768]{1,0:T(8,128)(2,1)} %cot_ref.7, bf16[128,640]{1,0:T(8,128)(2,1)S(1)} %copy-done.27, f32[1,640]{1,0:T(1,128)S(1)} %copy-done.28), custom_call_target="tpu_custom_call" | custom-call | flops 920000000 | bytes 1048576 | tf_op jit(solution)/shard_map/route/pallas_call | solution.py:114
  20.9 6.2 %project.2 = (bf16[1024,768]{1,0:T(8,128)(2,1)}, bf16[1024,384]{1,0:T(8,128)(2,1)}, bf16[1024,384]{1,0:T(8,128)(2,1)}, bf16[512,384]{1,0:T(8,128)(2,1)S(1)}) custom-call(bf16[512,768]{1,0:T(8,128)(2,1)} %x_ref.3, bf16[512,768]{1,0:T(8,128)(2,1)} %collective-permute-done.x1_ref, f32[1,768]{1,0:T(1,128)S(1)} %broadcast_in_dim.22.gain_ref.scale_ref, ...), custom_call_target="tpu_custom_call" | custom-call | flops 1150000000 | bytes 1048576 | tf_op jit(solution)/shard_map/project/pallas_call | solution.py:114
  33.7 5.2 %project.3 = (bf16[1024,768]{1,0:T(8,128)(2,1)}, bf16[1024,384]{1,0:T(8,128)(2,1)}, bf16[1024,384]{1,0:T(8,128)(2,1)}) custom-call(bf16[512,768]{1,0:T(8,128)(2,1)} %collective-permute-done.1.x0_ref, bf16[512,768]{1,0:T(8,128)(2,1)} %collective-permute-done.2.x1_ref, f32[1,768]{1,0:T(1,128)S(1)} %broadcast_in_dim.22.gain_ref.scale_ref, ...), custom_call_target="tpu_custom_call" | custom-call | flops 1150000000 | bytes 1048576 | tf_op jit(solution)/shard_map/project/pallas_call | solution.py:114
  39.8 14.0 %attend.1 = (bf16[512,384]{1,0:T(8,128)(2,1)S(1)}, f32[512,384]{1,0:T(8,128)}, bf16[512,768]{1,0:T(8,128)(2,1)}) custom-call(f32[4]{0:T(128)S(1)} %add_select_fusion.hide_ref, bf16[512,384]{1,0:T(8,128)(2,1)S(1)} %copy-done.25, bf16[1024,384]{1,0:T(8,128)(2,1)} %get-tuple-element.169.ka_ref, bf16[1024,384]{1,0:T(8,128)(2,1)} %get-tuple-element.170.va_ref, ...), custom_call_target="tpu_custom_call" | custom-call | flops 3220000000 | bytes 1048576 | tf_op jit(solution)/shard_map/attend/pallas_call | solution.py:114
  59.0 4.0 %turn_rows.1 = (bf16[768,1024]{1,0:T(8,128)(2,1)S(1)}, bf16[768,1024]{1,0:T(8,128)(2,1)}) custom-call(bf16[1024,768]{1,0:T(8,128)(2,1)} %get-tuple-element.178.a_ref, bf16[1024,768]{1,0:T(8,128)(2,1)} %get-tuple-element.179.b_ref), custom_call_target="tpu_custom_call" | custom-call | flops 690000000 | bytes 1048576 | tf_op jit(solution)/shard_map/turn_rows/pallas_call | solution.py:114
  64.2 11.0 %collective-permute-done.4.theirs_ref = bf16[512,768]{1,0:T(8,128)(2,1)S(1)} collective-permute-done((bf16[512,768]{1,0:T(8,128)(2,1)}, bf16[512,768]{1,0:T(8,128)(2,1)S(1)}, u32[]{:S(2)}, u32[]{:S(2)}) %collective-permute-start.4) | collective-permute-done | bytes 786464 | tf_op jit(solution)/shard_map/ppermute | solution.py:29
  76.2 4.8 %second.1 = (f32[512,768]{1,0:T(8,128)}, bf16[512,768]{1,0:T(8,128)(2,1)S(1)}, bf16[640,1664]{1,0:T(8,128)(2,1)}) custom-call(bf16[512,768]{1,0:T(8,128)(2,1)} %x_ref.3, bf16[512,768]{1,0:T(8,128)(2,1)} %get-tuple-element.176.mine_ref, bf16[512,768]{1,0:T(8,128)(2,1)} %copy-done.36, f32[1,768]{1,0:T(1,128)S(1)} %broadcast_in_dim.24.gain_ref, ...), custom_call_target="tpu_custom_call" | custom-call | flops 920000000 | bytes 1048576 | tf_op jit(solution)/shard_map/second/pallas_call | solution.py:114
  81.0 9.6 %all-to-all-start = ((bf16[16,40,1664]{2,1,0:T(8,128)(2,1)}), bf16[16,40,1664]{2,1,0:T(8,128)(2,1)}, u32[]{:S(2)}, u32[]{:S(2)}) async-start(bf16[16,40,1664]{2,1,0:T(8,128)(2,1)} %bitcast.44), calls=%async_computation | async-start | bytes 4259840 | tf_op jit(solution)/shard_map/all_to_all | solution.py:33
  93.8 12.8 %shared.1 = (bf16[512,1024]{1,0:T(8,128)(2,1)}, bf16[512,1024]{1,0:T(8,128)(2,1)}, bf16[512,1024]{1,0:T(8,128)(2,1)}, f32[512,768]{1,0:T(8,128)}, f32[512,768]{1,0:T(8,128)}, /*index=5*/f32[512,128]{1,0:T(8,128)S(1)}) custom-call(bf16[512,768]{1,0:T(8,128)(2,1)S(1)} %get-tuple-element.187.n_ref.n2_ref, bf16[512,768]{1,0:T(8,128)(2,1)} %cot_ref.7, ...), custom_call_target="tpu_custom_call" | custom-call | flops 2760000000 | bytes 1048576 | tf_op jit(solution)/shard_map/shared/pallas_call | solution.py:114
  106.6 8.2 %shared_weights.1 = (bf16[384,3072]{1,0:T(8,128)(2,1)}, bf16[384,3072]{1,0:T(8,128)(2,1)}) custom-call(s32[1]{0:T(128)} %bitcast.18.core_ref, bf16[512,768]{1,0:T(8,128)(2,1)S(1)} %get-tuple-element.187.n_ref.n2_ref, bf16[512,768]{1,0:T(8,128)(2,1)S(1)} %copy-done.10, bf16[512,1024]{1,0:T(8,128)(2,1)} %get-tuple-element.188.gg_ref, ...), custom_call_target="tpu_custom_call" | custom-call | flops 1380000000 | bytes 1048576 | tf_op jit(solution)/shard_map/shared_weights/pallas_call | solution.py:417
  114.8 5.7 %all-to-all-done = bf16[16,40,1664]{2,1,0:T(8,128)(2,1)} async-done(((bf16[16,40,1664]{2,1,0:T(8,128)(2,1)}), bf16[16,40,1664]{2,1,0:T(8,128)(2,1)}, u32[]{:S(2)}, u32[]{:S(2)}) %all-to-all-start) | async-done | bytes 2129952 | tf_op jit(solution)/shard_map/all_to_all | solution.py:33
  123.1 20.7 %expert_rows.1 = (bf16[8,640,256]{2,1,0:T(8,128)(2,1)}, bf16[8,640,512]{2,1,0:T(8,128)(2,1)}, bf16[640,896]{1,0:T(8,128)(2,1)}, bf16[640,768]{1,0:T(8,128)(2,1)S...) custom-call(s32[1]{0:T(128)} %bitcast.19.here_ref, bf16[640,1664]{1,0:T(8,128)(2,1)} %bitcast.17.sent_ref, ...), custom_call_target="tpu_custom_call" | custom-call | flops 4600000000 | bytes 1048576 | tf_op jit(solution)/shard_map/expert_rows/pallas_call | solution.py:114
  144.7 6.2 %all-to-all-start.1 = ((bf16[16,40,896]{2,1,0:T(8,128)(2,1)}), bf16[16,40,896]{2,1,0:T(8,128)(2,1)S(1)}, u32[]{:S(2)}, u32[]{:S(2)}) async-start(bf16[16,40,896]{2,1,0:T(8,128)(2,1)} %bitcast.46), calls=%async_computation.1 | async-start | bytes 2293760 | tf_op jit(solution)/shard_map/all_to_all | solution.py:33
  151.0 10.4 %expert_given.1 = (bf16[4,768,768]{2,1,0:T(8,128)(2,1)}, f32[640,768]{1,0:T(8,128)}, bf16[768,640]{1,0:T(8,128)(2,1)S(1)}, bf16[768,640]{1,0:T(8,128)(2,1)S(1)}) custom-call(bf16[640,768]{1,0:T(8,128)(2,1)} %copy-done.9, bf16[640,768]{1,0:T(8,128)(2,1)} %get-tuple-element.212.out_ref, bf16[8,640,256]{2,1,0:T(8,128)(2,1)} %get-tuple-element.213.hidden_ref, ...), custom_call_target="tpu_custom_call" | custom-call | flops 2070000000 | bytes 1048576 | tf_op jit(solution)/shard_map/expert_given/pallas_call | solution.py:114
  163.4 4.3 %half_sum.1 = bf16[384,3072]{1,0:T(8,128)(2,1)} custom-call(bf16[384,3072]{1,0:T(8,128)(2,1)} %get-tuple-element.220.kept_ref, bf16[384,3072]{1,0:T(8,128)(2,1)} %collective-permute-done.11.taken_ref), custom_call_target="tpu_custom_call" | custom-call | flops 920000000 | bytes 1048576 | tf_op jit(solution)/shard_map/half_sum/pallas_call | solution.py:114
  171.6 3.6 combine.1
  176.1 11.0 %expert_kept.1 = (bf16[4,768,768]{2,1,0:T(8,128)(2,1)}, bf16[640,768]{1,0:T(8,128)(2,1)}) custom-call(bf16[768,640]{1,0:T(8,128)(2,1)} %copy-done.7, bf16[768,640]{1,0:T(8,128)(2,1)} %copy-done.8, f32[640,128]{1,0:T(8,128)S(1)} %get-tuple-element.229.share_ref, f32[640,768]{1,0:T(8,128)} %get-tuple-element.230.first_ref, ...), custom_call_target="tpu_custom_call" | custom-call | flops 2070000000 | bytes 1048576 | tf_op jit(solution)/shard_map/expert_kept/pallas_call | solution.py:114
  187.1 7.5 %expert_sum.1 = (bf16[2,384,768]{2,1,0:T(8,128)(2,1)}, bf16[2,384,768]{2,1,0:T(8,128)(2,1)}, bf16[2,384,768]{2,1,0:T(8,128)(2,1)}, bf16[2,384,768]{2,1,0:T(8,128)(2,1)}) custom-call(bf16[4,768,768]{2,1,0:T(8,128)(2,1)} %get-tuple-element.231.kept_ref, bf16[4,768,768]{2,1,0:T(8,128)(2,1)} %collective-permute-done.13.taken_ref), custom_call_target="tpu_custom_call" | custom-call | flops 920000000 | bytes 1048576 | tf_op jit(solution)/shard_map/expert_sum/pallas_call | solution.py:114
  195.6 6.9 %all-to-all-start.2 = ((bf16[16,40,768]{2,1,0:T(8,128)(2,1)}), bf16[16,40,768]{2,1,0:T(8,128)(2,1)}, u32[]{:S(2)}, u32[]{:S(2)}) async-start(bf16[16,40,768]{2,1,0:T(8,128)(2,1)} %bitcast.22), calls=%async_computation.2 | async-start | bytes 1966080 | tf_op jit(solution)/shard_map/all_to_all | solution.py:33
  203.4 4.4 %back_two.1 = (f32[512,768]{1,0:T(8,128)}, bf16[512,768]{1,0:T(8,128)(2,1)S(1)}, bf16[512,384]{1,0:T(8,128)(2,1)S(1)}, f32[1,768]{1,0:T(1,128)S(1)}) custom-call(f32[512,768]{1,0:T(8,128)} %get-tuple-element.185.middle_ref, bf16[512,768]{1,0:T(8,128)(2,1)} %copy-done.11, bf16[512,768]{1,0:T(8,128)(2,1)} %copy-done.35, bf16[512,768]{1,0:T(8,128)(2,1)} %cot_ref.7, ...), custom_call_target="tpu_custom_call" | custom-call | flops 920000000 | bytes 1048576 | tf_op jit(solution)/shard_map/back_two/pallas_call | solution.py:114
  208.7 23.4 %attend_back.1 = (bf16[512,384]{1,0:T(8,128)(2,1)S(1)}, bf16[1024,384]{1,0:T(8,128)(2,1)}, bf16[1024,384]{1,0:T(8,128)(2,1)}, bf16[1024,384]{1,0:T(8,128)(2,1)}, bf16[1024,384]{1,0:T(8,128)(2,1)}) custom-call(f32[4]{0:T(128)S(1)} %add_select_fusion.hide_ref, bf16[512,384]{1,0:T(8,128)(2,1)S(1)} %copy-done.26, bf16[1024,384]{1,0:T(8,128)(2,1)} %get-tuple-element.169.ka_ref, ...), custom_call_target="tpu_custom_call" | custom-call | flops 5289999872 | bytes 1048576 | tf_op jit(solution)/shard_map/attend_back/pallas_call | solution.py:114
  232.1 5.9 %all-to-all-done.2 = bf16[16,40,768]{2,1,0:T(8,128)(2,1)} async-done(((bf16[16,40,768]{2,1,0:T(8,128)(2,1)}), bf16[16,40,768]{2,1,0:T(8,128)(2,1)}, u32[]{:S(2)}, u32[]{:S(2)}) %all-to-all-start.2) | async-done | bytes 983072 | tf_op jit(solution)/shard_map/all_to_all | solution.py:33
  238.0 10.5 %late_weights.1 = (bf16[384,1536]{1,0:T(8,128)(2,1)}, bf16[384,1536]{1,0:T(8,128)(2,1)}, bf16[384,128]{1,0:T(8,128)(2,1)S(1)}, bf16[384,128]{1,0:T(8,128)(2,1)S(1)}) custom-call(s32[1]{0:T(128)} %bitcast.18.core_ref, bf16[512,768]{1,0:T(8,128)(2,1)} %copy-done.12, bf16[512,768]{1,0:T(8,128)(2,1)} %copy-done.13, f32[1,768]{1,0:T(1,128)S(1)} %get-tuple-element.240.gain_ref, ...), custom_call_target="tpu_custom_call" | custom-call | flops 1840000000 | bytes 1048576 | tf_op jit(solution)/shard_map/late_weights/pallas_call | solution.py:417
  258.8 3.9 %collective-permute-done.20 = bf16[24,3072]{1,0:T(8,128)(2,1)S(1)} collective-permute-done((bf16[24,3072]{1,0:T(8,128)(2,1)}, bf16[24,3072]{1,0:T(8,128)(2,1)S(1)}, u32[]{:S(2)}, u32[]{:S(2)}) %collective-permute-start.20) | collective-permute-done | bytes 147488 | tf_op jit(solution)/shard_map/ppermute | solution.py:29
  265.6 7.6 %normed_back.1 = (bf16[512,768]{1,0:T(8,128)(2,1)}, bf16[512,768]{1,0:T(8,128)(2,1)}, f32[512,768]{1,0:T(8,128)}, f32[512,768]{1,0:T(8,128)}) custom-call(bf16[512,384]{1,0:T(8,128)(2,1)S(1)} %get-tuple-element.282.dq_ref, bf16[1024,384]{1,0:T(8,128)(2,1)} %get-tuple-element.255.dka_ref, bf16[1024,384]{1,0:T(8,128)(2,1)} %get-tuple-element.257.dva_ref, ...), custom_call_target="tpu_custom_call" | custom-call | flops 1840000000 | bytes 1048576 | tf_op jit(solution)/shard_map/normed_back/pallas_call | solution.py:114
  275.3 6.3 %all-to-all-start.3 = ((bf16[16,24,1664]{2,1,0:T(8,128)(2,1)}), bf16[16,24,1664]{2,1,0:T(8,128)(2,1)S(1)}, u32[]{:S(2)}, u32[]{:S(2)}) async-start(bf16[16,24,1664]{2,1,0:T(8,128)(2,1)} %pad_maximum_fusion.1), calls=%async_computation.5 | async-start | bytes 2555904 | tf_op jit(solution)/shard_map/all_to_all | solution.py:33
  289.9 9.4 %all-to-all-done.3 = bf16[16,24,1664]{2,1,0:T(8,128)(2,1)S(1)} async-done(((bf16[16,24,1664]{2,1,0:T(8,128)(2,1)}), bf16[16,24,1664]{2,1,0:T(8,128)(2,1)S(1)}, u32[]{:S(2)}, u32[]{:S(2)}) %all-to-all-start.3) | async-done | bytes 1277984 | tf_op jit(solution)/shard_map/all_to_all | solution.py:33
  305.3 19.7 %collective-permute-done.25 = bf16[512,768]{1,0:T(8,128)(2,1)} collective-permute-done((bf16[512,768]{1,0:T(8,128)(2,1)}, bf16[512,768]{1,0:T(8,128)(2,1)}, u32[]{:S(2)}, u32[]{:S(2)}) %collective-permute-start.25) | collective-permute-done | bytes 786464 | tf_op jit(solution)/shard_map/ppermute | solution.py:29
  327.5 5.0 %all-to-all-start.4 = ((bf16[16,24,1664]{2,1,0:T(8,128)(2,1)}), bf16[16,24,1664]{2,1,0:T(8,128)(2,1)S(1)}, u32[]{:S(2)}, u32[]{:S(2)}) async-start(bf16[16,24,1664]{2,1,0:T(8,128)(2,1)} %broadcast_in_dim.48), calls=%async_computation.6 | async-start | bytes 2555904 | tf_op jit(solution)/shard_map/all_to_all | solution.py:33
  334.7 16.8 %collective-permute-done.28.theirs_ref = bf16[512,768]{1,0:T(8,128)(2,1)} collective-permute-done((bf16[512,768]{1,0:T(8,128)(2,1)S(1)}, bf16[512,768]{1,0:T(8,128)(2,1)}, u32[]{:S(2)}, u32[]{:S(2)}) %collective-permute-start.28) | collective-permute-done | bytes 786464 | tf_op jit(solution)/shard_map/ppermute | solution.py:29
  365.0 3.8 late_out.1
  370.6 6.7 %early_out.1 = (f32[768,1024]{1,0:T(8,128)}, f32[768,1024]{1,0:T(8,128)}, f32[1024,768]{1,0:T(8,128)}) custom-call(s32[1]{0:T(128)} %bitcast.18.core_ref, bf16[384,3072]{1,0:T(8,128)(2,1)} %all-gather.2.cloned.1.call-done.mine_ref, bf16[384,3072]{1,0:T(8,128)(2,1)} %collective-permute-done.30.theirs_ref), custom_call_target="tpu_custom_call" | custom-call | flops 1150000000 | bytes 1048576 | tf_op jit(solution)/shard_map/early_out/pallas_call | solution.py:114
  (185 shorter events, 90.0 us)
Async XLA Ops:
  7.2 19.9 %collective-permute-start.1 = (bf16[512,768]{1,0:T(8,128)(2,1)}, bf16[512,768]{1,0:T(8,128)(2,1)}, u32[]{:S(2)}, u32[]{:S(2)}) collective-permute-start(bf16[512,768]{1,0:T(8,128)(2,1)} %x_ref.3), channel_id=1, source_target_pairs={{0,4},{4,0},{1,5},{5,1},{2,6},{6,2},{3,7},{7,3},{8,12},{12,8},{9,1... | collective-permute-start | bytes 2359304 | tf_op jit(solution)/shard_map/ppermute | solution.py:29
  9.4 11.5 %collective-permute-start = (bf16[512,768]{1,0:T(8,128)(2,1)}, bf16[512,768]{1,0:T(8,128)(2,1)}, u32[]{:S(2)}, u32[]{:S(2)}) collective-permute-start(bf16[512,768]{1,0:T(8,128)(2,1)} %x_ref.3), channel_id=1, source_target_pairs={{0,2},{2,0},{1,3},{3,1},{4,6},{6,4},{5,7},{7,5},{8,10},{10,8},{9,1... | collective-permute-start | bytes 2359304 | tf_op jit(solution)/shard_map/ppermute | solution.py:29
  28.2 28.2 %collective-permute-start.3 = (bf16[768,768]{1,0:T(8,128)(2,1)S(1)}, bf16[768,768]{1,0:T(8,128)(2,1)}, u32[]{:S(2)}, u32[]{:S(2)}) collective-permute-start(bf16[768,768]{1,0:T(8,128)(2,1)S(1)} %pad_maximum_fusion.2.refs_4_.refs_0_), channel_id=1, source_target_pairs={{0,1},{1,0},{2,3},{3,2},{4,5},{5,4},{6,7},{7,6},{8,9},{9,8},{10,11... | collective-permute-start | bytes 3538952 | tf_op jit(solution)/shard_map/ppermute | solution.py:29
  30.1 34.1 %collective-permute-start.5 = (bf16[768,768]{1,0:T(8,128)(2,1)S(1)}, bf16[768,768]{1,0:T(8,128)(2,1)S(1)}, u32[]{:S(2)}, u32[]{:S(2)}) collective-permute-start(bf16[768,768]{1,0:T(8,128)(2,1)S(1)} %pad_maximum_fusion.2.refs_4_.refs_0_), channel_id=1, source_target_pairs={{0,4},{4,0},{1,5},{5,1},{2,6},{6,2},{3,7},{7,3},{8,12},{12,8},{9,1... | collective-permute-start | bytes 3538952 | tf_op jit(solution)/shard_map/ppermute | solution.py:29
  56.4 18.8 %collective-permute-start.4 = (bf16[512,768]{1,0:T(8,128)(2,1)}, bf16[512,768]{1,0:T(8,128)(2,1)S(1)}, u32[]{:S(2)}, u32[]{:S(2)}) collective-permute-start(bf16[512,768]{1,0:T(8,128)(2,1)} %get-tuple-element.176.mine_ref), channel_id=1, source_target_pairs={{0,1},{1,0},{2,3},{3,2},{4,5},{5,4},{6,7},{7,6},{8,9},{9,8},{10,11... | collective-permute-start | bytes 2359304 | tf_op jit(solution)/shard_map/ppermute | solution.py:29
  57.7 35.4 %collective-permute-start.9 = (bf16[768,768]{1,0:T(8,128)(2,1)}, bf16[768,768]{1,0:T(8,128)(2,1)}, u32[]{:S(2)}, u32[]{:S(2)}) collective-permute-start(bf16[768,768]{1,0:T(8,128)(2,1)} %collective-permute-done.3.refs_5_.refs_1_), channel_id=1, source_target_pairs={{0,4},{4,0},{1,5},{5,1},{2,6},{6,2},{3,7},{7,3},{8,12},{12,8},{9,1... | collective-permute-start | bytes 3538952 | tf_op jit(solution)/shard_map/ppermute | solution.py:29
  81.0 39.6 %all-to-all-start = ((bf16[16,40,1664]{2,1,0:T(8,128)(2,1)}), bf16[16,40,1664]{2,1,0:T(8,128)(2,1)}, u32[]{:S(2)}, u32[]{:S(2)}) async-start(bf16[16,40,1664]{2,1,0:T(8,128)(2,1)} %bitcast.44), calls=%async_computation | async-start | bytes 4259840 | tf_op jit(solution)/shard_map/all_to_all | solution.py:33
  90.6 24.2 %collective-permute-start.7 = (bf16[768,768]{1,0:T(8,128)(2,1)}, bf16[768,768]{1,0:T(8,128)(2,1)}, u32[]{:S(2)}, u32[]{:S(2)}) collective-permute-start(bf16[768,768]{1,0:T(8,128)(2,1)} %collective-permute-done.3.refs_5_.refs_1_), channel_id=1, source_target_pairs={{0,2},{2,0},{1,3},{3,1},{4,6},{6,4},{5,7},{7,5},{8,10},{10,8},{9,1... | collective-permute-start | bytes 3538952 | tf_op jit(solution)/shard_map/ppermute | solution.py:29
  92.5 22.3 %collective-permute-start.6 = (bf16[768,768]{1,0:T(8,128)(2,1)}, bf16[768,768]{1,0:T(8,128)(2,1)}, u32[]{:S(2)}, u32[]{:S(2)}) collective-permute-start(bf16[768,768]{1,0:T(8,128)(2,1)} %copy-done.30), channel_id=1, source_target_pairs={{0,2},{2,0},{1,3},{3,1},{4,6},{6,4},{5,7},{7,5},{8,10},{10,8},{9,1... | collective-permute-start | bytes 3538952 | tf_op jit(solution)/shard_map/ppermute | solution.py:29
  92.6 22.2 %collective-permute-start.8 = (bf16[768,768]{1,0:T(8,128)(2,1)}, bf16[768,768]{1,0:T(8,128)(2,1)}, u32[]{:S(2)}, u32[]{:S(2)}) collective-permute-start(bf16[768,768]{1,0:T(8,128)(2,1)} %copy-done.34), channel_id=1, source_target_pairs={{0,2},{2,0},{1,3},{3,1},{4,6},{6,4},{5,7},{7,5},{8,10},{10,8},{9,1... | collective-permute-start | bytes 3538952 | tf_op jit(solution)/shard_map/ppermute | solution.py:29
  93.1 21.7 %collective-permute-start.10 = (bf16[768,768]{1,0:T(8,128)(2,1)}, bf16[768,768]{1,0:T(8,128)(2,1)}, u32[]{:S(2)}, u32[]{:S(2)}) collective-permute-start(bf16[768,768]{1,0:T(8,128)(2,1)} %collective-permute-done.9.refs_7_.refs_3_), channel_id=1, source_target_pairs={{0,2},{2,0},{1,3},{3,1},{4,6},{6,4},{5,7},{7,5},{8,10},{10,8},{9,1... | collective-permute-start | bytes 3538952 | tf_op jit(solution)/shard_map/ppermute | solution.py:29
  120.5 42.8 %collective-permute-start.11 = (bf16[384,3072]{1,0:T(8,128)(2,1)}, bf16[384,3072]{1,0:T(8,128)(2,1)}, u32[]{:S(2)}, u32[]{:S(2)}) collective-permute-start(bf16[384,3072]{1,0:T(8,128)(2,1)} %get-tuple-element.221), channel_id=1, source_target_pairs={{0,2},{2,0},{1,3},{3,1},{4,6},{6,4},{5,7},{7,5},{8,10},{10,8},{9,1... | collective-permute-start | bytes 7077896 | tf_op jit(solution)/shard_map/ppermute | solution.py:29
  144.7 25.8 %all-to-all-start.1 = ((bf16[16,40,896]{2,1,0:T(8,128)(2,1)}), bf16[16,40,896]{2,1,0:T(8,128)(2,1)S(1)}, u32[]{:S(2)}, u32[]{:S(2)}) async-start(bf16[16,40,896]{2,1,0:T(8,128)(2,1)} %bitcast.46), calls=%async_computation.1 | async-start | bytes 2293760 | tf_op jit(solution)/shard_map/all_to_all | solution.py:33
  150.9 51.5 %reduce-scatter.3.cloned.1.call-start = ((), (), s32[]{:S(2)}) async-start(), calls=%async_computation.7 | async-start | bytes 2949120 | tf_op jit(solution)/shard_map/reduce_scatter | solution.py:920
  170.6 16.5 %collective-permute-start.13 = (bf16[4,768,768]{2,1,0:T(8,128)(2,1)}, bf16[4,768,768]{2,1,0:T(8,128)(2,1)}, u32[]{:S(2)}, u32[]{:S(2)}) collective-permute-start(bf16[4,768,768]{2,1,0:T(8,128)(2,1)} %get-tuple-element.232), channel_id=1, source_target_pairs={{0,2},{2,0},{1,3},{3,1},{4,6},{6,4},{5,7},{7,5},{8,10},{10,8},{9,1... | collective-permute-start | bytes 14155784 | tf_op jit(solution)/shard_map/ppermute | solution.py:29
  175.3 19.4 %collective-permute-start.12 = (bf16[512,768]{1,0:T(8,128)(2,1)S(1)}, bf16[512,768]{1,0:T(8,128)(2,1)S(1)}, u32[]{:S(2)}, u32[]{:S(2)}) collective-permute-start(bf16[512,768]{1,0:T(8,128)(2,1)S(1)} %get-tuple-element.225.mine_ref), channel_id=1, source_target_pairs={{0,1},{1,0},{2,3},{3,2},{4,5},{5,4},{6,7},{7,6},{8,9},{9,8},{10,11... | collective-permute-start | bytes 2359304 | tf_op jit(solution)/shard_map/ppermute | solution.py:29
  194.7 43.3 %collective-permute-start.14 = (bf16[2,384,768]{2,1,0:T(8,128)(2,1)}, bf16[2,384,768]{2,1,0:T(8,128)(2,1)}, u32[]{:S(2)}, u32[]{:S(2)}) collective-permute-start(bf16[2,384,768]{2,1,0:T(8,128)(2,1)} %get-tuple-element.252), channel_id=1, source_target_pairs={{0,4},{4,0},{1,5},{5,1},{2,6},{6,2},{3,7},{7,3},{8,12},{12,8},{9,1... | collective-permute-start | bytes 3538952 | tf_op jit(solution)/shard_map/ppermute | solution.py:29
  194.9 43.1 %collective-permute-start.15 = (bf16[2,384,768]{2,1,0:T(8,128)(2,1)}, bf16[2,384,768]{2,1,0:T(8,128)(2,1)}, u32[]{:S(2)}, u32[]{:S(2)}) collective-permute-start(bf16[2,384,768]{2,1,0:T(8,128)(2,1)} %get-tuple-element.253), channel_id=1, source_target_pairs={{0,1},{1,0},{2,3},{3,2},{4,5},{5,4},{6,7},{7,6},{8,9},{9,8},{10,11... | collective-permute-start | bytes 3538952 | tf_op jit(solution)/shard_map/ppermute | solution.py:29
  195.6 42.4 %all-to-all-start.2 = ((bf16[16,40,768]{2,1,0:T(8,128)(2,1)}), bf16[16,40,768]{2,1,0:T(8,128)(2,1)}, u32[]{:S(2)}, u32[]{:S(2)}) async-start(bf16[16,40,768]{2,1,0:T(8,128)(2,1)} %bitcast.22), calls=%async_computation.2 | async-start | bytes 1966080 | tf_op jit(solution)/shard_map/all_to_all | solution.py:33
  202.4 50.5 %reduce-scatter.5.cloned.1.call-start = ((), (), s32[]{:S(2)}) async-start(), calls=%async_computation.8 | async-start | bytes 737280 | tf_op jit(solution)/shard_map/reduce_scatter | solution.py:921
  203.2 148.3 %all-gather.2.cloned.1.call-start = ((), (), s32[]{:S(2)}) async-start(), calls=%async_computation.9 | async-start | bytes 2506752 | tf_op jit(solution)/shard_map/all_gather | solution.py:974
  248.5 14.2 %collective-permute-start.16 = (bf16[384,1536]{1,0:T(8,128)(2,1)}, bf16[384,1536]{1,0:T(8,128)(2,1)}, u32[]{:S(2)}, u32[]{:S(2)}) collective-permute-start(bf16[384,1536]{1,0:T(8,128)(2,1)} %get-tuple-element.261), channel_id=1, source_target_pairs={{0,2},{2,0},{1,3},{3,1},{4,6},{6,4},{5,7},{7,5},{8,10},{10,8},{9,1... | collective-permute-start | bytes 3538952 | tf_op jit(solution)/shard_map/ppermute | solution.py:29
  265.4 24.6 %collective-permute-start.21 = (bf16[384,768]{1,0:T(8,128)(2,1)}, bf16[384,768]{1,0:T(8,128)(2,1)S(1)}, u32[]{:S(2)}, u32[]{:S(2)}) collective-permute-start(bf16[384,768]{1,0:T(8,128)(2,1)} %get-tuple-element.279), channel_id=1, source_target_pairs={{0,1},{1,0},{2,3},{3,2},{4,5},{5,4},{6,7},{7,6},{8,9},{9,8},{10,11... | collective-permute-start | bytes 1769480 | tf_op jit(solution)/shard_map/ppermute | solution.py:29
  265.5 24.5 %collective-permute-start.22 = (bf16[384,768]{1,0:T(8,128)(2,1)}, bf16[384,768]{1,0:T(8,128)(2,1)}, u32[]{:S(2)}, u32[]{:S(2)}) collective-permute-start(bf16[384,768]{1,0:T(8,128)(2,1)} %copy-done.23), channel_id=1, source_target_pairs={{0,4},{4,0},{1,5},{5,1},{2,6},{6,2},{3,7},{7,3},{8,12},{12,8},{9,1... | collective-permute-start | bytes 1769480 | tf_op jit(solution)/shard_map/ppermute | solution.py:29
  273.2 13.2 %collective-permute-start.24 = (bf16[512,768]{1,0:T(8,128)(2,1)}, bf16[512,768]{1,0:T(8,128)(2,1)}, u32[]{:S(2)}, u32[]{:S(2)}) collective-permute-start(bf16[512,768]{1,0:T(8,128)(2,1)} %get-tuple-element.284), channel_id=1, source_target_pairs={{0,2},{2,0},{1,3},{3,1},{4,6},{6,4},{5,7},{7,5},{8,10},{10,8},{9,1... | collective-permute-start | bytes 2359304 | tf_op jit(solution)/shard_map/ppermute | solution.py:29
  274.2 27.2 %collective-permute-start.27 = (bf16[512,768]{1,0:T(8,128)(2,1)}, bf16[512,768]{1,0:T(8,128)(2,1)}, u32[]{:S(2)}, u32[]{:S(2)}) collective-permute-start(bf16[512,768]{1,0:T(8,128)(2,1)} %get-tuple-element.286), channel_id=1, source_target_pairs={{0,2},{2,0},{1,3},{3,1},{4,6},{6,4},{5,7},{7,5},{8,10},{10,8},{9,1... | collective-permute-start | bytes 2359304 | tf_op jit(solution)/shard_map/ppermute | solution.py:29
  275.3 24.0 %all-to-all-start.3 = ((bf16[16,24,1664]{2,1,0:T(8,128)(2,1)}), bf16[16,24,1664]{2,1,0:T(8,128)(2,1)S(1)}, u32[]{:S(2)}, u32[]{:S(2)}) async-start(bf16[16,24,1664]{2,1,0:T(8,128)(2,1)} %pad_maximum_fusion.1), calls=%async_computation.5 | async-start | bytes 2555904 | tf_op jit(solution)/shard_map/all_to_all | solution.py:33
  284.7 19.0 %collective-permute-start.26 = (bf16[512,768]{1,0:T(8,128)(2,1)}, bf16[512,768]{1,0:T(8,128)(2,1)}, u32[]{:S(2)}, u32[]{:S(2)}) collective-permute-start(bf16[512,768]{1,0:T(8,128)(2,1)} %add_convert_fusion.4), channel_id=1, source_target_pairs={{0,1},{1,0},{2,3},{3,2},{4,5},{5,4},{6,7},{7,6},{8,9},{9,8},{10,11... | collective-permute-start | bytes 2359304 | tf_op jit(solution)/shard_map/ppermute | solution.py:29
  288.6 36.5 %collective-permute-start.25 = (bf16[512,768]{1,0:T(8,128)(2,1)}, bf16[512,768]{1,0:T(8,128)(2,1)}, u32[]{:S(2)}, u32[]{:S(2)}) collective-permute-start(bf16[512,768]{1,0:T(8,128)(2,1)} %add_convert_fusion.3), channel_id=1, source_target_pairs={{0,4},{4,0},{1,5},{5,1},{2,6},{6,2},{3,7},{7,3},{8,12},{12,8},{9,1... | collective-permute-start | bytes 2359304 | tf_op jit(solution)/shard_map/ppermute | solution.py:29
  327.5 24.0 %all-to-all-start.4 = ((bf16[16,24,1664]{2,1,0:T(8,128)(2,1)}), bf16[16,24,1664]{2,1,0:T(8,128)(2,1)S(1)}, u32[]{:S(2)}, u32[]{:S(2)}) async-start(bf16[16,24,1664]{2,1,0:T(8,128)(2,1)} %broadcast_in_dim.48), calls=%async_computation.6 | async-start | bytes 2555904 | tf_op jit(solution)/shard_map/all_to_all | solution.py:33
  332.5 19.0 %collective-permute-start.28 = (bf16[512,768]{1,0:T(8,128)(2,1)S(1)}, bf16[512,768]{1,0:T(8,128)(2,1)}, u32[]{:S(2)}, u32[]{:S(2)}) collective-permute-start(bf16[512,768]{1,0:T(8,128)(2,1)S(1)} %add_convert_fusion.1.mine_ref), channel_id=1, source_target_pairs={{0,1},{1,0},{2,3},{3,2},{4,5},{5,4},{6,7},{7,6},{8,9},{9,8},{10,11... | collective-permute-start | bytes 2359304 | tf_op jit(solution)/shard_map/ppermute | solution.py:29
  351.5 19.1 %collective-permute-start.30 = (bf16[384,3072]{1,0:T(8,128)(2,1)}, bf16[384,3072]{1,0:T(8,128)(2,1)}, u32[]{:S(2)}, u32[]{:S(2)}) collective-permute-start(bf16[384,3072]{1,0:T(8,128)(2,1)} %all-gather.2.cloned.1.call-done.mine_ref), channel_id=1, source_target_pairs={{0,2},{2,0},{1,3},{3,1},{4,6},{6,4},{5,7},{7,5},{8,10},{10,8},{9,1... | collective-permute-start | bytes 7077896 | tf_op jit(solution)/shard_map/ppermute | solution.py:29
  (50 other events, 366.2 us)
Sparse Core Ops, SparseCore 0:
  171.7 29.3 reduce-scatter.2
  205.7 24.2 reduce-scatter.4
  263.5 54.7 all-gather.1
where the time goes:
time: 390 us; the launch traced here: 384 us
  Pallas kernels  183 us (47%)
  waiting for transfers between devices  80.9 us (21%)
  starting transfers between devices  69.8 us (18%)
  local copies, waits for them, and re-layouts  18.2 us (5%)
  other arithmetic  15.3 us (4%)
  between operations  14.5 us (4%)
    pallas_call x21, Pallas kernels, call(): pl.pallas_call(kernel, **{} if grid is None else {'grid': grid}, in_specs...  165 us
    ppermute x30, waiting for transfers between devices, swap(): return lax.ppermute(x, axis, [(0, 1), (1, 0)])  56.3 us
    ppermute x30, starting transfers between devices, swap(): return lax.ppermute(x, axis, [(0, 1), (1, 0)])  34.6 us
    all_to_all x5, starting transfers between devices, exchange(): return lax.all_to_all(x, axis, split_axis=0, concat_axis=0, tiled=True)  34 us
    all_to_all x5, waiting for transfers between devices, exchange(): return lax.all_to_all(x, axis, split_axis=0, concat_axis=0, tiled=True)  23.9 us
    pallas_call x2, Pallas kernels, half_call(): pl.pallas_call(kernel, grid_spec=pltpu.PrefetchScalarGridSpec(num_scalar_...  18.6 us
    unnamed x90, local copies, waits for them, and re-layouts  14.1 us
  transfers between devices with their start and end apart: 39, of which 11 were waited for; matrix products, arithmetic and copies ran while one was open for 6% of the time, Pallas kernels for 46%

commit v1 on v0

--- a/solution.py
+++ b/solution.py
@@ -17,6 +17,7 @@
 EXPERT = AXES[:5]
 ROUTE = ("zh", "x", "yh")
 PLANE = ("x", "yh", "yl")
+CHIPS = ("zh",) + PLANE
 
 epsilon = 1e-06
 rope_base = 10000.0
@@ -319,7 +320,7 @@
 
 
 def half_sum_kernel(kept_ref, taken_ref, out_ref):
-    out_ref[...] = (kept_ref[...].astype(f32) + taken_ref[...].astype(f32)).astype(bf16)
+    out_ref[...] = kept_ref[...] + taken_ref[...]
 
 
 def second_kernel(x_ref, mine_ref, theirs_ref, gain_ref, turned_ref, cot_ref, middle_ref, n_ref, sent_ref):
@@ -372,7 +373,7 @@
 def shared(normed, cot, shared_gate, shared_up, shared_down, router, routes):
     rows, width = normed.shape
     hidden = shared_gate.shape[1]
-    block = 256
+    block = 512
     columns = pl.BlockSpec((width, block), lambda k: (0, k))
     of_hidden = pl.BlockSpec((rows, block), lambda k: (0, k))
     return call(
@@ -621,7 +622,7 @@
 def expert_sum_kernel(kept_ref, taken_ref, high_ref, tensor_ref, keep_high_ref, keep_tensor_ref):
     shard = pl.program_id(0)
     half = kept_ref.shape[1] // 2
-    total = (kept_ref[0].astype(f32) + taken_ref[0].astype(f32)).astype(bf16)
+    total = kept_ref[0] + taken_ref[0]
     for ref, at, here in (
         (keep_high_ref, 0, shard < 2),
         (high_ref, 0, shard >= 2),
@@ -634,10 +635,10 @@
 
 
 def expert_sums_kernel(kh_ref, fh_ref, kt_ref, ft_ref, to_t_ref, to_y_ref, kept_u_ref, kept_l_ref):
-    to_t_ref[...] = (kh_ref[1].astype(f32) + fh_ref[1].astype(f32)).astype(bf16)
-    to_y_ref[...] = (kt_ref[1].astype(f32) + ft_ref[1].astype(f32)).astype(bf16)
-    kept_u_ref[...] = (kh_ref[0].astype(f32) + fh_ref[0].astype(f32)).astype(bf16)
-    kept_l_ref[...] = (kt_ref[0].astype(f32) + ft_ref[0].astype(f32)).astype(bf16)
+    to_t_ref[...] = kh_ref[1] + fh_ref[1]
+    to_y_ref[...] = kt_ref[1] + ft_ref[1]
+    kept_u_ref[...] = kh_ref[0] + fh_ref[0]
+    kept_l_ref[...] = kt_ref[0] + ft_ref[0]
 
 
 def expert_out_kernel(ku_ref, fu_ref, kl_ref, fl_ref, gate_ref, up_ref, down_ref):
@@ -894,9 +895,12 @@
     )
     picked = exchange(picked.reshape(experts, SLOTS, width), ROUTE).reshape(seats, width)
     from_high, from_tensor = swap(to_high, "yl"), swap(to_tensor, "t")
-    dq, dka, dva, dkb, dvb, picked, from_high, from_tensor = lax.optimization_barrier(
-        (dq, dka, dva, dkb, dvb, picked, from_high, from_tensor)
-    )
+    early = lax.psum_scatter(early, "x", scatter_dimension=0, tiled=True)
+    early = lax.psum_scatter(early, ("yh", "yl"), scatter_dimension=0, tiled=True)
+    dq, dka, dva, dkb, dvb, picked, from_high, from_tensor, early = lax.optimization_barrier(
+        (dq, dka, dva, dkb, dvb, picked, from_high, from_tensor, early)
+    )
+    early_zh = swap(early, "zh")
     late_given, late_kept, small_given, small_kept = half_call(
         functools.partial(late_weights_kernel, experts=experts),
         "late_weights",
@@ -917,18 +921,15 @@
         (keep_high, after(from_high, late_given), keep_tensor, from_tensor),
         [((width // 2, 3 * part), bf16)] * 4,
     )
-    early = lax.psum_scatter(early, "x", scatter_dimension=0, tiled=True)
-    early = lax.psum_scatter(early, ("yh", "yl"), scatter_dimension=0, tiled=True)
-    early_zh = swap(after(early, late_given), "zh")
-    late_taken, small, next_t, next_y, kept_u, kept_l, early, early_zh = lax.optimization_barrier(
-        (swap(late_given, "c"), small, *sums, early, early_zh)
+    early = early.astype(f32) + after(early_zh, late_given).astype(f32)
+    early = lax.all_gather(early.astype(bf16), PLANE, axis=0, tiled=True)
+    late_taken, small, next_t, next_y, kept_u, kept_l = lax.optimization_barrier(
+        (swap(late_given, "c"), small, *sums)
     )
     total = late_kept.astype(f32) + late_taken.astype(f32)
     total = jnp.concatenate([total, small], axis=1).astype(bf16)
     parts = exchange(total.reshape(16, -1, total.shape[1]), PLANE)
-    parts, from_next_t, from_next_y = lax.optimization_barrier(
-        (parts, swap(next_t, "t"), swap(next_y, "yl"))
-    )
+    parts, from_next_t = lax.optimization_barrier((parts, swap(next_t, "t")))
 
     to_core, to_far, to_y, own_part = call(
         normed_back_kernel,
@@ -941,15 +942,26 @@
     from_y = swap((to_y + from_far).astype(bf16), "yl")
     block_part = (shared_out + dot(after(placer, total), picked)).astype(bf16)
     part_sum = jnp.sum(parts.astype(f32), axis=0).astype(bf16)
-    part_zh, from_y, from_block, own_part = lax.optimization_barrier(
-        (swap(part_sum, "zh"), from_y, swap(block_part, "t"), own_part)
-    )
-    own_part = (own_part + from_y.astype(f32)).astype(bf16)
+    part_zh, from_block, own_part = lax.optimization_barrier(
+        (swap(part_sum, "zh"), swap(block_part, "t"), own_part)
+    )
     total = (part_sum.astype(f32) + part_zh.astype(f32)).astype(bf16)
-    total, from_t = lax.optimization_barrier(
-        (spread(after(total, own_part)), swap(own_part, "t"))
-    )
-    block_out = (middle + block_part.astype(f32) + from_block.astype(f32)).astype(bf16)
+    own_part = (own_part + after(from_y, total).astype(f32)).astype(bf16)
+    block_out = (middle + block_part.astype(f32) + after(from_block, own_part).astype(f32)).astype(bf16)
+    hidden = (width, shared_part)
+    early = after(early, own_part)
+    shared_grads = call(
+        early_out_kernel,
+        "early_out",
+        (core[None], early, swap(early, "c")),
+        [(hidden, f32), (hidden, f32), (hidden[::-1], f32)],
+        smem=(0,),
+    )
+    from_next_y = swap(after(next_y, own_part), "yl")
+    total, from_t, block_out, *shared_grads = lax.optimization_barrier(
+        (spread(total), swap(own_part, "t"), block_out, *shared_grads)
+    )
+    grad_shared_gate, grad_shared_up, grad_shared_down = shared_grads
     (grad_tokens,) = call(
         first_kernel,
         "first",
@@ -967,19 +979,8 @@
     grad_expert_gate, grad_expert_up, grad_expert_down = call(
         expert_out_kernel,
         "expert_out",
-        (kept_u, from_next_t, kept_l, from_next_y),
+        (kept_u, from_next_t, kept_l, after(from_next_y, grad_query)),
         [((1, width, part), f32), ((1, width, part), f32), ((1, part, width), f32)],
-    )
-    early = (early.astype(f32) + early_zh.astype(f32)).astype(bf16)
-    early = lax.all_gather(early, PLANE, axis=0, tiled=True)
-    early = after(early, from_t)
-    hidden = (width, shared_part)
-    grad_shared_gate, grad_shared_up, grad_shared_down = call(
-        early_out_kernel,
-        "early_out",
-        (core[None], early, swap(early, "c")),
-        [(hidden, f32), (hidden, f32), (hidden[::-1], f32)],
-        smem=(0,),
     )
     return (
         block_out,

time: 390 us -> 379 us (0.972)
  waiting for transfers between devices: 80.9 us -> 71.2 us
  Pallas kernels: 183 us -> 179 us
    all_to_all x5, waiting for transfers between devices: 23.9 us -> 12.8 us  [exchange(): return lax.all_to_all(x, axis, split_axis=0, concat_axis=0, tiled=True)]
    reduce_scatter x1, waiting for transfers between devices: 0.02 us -> 4.28 us  [local(): early = lax.psum_scatter(early, 'x', scatter_dimension=0, tiled=True)]
    pallas_call x21, Pallas kernels: 165 us -> 161 us  [call(): pl.pallas_call(kernel, **{} if grid is None else {'grid': grid}, in_specs...]
    unnamed x90 -> x96, local copies, waits for them, and re-layouts: 14.1 us -> 14.6 us
  transfers between devices with their start and end apart: 39 -> 39, of which waited for: 11 -> 15; matrix products, arithmetic and copies ran while one was open for 6% -> 6% of each run, Pallas kernels for 46% -> 47%
where the time goes in v1:
time: 379 us; the launch traced here: 373 us
  Pallas kernels  179 us (47%)
  starting transfers between devices  71.2 us (19%)
  waiting for transfers between devices  71.2 us (19%)
  local copies, waits for them, and re-layouts  18.8 us (5%)
  other arithmetic  16.2 us (4%)
  between operations  14.4 us (4%)
    pallas_call x21, Pallas kernels, call(): pl.pallas_call(kernel, **{} if grid is None else {'grid': grid}, in_specs...  161 us
    ppermute x30, waiting for transfers between devices, swap(): return lax.ppermute(x, axis, [(0, 1), (1, 0)])  52.6 us
    all_to_all x5, starting transfers between devices, exchange(): return lax.all_to_all(x, axis, split_axis=0, concat_axis=0, tiled=True)  35.9 us
    ppermute x30, starting transfers between devices, swap(): return lax.ppermute(x, axis, [(0, 1), (1, 0)])  34.3 us
    pallas_call x2, Pallas kernels, half_call(): pl.pallas_call(kernel, grid_spec=pltpu.PrefetchScalarGridSpec(num_scalar_...  18.6 us
    unnamed x96, local copies, waits for them, and re-layouts  14.6 us
    all_to_all x5, waiting for transfers between devices, exchange(): return lax.all_to_all(x, axis, split_axis=0, concat_axis=0, tiled=True)  12.8 us
  transfers between devices with their start and end apart: 39, of which 15 were waited for; matrix products, arithmetic and copies ran while one was open for 6% of the time, Pallas kernels for 47%

profile of v1, /device:TPU:1, one launch (start us, length us, event | category | flops | bytes accessed | tf_op | source)
XLA Modules:
  0.0 373.1 jit_solution(7431658074496927996)
XLA Ops:
  16.3 3.8 %route.1 = (bf16[512,640]{1,0:T(8,128)(2,1)S(1)}, bf16[640,512]{1,0:T(8,128)(2,1)S(1)}, bf16[640,896]{1,0:T(8,128)(2,1)}) custom-call(s32[1]{0:T(128)} %bitcast.10.tensor_ref, s32[512,2]{1,0:T(8,128)S(1)} %copy.41.routes_ref, bf16[512,768]{1,0:T(8,128)(2,1)} %cot_ref.7, bf16[128,640]{1,0:T(8,128)(2,1)S(1)} %copy-done.31, f32[1,640]{1,0:T(1,128)S(1)} %copy-done.32), custom_call_target="tpu_custom_call" | custom-call | flops 920000000 | bytes 1048576 | tf_op jit(solution)/shard_map/route/pallas_call | solution.py:115
  21.5 6.2 %project.2 = (bf16[1024,768]{1,0:T(8,128)(2,1)}, bf16[1024,384]{1,0:T(8,128)(2,1)}, bf16[1024,384]{1,0:T(8,128)(2,1)}, bf16[512,384]{1,0:T(8,128)(2,1)S(1)}) custom-call(bf16[512,768]{1,0:T(8,128)(2,1)} %x_ref.3, bf16[512,768]{1,0:T(8,128)(2,1)} %collective-permute-done.x1_ref, f32[1,768]{1,0:T(1,128)S(1)} %broadcast_in_dim.23.gain_ref.scale_ref, ...), custom_call_target="tpu_custom_call" | custom-call | flops 1150000000 | bytes 1048576 | tf_op jit(solution)/shard_map/project/pallas_call | solution.py:115
  34.9 5.2 %project.3 = (bf16[1024,768]{1,0:T(8,128)(2,1)}, bf16[1024,384]{1,0:T(8,128)(2,1)}, bf16[1024,384]{1,0:T(8,128)(2,1)}) custom-call(bf16[512,768]{1,0:T(8,128)(2,1)} %collective-permute-done.1.x0_ref, bf16[512,768]{1,0:T(8,128)(2,1)} %copy-done.45, f32[1,768]{1,0:T(1,128)S(1)} %broadcast_in_dim.23.gain_ref.scale_ref, bf16[768,384]{1,0:T(8,128)(2,1)S(1)} %copy-done.1, ...), custom_call_target="tpu_custom_call" | custom-call | flops 1150000000 | bytes 1048576 | tf_op jit(solution)/shard_map/project/pallas_call | solution.py:115
  40.1 14.0 %attend.1 = (bf16[512,384]{1,0:T(8,128)(2,1)S(1)}, f32[512,384]{1,0:T(8,128)}, bf16[512,768]{1,0:T(8,128)(2,1)}) custom-call(f32[4]{0:T(128)S(1)} %add_select_fusion.hide_ref, bf16[512,384]{1,0:T(8,128)(2,1)S(1)} %copy-done.29, bf16[1024,384]{1,0:T(8,128)(2,1)} %get-tuple-element.173.ka_ref, bf16[1024,384]{1,0:T(8,128)(2,1)} %get-tuple-element.174.va_ref, ...), custom_call_target="tpu_custom_call" | custom-call | flops 3220000000 | bytes 1048576 | tf_op jit(solution)/shard_map/attend/pallas_call | solution.py:115
  59.2 4.0 %turn_rows.1 = (bf16[768,1024]{1,0:T(8,128)(2,1)S(1)}, bf16[768,1024]{1,0:T(8,128)(2,1)}) custom-call(bf16[1024,768]{1,0:T(8,128)(2,1)} %get-tuple-element.182.a_ref, bf16[1024,768]{1,0:T(8,128)(2,1)} %get-tuple-element.183.b_ref), custom_call_target="tpu_custom_call" | custom-call | flops 690000000 | bytes 1048576 | tf_op jit(solution)/shard_map/turn_rows/pallas_call | solution.py:115
  64.4 9.9 %collective-permute-done.4.theirs_ref = bf16[512,768]{1,0:T(8,128)(2,1)S(1)} collective-permute-done((bf16[512,768]{1,0:T(8,128)(2,1)}, bf16[512,768]{1,0:T(8,128)(2,1)S(1)}, u32[]{:S(2)}, u32[]{:S(2)}) %collective-permute-start.4) | collective-permute-done | bytes 786464 | tf_op jit(solution)/shard_map/ppermute | solution.py:30
  75.3 4.8 %second.1 = (f32[512,768]{1,0:T(8,128)}, bf16[512,768]{1,0:T(8,128)(2,1)S(1)}, bf16[640,1664]{1,0:T(8,128)(2,1)}) custom-call(bf16[512,768]{1,0:T(8,128)(2,1)} %x_ref.3, bf16[512,768]{1,0:T(8,128)(2,1)} %get-tuple-element.180.mine_ref, bf16[512,768]{1,0:T(8,128)(2,1)} %copy-done.38, f32[1,768]{1,0:T(1,128)S(1)} %broadcast_in_dim.46.gain_ref, ...), custom_call_target="tpu_custom_call" | custom-call | flops 920000000 | bytes 1048576 | tf_op jit(solution)/shard_map/second/pallas_call | solution.py:115
  80.0 10.0 %all-to-all-start = ((bf16[16,40,1664]{2,1,0:T(8,128)(2,1)}), bf16[16,40,1664]{2,1,0:T(8,128)(2,1)}, u32[]{:S(2)}, u32[]{:S(2)}) async-start(bf16[16,40,1664]{2,1,0:T(8,128)(2,1)} %bitcast.43), calls=%async_computation | async-start | bytes 4259840 | tf_op jit(solution)/shard_map/all_to_all | solution.py:34
  93.4 11.2 %shared.1 = (bf16[512,1024]{1,0:T(8,128)(2,1)}, bf16[512,1024]{1,0:T(8,128)(2,1)}, bf16[512,1024]{1,0:T(8,128)(2,1)}, f32[512,768]{1,0:T(8,128)}, f32[512,768]{1,0:T(8,128)}, /*index=5*/f32[512,128]{1,0:T(8,128)S(1)}) custom-call(bf16[512,768]{1,0:T(8,128)(2,1)S(1)} %get-tuple-element.189.n_ref.n2_ref, bf16[512,768]{1,0:T(8,128)(2,1)} %cot_ref.7, ...), custom_call_target="tpu_custom_call" | custom-call | flops 2760000000 | bytes 1048576 | tf_op jit(solution)/shard_map/shared/pallas_call | solution.py:115
  104.6 8.2 %shared_weights.1 = (bf16[384,3072]{1,0:T(8,128)(2,1)}, bf16[384,3072]{1,0:T(8,128)(2,1)}) custom-call(s32[1]{0:T(128)} %bitcast.core_ref, bf16[512,768]{1,0:T(8,128)(2,1)S(1)} %get-tuple-element.189.n_ref.n2_ref, bf16[512,768]{1,0:T(8,128)(2,1)S(1)} %copy-done.10, bf16[512,1024]{1,0:T(8,128)(2,1)} %get-tuple-element.193.gg_ref, ...), custom_call_target="tpu_custom_call" | custom-call | flops 1380000000 | bytes 1048576 | tf_op jit(solution)/shard_map/shared_weights/pallas_call | solution.py:418
  112.8 6.4 %all-to-all-done = bf16[16,40,1664]{2,1,0:T(8,128)(2,1)} async-done(((bf16[16,40,1664]{2,1,0:T(8,128)(2,1)}), bf16[16,40,1664]{2,1,0:T(8,128)(2,1)}, u32[]{:S(2)}, u32[]{:S(2)}) %all-to-all-start) | async-done | bytes 2129952 | tf_op jit(solution)/shard_map/all_to_all | solution.py:34
  122.2 20.7 %expert_rows.1 = (bf16[8,640,256]{2,1,0:T(8,128)(2,1)}, bf16[8,640,512]{2,1,0:T(8,128)(2,1)}, bf16[640,896]{1,0:T(8,128)(2,1)}, bf16[640,768]{1,0:T(8,128)(2,1)S...) custom-call(s32[1]{0:T(128)} %bitcast.17.here_ref, bf16[640,1664]{1,0:T(8,128)(2,1)} %bitcast.19.sent_ref, ...), custom_call_target="tpu_custom_call" | custom-call | flops 4600000000 | bytes 1048576 | tf_op jit(solution)/shard_map/expert_rows/pallas_call | solution.py:115
  143.8 6.1 %all-to-all-start.1 = ((bf16[16,40,896]{2,1,0:T(8,128)(2,1)}), bf16[16,40,896]{2,1,0:T(8,128)(2,1)}, u32[]{:S(2)}, u32[]{:S(2)}) async-start(bf16[16,40,896]{2,1,0:T(8,128)(2,1)} %bitcast.45), calls=%async_computation.1 | async-start | bytes 2293760 | tf_op jit(solution)/shard_map/all_to_all | solution.py:34
  149.9 10.3 %expert_given.1 = (bf16[4,768,768]{2,1,0:T(8,128)(2,1)}, f32[640,768]{1,0:T(8,128)}, bf16[768,640]{1,0:T(8,128)(2,1)S(1)}, bf16[768,640]{1,0:T(8,128)(2,1)S(1)}) custom-call(bf16[640,768]{1,0:T(8,128)(2,1)} %copy-done.9, bf16[640,768]{1,0:T(8,128)(2,1)} %get-tuple-element.215.out_ref, bf16[8,640,256]{2,1,0:T(8,128)(2,1)} %get-tuple-element.216.hidden_ref, ...), custom_call_target="tpu_custom_call" | custom-call | flops 2070000000 | bytes 1048576 | tf_op jit(solution)/shard_map/expert_given/pallas_call | solution.py:115
  162.2 4.0 %half_sum.1 = bf16[384,3072]{1,0:T(8,128)(2,1)} custom-call(bf16[384,3072]{1,0:T(8,128)(2,1)} %get-tuple-element.223.kept_ref, bf16[384,3072]{1,0:T(8,128)(2,1)} %collective-permute-done.11.taken_ref), custom_call_target="tpu_custom_call" | custom-call | flops 920000000 | bytes 1048576 | tf_op jit(solution)/shard_map/half_sum/pallas_call | solution.py:115
  170.7 3.6 combine.1
  175.3 10.8 %expert_kept.1 = (bf16[4,768,768]{2,1,0:T(8,128)(2,1)}, bf16[640,768]{1,0:T(8,128)(2,1)}) custom-call(bf16[768,640]{1,0:T(8,128)(2,1)} %copy-done.7, bf16[768,640]{1,0:T(8,128)(2,1)} %copy-done.8, f32[640,128]{1,0:T(8,128)S(1)} %get-tuple-element.232.share_ref, f32[640,768]{1,0:T(8,128)} %get-tuple-element.233.first_ref, ...), custom_call_target="tpu_custom_call" | custom-call | flops 2070000000 | bytes 1048576 | tf_op jit(solution)/shard_map/expert_kept/pallas_call | solution.py:115
  186.2 6.4 %expert_sum.1 = (bf16[2,384,768]{2,1,0:T(8,128)(2,1)S(1)}, bf16[2,384,768]{2,1,0:T(8,128)(2,1)}, bf16[2,384,768]{2,1,0:T(8,128)(2,1)}, bf16[2,384,768]{2,1,0:T(8,128)(2,1)}) custom-call(bf16[4,768,768]{2,1,0:T(8,128)(2,1)} %get-tuple-element.234.kept_ref, bf16[4,768,768]{2,1,0:T(8,128)(2,1)} %collective-permute-done.13.taken_ref), custom_call_target="tpu_custom_call" | custom-call | flops 920000000 | bytes 1048576 | tf_op jit(solution)/shard_map/expert_sum/pallas_call | solution.py:115
  196.4 4.3 %reduce-scatter.3.cloned.1.call-done = bf16[96,3072]{1,0:T(8,128)(2,1)} async-done(((bf16[384,3072]{1,0:T(8,128)(2,1)}), bf16[96,3072]{1,0:T(8,128)(2,1)}) %reduce-scatter.3.cloned.1.call-update) | async-done | bytes 589840 | tf_op jit(solution)/shard_map/reduce_scatter | solution.py:898
  202.0 7.3 %all-to-all-start.2 = ((bf16[16,40,768]{2,1,0:T(8,128)(2,1)}), bf16[16,40,768]{2,1,0:T(8,128)(2,1)}, u32[]{:S(2)}, u32[]{:S(2)}) async-start(bf16[16,40,768]{2,1,0:T(8,128)(2,1)} %bitcast.22), calls=%async_computation.2 | async-start | bytes 1966080 | tf_op jit(solution)/shard_map/all_to_all | solution.py:34
  209.5 4.4 %back_two.1 = (f32[512,768]{1,0:T(8,128)}, bf16[512,768]{1,0:T(8,128)(2,1)S(1)}, bf16[512,384]{1,0:T(8,128)(2,1)S(1)}, f32[1,768]{1,0:T(1,128)S(1)}) custom-call(f32[512,768]{1,0:T(8,128)} %get-tuple-element.190.middle_ref, bf16[512,768]{1,0:T(8,128)(2,1)} %copy-done.11, bf16[512,768]{1,0:T(8,128)(2,1)} %copy-done.37, bf16[512,768]{1,0:T(8,128)(2,1)} %cot_ref.7, ...), custom_call_target="tpu_custom_call" | custom-call | flops 920000000 | bytes 1048576 | tf_op jit(solution)/shard_map/back_two/pallas_call | solution.py:115
  214.8 23.4 %attend_back.1 = (bf16[512,384]{1,0:T(8,128)(2,1)S(1)}, bf16[1024,384]{1,0:T(8,128)(2,1)}, bf16[1024,384]{1,0:T(8,128)(2,1)}, bf16[1024,384]{1,0:T(8,128)(2,1)}, bf16[1024,384]{1,0:T(8,128)(2,1)}) custom-call(f32[4]{0:T(128)S(1)} %add_select_fusion.hide_ref, bf16[512,384]{1,0:T(8,128)(2,1)S(1)} %copy-done.30, bf16[1024,384]{1,0:T(8,128)(2,1)} %get-tuple-element.173.ka_ref, ...), custom_call_target="tpu_custom_call" | custom-call | flops 5289999872 | bytes 1048576 | tf_op jit(solution)/shard_map/attend_back/pallas_call | solution.py:115
  241.7 10.4 %late_weights.1 = (bf16[384,1536]{1,0:T(8,128)(2,1)}, bf16[384,1536]{1,0:T(8,128)(2,1)}, bf16[384,128]{1,0:T(8,128)(2,1)S(1)}, bf16[384,128]{1,0:T(8,128)(2,1)S(1)}) custom-call(s32[1]{0:T(128)} %bitcast.core_ref, bf16[512,768]{1,0:T(8,128)(2,1)} %copy-done.12, bf16[512,768]{1,0:T(8,128)(2,1)} %copy-done.13, f32[1,768]{1,0:T(1,128)S(1)} %get-tuple-element.243.gain_ref, ...), custom_call_target="tpu_custom_call" | custom-call | flops 1840000000 | bytes 1048576 | tf_op jit(solution)/shard_map/late_weights/pallas_call | solution.py:418
  265.1 5.5 %all-to-all-start.3 = ((bf16[16,24,1664]{2,1,0:T(8,128)(2,1)}), bf16[16,24,1664]{2,1,0:T(8,128)(2,1)}, u32[]{:S(2)}, u32[]{:S(2)}) async-start(bf16[16,24,1664]{2,1,0:T(8,128)(2,1)} %pad_maximum_fusion), calls=%async_computation.5 | async-start | bytes 2555904 | tf_op jit(solution)/shard_map/all_to_all | solution.py:34
  270.7 7.6 %normed_back.1 = (bf16[512,768]{1,0:T(8,128)(2,1)}, bf16[512,768]{1,0:T(8,128)(2,1)}, f32[512,768]{1,0:T(8,128)}, f32[512,768]{1,0:T(8,128)}) custom-call(bf16[512,384]{1,0:T(8,128)(2,1)S(1)} %get-tuple-element.284.dq_ref, bf16[1024,384]{1,0:T(8,128)(2,1)} %get-tuple-element.259.dka_ref, bf16[1024,384]{1,0:T(8,128)(2,1)} %get-tuple-element.261.dva_ref, ...), custom_call_target="tpu_custom_call" | custom-call | flops 1840000000 | bytes 1048576 | tf_op jit(solution)/shard_map/normed_back/pallas_call | solution.py:115
  286.5 7.3 %collective-permute-done.20.fu_ref = bf16[384,768]{1,0:T(8,128)(2,1)S(1)} collective-permute-done((bf16[384,768]{1,0:T(8,128)(2,1)S(1)}, bf16[384,768]{1,0:T(8,128)(2,1)S(1)}, u32[]{:S(2)}, u32[]{:S(2)}) %collective-permute-start.20) | collective-permute-done | bytes 589856 | tf_op jit(solution)/shard_map/ppermute | solution.py:30
  298.3 12.5 %collective-permute-done.22 = bf16[512,768]{1,0:T(8,128)(2,1)} collective-permute-done((bf16[512,768]{1,0:T(8,128)(2,1)}, bf16[512,768]{1,0:T(8,128)(2,1)}, u32[]{:S(2)}, u32[]{:S(2)}) %collective-permute-start.22) | collective-permute-done | bytes 786464 | tf_op jit(solution)/shard_map/ppermute | solution.py:30
  318.0 6.9 %all-to-all-start.4 = ((bf16[16,24,1664]{2,1,0:T(8,128)(2,1)}), bf16[16,24,1664]{2,1,0:T(8,128)(2,1)S(1)}, u32[]{:S(2)}, u32[]{:S(2)}) async-start(bf16[16,24,1664]{2,1,0:T(8,128)(2,1)} %broadcast_in_dim.48), calls=%async_computation.6 | async-start | bytes 2555904 | tf_op jit(solution)/shard_map/all_to_all | solution.py:34
  328.4 6.8 %early_out.1 = (f32[768,1024]{1,0:T(8,128)}, f32[768,1024]{1,0:T(8,128)}, f32[1024,768]{1,0:T(8,128)}) custom-call(s32[1]{0:T(128)} %bitcast.core_ref, bf16[384,3072]{1,0:T(8,128)(2,1)} %all-gather.2.cloned.1.call-done.mine_ref, bf16[384,3072]{1,0:T(8,128)(2,1)} %collective-permute-done.28.theirs_ref), custom_call_target="tpu_custom_call" | custom-call | flops 1150000000 | bytes 1048576 | tf_op jit(solution)/shard_map/early_out/pallas_call | solution.py:115
  335.3 8.9 %collective-permute-done.26.theirs_ref = bf16[512,768]{1,0:T(8,128)(2,1)} collective-permute-done((bf16[512,768]{1,0:T(8,128)(2,1)S(1)}, bf16[512,768]{1,0:T(8,128)(2,1)}, u32[]{:S(2)}, u32[]{:S(2)}) %collective-permute-start.26) | collective-permute-done | bytes 786464 | tf_op jit(solution)/shard_map/ppermute | solution.py:30
  351.4 3.8 %late_out.1 = (f32[768,384]{1,0:T(8,128)}, f32[768,384]{1,0:T(8,128)}, f32[768,384]{1,0:T(8,128)}, f32[384,768]{1,0:T(8,128)}, f32[768,128]{1,0:T(8,128)S(1)}) custom-call(s32[1]{0:T(128)} %bitcast.core_ref, bf16[384,1664]{1,0:T(8,128)(2,1)S(1)} %bitcast.37, bf16[384,1664]{1,0:T(8,128)(2,1)} %copy-done.44), custom_call_target="tpu_custom_call" | custom-call | flops 920000000 | bytes 1048576 | tf_op jit(solution)/shard_map/late_out/pallas_call | solution.py:115
  355.2 6.6 %collective-permute-done.30.fl_ref = bf16[384,768]{1,0:T(8,128)(2,1)} collective-permute-done((bf16[384,768]{1,0:T(8,128)(2,1)}, bf16[384,768]{1,0:T(8,128)(2,1)}, u32[]{:S(2)}, u32[]{:S(2)}) %collective-permute-start.30) | collective-permute-done | bytes 589856 | tf_op jit(solution)/shard_map/ppermute | solution.py:30
  (191 shorter events, 97.3 us)
Async XLA Ops:
  7.2 21.3 %collective-permute-start.1 = (bf16[512,768]{1,0:T(8,128)(2,1)}, bf16[512,768]{1,0:T(8,128)(2,1)}, u32[]{:S(2)}, u32[]{:S(2)}) collective-permute-start(bf16[512,768]{1,0:T(8,128)(2,1)} %x_ref.3), channel_id=1, source_target_pairs={{0,4},{4,0},{1,5},{5,1},{2,6},{6,2},{3,7},{7,3},{8,12},{12,8},{9,1... | collective-permute-start | bytes 2359304 | tf_op jit(solution)/shard_map/ppermute | solution.py:30
  9.4 12.1 %collective-permute-start = (bf16[512,768]{1,0:T(8,128)(2,1)}, bf16[512,768]{1,0:T(8,128)(2,1)}, u32[]{:S(2)}, u32[]{:S(2)}) collective-permute-start(bf16[512,768]{1,0:T(8,128)(2,1)} %x_ref.3), channel_id=1, source_target_pairs={{0,2},{2,0},{1,3},{3,1},{4,6},{6,4},{5,7},{7,5},{8,10},{10,8},{9,1... | collective-permute-start | bytes 2359304 | tf_op jit(solution)/shard_map/ppermute | solution.py:30
  28.5 27.7 %collective-permute-start.3 = (bf16[768,768]{1,0:T(8,128)(2,1)}, bf16[768,768]{1,0:T(8,128)(2,1)}, u32[]{:S(2)}, u32[]{:S(2)}) collective-permute-start(bf16[768,768]{1,0:T(8,128)(2,1)} %pad_maximum_fusion.2.refs_4_.refs_0_), channel_id=1, source_target_pairs={{0,1},{1,0},{2,3},{3,2},{4,5},{5,4},{6,7},{7,6},{8,9},{9,8},{10,11... | collective-permute-start | bytes 3538952 | tf_op jit(solution)/shard_map/ppermute | solution.py:30
  30.2 34.3 %collective-permute-start.5 = (bf16[768,768]{1,0:T(8,128)(2,1)}, bf16[768,768]{1,0:T(8,128)(2,1)}, u32[]{:S(2)}, u32[]{:S(2)}) collective-permute-start(bf16[768,768]{1,0:T(8,128)(2,1)} %pad_maximum_fusion.2.refs_4_.refs_0_), channel_id=1, source_target_pairs={{0,4},{4,0},{1,5},{5,1},{2,6},{6,2},{3,7},{7,3},{8,12},{12,8},{9,1... | collective-permute-start | bytes 3538952 | tf_op jit(solution)/shard_map/ppermute | solution.py:30
  56.2 18.2 %collective-permute-start.4 = (bf16[512,768]{1,0:T(8,128)(2,1)}, bf16[512,768]{1,0:T(8,128)(2,1)S(1)}, u32[]{:S(2)}, u32[]{:S(2)}) collective-permute-start(bf16[512,768]{1,0:T(8,128)(2,1)} %get-tuple-element.180.mine_ref), channel_id=1, source_target_pairs={{0,1},{1,0},{2,3},{3,2},{4,5},{5,4},{6,7},{7,6},{8,9},{9,8},{10,11... | collective-permute-start | bytes 2359304 | tf_op jit(solution)/shard_map/ppermute | solution.py:30
  57.4 35.4 %collective-permute-start.9 = (bf16[768,768]{1,0:T(8,128)(2,1)}, bf16[768,768]{1,0:T(8,128)(2,1)}, u32[]{:S(2)}, u32[]{:S(2)}) collective-permute-start(bf16[768,768]{1,0:T(8,128)(2,1)} %collective-permute-done.3.refs_5_.refs_1_), channel_id=1, source_target_pairs={{0,4},{4,0},{1,5},{5,1},{2,6},{6,2},{3,7},{7,3},{8,12},{12,8},{9,1... | collective-permute-start | bytes 3538952 | tf_op jit(solution)/shard_map/ppermute | solution.py:30
  80.0 39.2 %all-to-all-start = ((bf16[16,40,1664]{2,1,0:T(8,128)(2,1)}), bf16[16,40,1664]{2,1,0:T(8,128)(2,1)}, u32[]{:S(2)}, u32[]{:S(2)}) async-start(bf16[16,40,1664]{2,1,0:T(8,128)(2,1)} %bitcast.43), calls=%async_computation | async-start | bytes 4259840 | tf_op jit(solution)/shard_map/all_to_all | solution.py:34
  90.0 22.8 %collective-permute-start.7 = (bf16[768,768]{1,0:T(8,128)(2,1)}, bf16[768,768]{1,0:T(8,128)(2,1)}, u32[]{:S(2)}, u32[]{:S(2)}) collective-permute-start(bf16[768,768]{1,0:T(8,128)(2,1)} %collective-permute-done.3.refs_5_.refs_1_), channel_id=1, source_target_pairs={{0,2},{2,0},{1,3},{3,1},{4,6},{6,4},{5,7},{7,5},{8,10},{10,8},{9,1... | collective-permute-start | bytes 3538952 | tf_op jit(solution)/shard_map/ppermute | solution.py:30
  92.4 20.4 %collective-permute-start.6 = (bf16[768,768]{1,0:T(8,128)(2,1)}, bf16[768,768]{1,0:T(8,128)(2,1)}, u32[]{:S(2)}, u32[]{:S(2)}) collective-permute-start(bf16[768,768]{1,0:T(8,128)(2,1)} %pad_maximum_fusion.2.refs_4_.refs_0_), channel_id=1, source_target_pairs={{0,2},{2,0},{1,3},{3,1},{4,6},{6,4},{5,7},{7,5},{8,10},{10,8},{9,1... | collective-permute-start | bytes 3538952 | tf_op jit(solution)/shard_map/ppermute | solution.py:30
  92.5 20.4 %collective-permute-start.8 = (bf16[768,768]{1,0:T(8,128)(2,1)}, bf16[768,768]{1,0:T(8,128)(2,1)}, u32[]{:S(2)}, u32[]{:S(2)}) collective-permute-start(bf16[768,768]{1,0:T(8,128)(2,1)} %collective-permute-done.5.refs_6_.refs_2_), channel_id=1, source_target_pairs={{0,2},{2,0},{1,3},{3,1},{4,6},{6,4},{5,7},{7,5},{8,10},{10,8},{9,1... | collective-permute-start | bytes 3538952 | tf_op jit(solution)/shard_map/ppermute | solution.py:30
  92.9 19.9 %collective-permute-start.10 = (bf16[768,768]{1,0:T(8,128)(2,1)}, bf16[768,768]{1,0:T(8,128)(2,1)}, u32[]{:S(2)}, u32[]{:S(2)}) collective-permute-start(bf16[768,768]{1,0:T(8,128)(2,1)} %collective-permute-done.9.refs_7_.refs_3_), channel_id=1, source_target_pairs={{0,2},{2,0},{1,3},{3,1},{4,6},{6,4},{5,7},{7,5},{8,10},{10,8},{9,1... | collective-permute-start | bytes 3538952 | tf_op jit(solution)/shard_map/ppermute | solution.py:30
  119.2 43.0 %collective-permute-start.11 = (bf16[384,3072]{1,0:T(8,128)(2,1)}, bf16[384,3072]{1,0:T(8,128)(2,1)}, u32[]{:S(2)}, u32[]{:S(2)}) collective-permute-start(bf16[384,3072]{1,0:T(8,128)(2,1)} %get-tuple-element.224), channel_id=1, source_target_pairs={{0,2},{2,0},{1,3},{3,1},{4,6},{6,4},{5,7},{7,5},{8,10},{10,8},{9,1... | collective-permute-start | bytes 7077896 | tf_op jit(solution)/shard_map/ppermute | solution.py:30
  143.8 25.8 %all-to-all-start.1 = ((bf16[16,40,896]{2,1,0:T(8,128)(2,1)}), bf16[16,40,896]{2,1,0:T(8,128)(2,1)}, u32[]{:S(2)}, u32[]{:S(2)}) async-start(bf16[16,40,896]{2,1,0:T(8,128)(2,1)} %bitcast.45), calls=%async_computation.1 | async-start | bytes 2293760 | tf_op jit(solution)/shard_map/all_to_all | solution.py:34
  149.9 50.8 %reduce-scatter.3.cloned.1.call-start = ((), (), s32[]{:S(2)}) async-start(), calls=%async_computation.7 | async-start | bytes 2949120 | tf_op jit(solution)/shard_map/reduce_scatter | solution.py:898
  169.6 16.6 %collective-permute-start.13 = (bf16[4,768,768]{2,1,0:T(8,128)(2,1)}, bf16[4,768,768]{2,1,0:T(8,128)(2,1)}, u32[]{:S(2)}, u32[]{:S(2)}) collective-permute-start(bf16[4,768,768]{2,1,0:T(8,128)(2,1)} %get-tuple-element.235), channel_id=1, source_target_pairs={{0,2},{2,0},{1,3},{3,1},{4,6},{6,4},{5,7},{7,5},{8,10},{10,8},{9,1... | collective-permute-start | bytes 14155784 | tf_op jit(solution)/shard_map/ppermute | solution.py:30
  170.6 69.7 %reduce-scatter.5.cloned.1.call-start = ((), (), s32[]{:S(2)}) async-start(), calls=%async_computation.8 | async-start | bytes 737280 | tf_op jit(solution)/shard_map/reduce_scatter | solution.py:899
  174.3 19.6 %collective-permute-start.12 = (bf16[512,768]{1,0:T(8,128)(2,1)S(1)}, bf16[512,768]{1,0:T(8,128)(2,1)S(1)}, u32[]{:S(2)}, u32[]{:S(2)}) collective-permute-start(bf16[512,768]{1,0:T(8,128)(2,1)S(1)} %get-tuple-element.228.mine_ref), channel_id=1, source_target_pairs={{0,1},{1,0},{2,3},{3,2},{4,5},{5,4},{6,7},{7,6},{8,9},{9,8},{10,11... | collective-permute-start | bytes 2359304 | tf_op jit(solution)/shard_map/ppermute | solution.py:30
  194.7 45.6 %collective-permute-start.14 = (bf16[2,384,768]{2,1,0:T(8,128)(2,1)S(1)}, bf16[2,384,768]{2,1,0:T(8,128)(2,1)}, u32[]{:S(2)}, u32[]{:S(2)}) collective-permute-start(bf16[2,384,768]{2,1,0:T(8,128)(2,1)S(1)} %get-tuple-element.255), channel_id=1, source_target_pairs={{0,4},{4,0},{1,5},{5,1},{2,6},{6,2},{3,7},{7,3},{8,12},{12,8},{9,1... | collective-permute-start | bytes 3538952 | tf_op jit(solution)/shard_map/ppermute | solution.py:30
  200.7 39.7 %collective-permute-start.15 = (bf16[2,384,768]{2,1,0:T(8,128)(2,1)}, bf16[2,384,768]{2,1,0:T(8,128)(2,1)}, u32[]{:S(2)}, u32[]{:S(2)}) collective-permute-start(bf16[2,384,768]{2,1,0:T(8,128)(2,1)} %get-tuple-element.256), channel_id=1, source_target_pairs={{0,1},{1,0},{2,3},{3,2},{4,5},{5,4},{6,7},{7,6},{8,9},{9,8},{10,11... | collective-permute-start | bytes 3538952 | tf_op jit(solution)/shard_map/ppermute | solution.py:30
  202.0 38.3 %all-to-all-start.2 = ((bf16[16,40,768]{2,1,0:T(8,128)(2,1)}), bf16[16,40,768]{2,1,0:T(8,128)(2,1)}, u32[]{:S(2)}, u32[]{:S(2)}) async-start(bf16[16,40,768]{2,1,0:T(8,128)(2,1)} %bitcast.22), calls=%async_computation.2 | async-start | bytes 1966080 | tf_op jit(solution)/shard_map/all_to_all | solution.py:34
  209.4 106.6 %all-gather.2.cloned.1.call-start = ((), (), s32[]{:S(2)}) async-start(), calls=%async_computation.9 | async-start | bytes 2506752 | tf_op jit(solution)/shard_map/all_gather | solution.py:925
  240.4 14.5 %collective-permute-start.27 = (bf16[24,3072]{1,0:T(8,128)(2,1)}, bf16[24,3072]{1,0:T(8,128)(2,1)S(1)}, u32[]{:S(2)}, u32[]{:S(2)}) collective-permute-start(bf16[24,3072]{1,0:T(8,128)(2,1)} %reduce-scatter.5.cloned.1.call-done), channel_id=1, source_target_pairs={{0,64},{64,0},{1,65},{65,1},{2,66},{66,2},{3,67},{67,3},{4,68},{68... | collective-permute-start | bytes 442376 | tf_op jit(solution)/shard_map/ppermute | solution.py:30
  265.1 28.7 %all-to-all-start.3 = ((bf16[16,24,1664]{2,1,0:T(8,128)(2,1)}), bf16[16,24,1664]{2,1,0:T(8,128)(2,1)}, u32[]{:S(2)}, u32[]{:S(2)}) async-start(bf16[16,24,1664]{2,1,0:T(8,128)(2,1)} %pad_maximum_fusion), calls=%async_computation.5 | async-start | bytes 2555904 | tf_op jit(solution)/shard_map/all_to_all | solution.py:34
  278.9 15.0 %collective-permute-start.20 = (bf16[384,768]{1,0:T(8,128)(2,1)S(1)}, bf16[384,768]{1,0:T(8,128)(2,1)S(1)}, u32[]{:S(2)}, u32[]{:S(2)}) collective-permute-start(bf16[384,768]{1,0:T(8,128)(2,1)S(1)} %copy-done.27), channel_id=1, source_target_pairs={{0,1},{1,0},{2,3},{3,2},{4,5},{5,4},{6,7},{7,6},{8,9},{9,8},{10,11... | collective-permute-start | bytes 1769480 | tf_op jit(solution)/shard_map/ppermute | solution.py:30
  279.0 18.0 %collective-permute-start.23 = (bf16[512,768]{1,0:T(8,128)(2,1)}, bf16[512,768]{1,0:T(8,128)(2,1)}, u32[]{:S(2)}, u32[]{:S(2)}) collective-permute-start(bf16[512,768]{1,0:T(8,128)(2,1)} %get-tuple-element.286), channel_id=1, source_target_pairs={{0,2},{2,0},{1,3},{3,1},{4,6},{6,4},{5,7},{7,5},{8,10},{10,8},{9,1... | collective-permute-start | bytes 2359304 | tf_op jit(solution)/shard_map/ppermute | solution.py:30
  282.5 28.2 %collective-permute-start.22 = (bf16[512,768]{1,0:T(8,128)(2,1)}, bf16[512,768]{1,0:T(8,128)(2,1)}, u32[]{:S(2)}, u32[]{:S(2)}) collective-permute-start(bf16[512,768]{1,0:T(8,128)(2,1)} %add_convert_fusion.4), channel_id=1, source_target_pairs={{0,1},{1,0},{2,3},{3,2},{4,5},{5,4},{6,7},{7,6},{8,9},{9,8},{10,11... | collective-permute-start | bytes 2359304 | tf_op jit(solution)/shard_map/ppermute | solution.py:30
  284.9 29.7 %collective-permute-start.25 = (bf16[512,768]{1,0:T(8,128)(2,1)}, bf16[512,768]{1,0:T(8,128)(2,1)}, u32[]{:S(2)}, u32[]{:S(2)}) collective-permute-start(bf16[512,768]{1,0:T(8,128)(2,1)} %add_convert_fusion.3), channel_id=1, source_target_pairs={{0,4},{4,0},{1,5},{5,1},{2,6},{6,2},{3,7},{7,3},{8,12},{12,8},{9,1... | collective-permute-start | bytes 2359304 | tf_op jit(solution)/shard_map/ppermute | solution.py:30
  295.6 17.1 %collective-permute-start.21 = (bf16[24,1664]{1,0:T(8,128)(2,1)S(1)}, bf16[24,1664]{1,0:T(8,128)(2,1)S(1)}, u32[]{:S(2)}, u32[]{:S(2)}) collective-permute-start(bf16[24,1664]{1,0:T(8,128)(2,1)S(1)} %reduce_sum.12), channel_id=1, source_target_pairs={{0,64},{64,0},{1,65},{65,1},{2,66},{66,2},{3,67},{67,3},{4,68},{68... | collective-permute-start | bytes 239624 | tf_op jit(solution)/shard_map/ppermute | solution.py:30
  316.0 12.5 %collective-permute-start.28 = (bf16[384,3072]{1,0:T(8,128)(2,1)}, bf16[384,3072]{1,0:T(8,128)(2,1)}, u32[]{:S(2)}, u32[]{:S(2)}) collective-permute-start(bf16[384,3072]{1,0:T(8,128)(2,1)} %all-gather.2.cloned.1.call-done.mine_ref), channel_id=1, source_target_pairs={{0,2},{2,0},{1,3},{3,1},{4,6},{6,4},{5,7},{7,5},{8,10},{10,8},{9,1... | collective-permute-start | bytes 7077896 | tf_op jit(solution)/shard_map/ppermute | solution.py:30
  318.0 27.0 %all-to-all-start.4 = ((bf16[16,24,1664]{2,1,0:T(8,128)(2,1)}), bf16[16,24,1664]{2,1,0:T(8,128)(2,1)S(1)}, u32[]{:S(2)}, u32[]{:S(2)}) async-start(bf16[16,24,1664]{2,1,0:T(8,128)(2,1)} %broadcast_in_dim.48), calls=%async_computation.6 | async-start | bytes 2555904 | tf_op jit(solution)/shard_map/all_to_all | solution.py:34
  324.9 19.2 %collective-permute-start.26 = (bf16[512,768]{1,0:T(8,128)(2,1)S(1)}, bf16[512,768]{1,0:T(8,128)(2,1)}, u32[]{:S(2)}, u32[]{:S(2)}) collective-permute-start(bf16[512,768]{1,0:T(8,128)(2,1)S(1)} %add_convert_fusion.2.mine_ref), channel_id=1, source_target_pairs={{0,1},{1,0},{2,3},{3,2},{4,5},{5,4},{6,7},{7,6},{8,9},{9,8},{10,11... | collective-permute-start | bytes 2359304 | tf_op jit(solution)/shard_map/ppermute | solution.py:30
  346.5 15.3 %collective-permute-start.30 = (bf16[384,768]{1,0:T(8,128)(2,1)}, bf16[384,768]{1,0:T(8,128)(2,1)}, u32[]{:S(2)}, u32[]{:S(2)}) collective-permute-start(bf16[384,768]{1,0:T(8,128)(2,1)} %copy-done.23), channel_id=1, source_target_pairs={{0,4},{4,0},{1,5},{5,1},{2,6},{6,2},{3,7},{7,3},{8,12},{12,8},{9,1... | collective-permute-start | bytes 1769480 | tf_op jit(solution)/shard_map/ppermute | solution.py:30
  (53 other events, 384.8 us)
Sparse Core Ops, SparseCore 0:
  170.7 29.8 reduce-scatter.2
  203.0 29.1 reduce-scatter.4
  255.8 58.2 all-gather.1

commit v2 on v1

--- a/solution.py
+++ b/solution.py
@@ -67,7 +67,7 @@
     )
 
 
-RATE = 230000000
+RATE = 57500000
 TIMES = dict(
     route=4,
     project=5,

time: 379 us -> 374 us (0.987)
    unnamed x96 -> x102, local copies, waits for them, and re-layouts: 14.6 us -> 14.1 us
  transfers between devices with their start and end apart: 39 -> 39, of which waited for: 15 -> 14; matrix products, arithmetic and copies ran while one was open for 6% -> 5% of each run, Pallas kernels for 47% -> 48%
where the time goes in v2:
time: 374 us; the launch traced here: 368 us
  Pallas kernels  180 us (48%)
  waiting for transfers between devices  72.1 us (19%)
  starting transfers between devices  68.8 us (18%)
  local copies, waits for them, and re-layouts  16.6 us (4%)
  between operations  14.5 us (4%)
  other arithmetic  13.7 us (4%)
    pallas_call x21, Pallas kernels, call(): pl.pallas_call(kernel, **{} if grid is None else {'grid': grid}, in_specs...  162 us
    ppermute x30, waiting for transfers between devices, swap(): return lax.ppermute(x, axis, [(0, 1), (1, 0)])  50.1 us
    all_to_all x5, starting transfers between devices, exchange(): return lax.all_to_all(x, axis, split_axis=0, concat_axis=0, tiled=True)  36.1 us
    ppermute x30, starting transfers between devices, swap(): return lax.ppermute(x, axis, [(0, 1), (1, 0)])  31.5 us
    pallas_call x2, Pallas kernels, half_call(): pl.pallas_call(kernel, grid_spec=pltpu.PrefetchScalarGridSpec(num_scalar_...  18.6 us
    all_to_all x5, waiting for transfers between devices, exchange(): return lax.all_to_all(x, axis, split_axis=0, concat_axis=0, tiled=True)  14.9 us
    unnamed x102, local copies, waits for them, and re-layouts  14.1 us
  transfers between devices with their start and end apart: 39, of which 14 were waited for; matrix products, arithmetic and copies ran while one was open for 5% of the time, Pallas kernels for 48%

profile of v2, /device:TPU:1, one launch (start us, length us, event | category | flops | bytes accessed | tf_op | source)
XLA Modules:
  0.0 367.9 jit_solution(15045166029317526763)
XLA Ops:
  15.7 3.7 %route.1 = (bf16[512,640]{1,0:T(8,128)(2,1)S(1)}, bf16[640,512]{1,0:T(8,128)(2,1)S(1)}, bf16[640,896]{1,0:T(8,128)(2,1)}) custom-call(s32[1]{0:T(128)} %bitcast.10.tensor_ref, s32[512,2]{1,0:T(8,128)S(1)} %copy.41.routes_ref, bf16[512,768]{1,0:T(8,128)(2,1)} %cot_ref.7, bf16[128,640]{1,0:T(8,128)(2,1)S(1)} %copy-done.28, f32[1,640]{1,0:T(1,128)S(1)} %copy-done.29), custom_call_target="tpu_custom_call" | custom-call | flops 230000000 | bytes 1048576 | tf_op jit(solution)/shard_map/route/pallas_call | solution.py:115
  20.6 6.6 %project.2 = (bf16[1024,768]{1,0:T(8,128)(2,1)}, bf16[1024,384]{1,0:T(8,128)(2,1)}, bf16[1024,384]{1,0:T(8,128)(2,1)}, bf16[512,384]{1,0:T(8,128)(2,1)S(1)}) custom-call(bf16[512,768]{1,0:T(8,128)(2,1)} %x_ref.3, bf16[512,768]{1,0:T(8,128)(2,1)} %collective-permute-done.x1_ref, f32[1,768]{1,0:T(1,128)S(1)} %broadcast_in_dim.23.gain_ref.scale_ref, ...), custom_call_target="tpu_custom_call" | custom-call | flops 287500000 | bytes 1048576 | tf_op jit(solution)/shard_map/project/pallas_call | solution.py:115
  31.3 5.1 %project.3 = (bf16[1024,768]{1,0:T(8,128)(2,1)}, bf16[1024,384]{1,0:T(8,128)(2,1)}, bf16[1024,384]{1,0:T(8,128)(2,1)}) custom-call(bf16[512,768]{1,0:T(8,128)(2,1)} %collective-permute-done.1.x0_ref, bf16[512,768]{1,0:T(8,128)(2,1)} %copy-done.40, f32[1,768]{1,0:T(1,128)S(1)} %broadcast_in_dim.23.gain_ref.scale_ref, bf16[768,384]{1,0:T(8,128)(2,1)S(1)} %copy-done.1, ...), custom_call_target="tpu_custom_call" | custom-call | flops 287500000 | bytes 1048576 | tf_op jit(solution)/shard_map/project/pallas_call | solution.py:115
  36.4 14.0 %attend.1 = (bf16[512,384]{1,0:T(8,128)(2,1)S(1)}, f32[512,384]{1,0:T(8,128)}, bf16[512,768]{1,0:T(8,128)(2,1)}) custom-call(f32[4]{0:T(128)S(1)} %add_select_fusion.hide_ref, bf16[512,384]{1,0:T(8,128)(2,1)S(1)} %copy-done.15, bf16[1024,384]{1,0:T(8,128)(2,1)} %get-tuple-element.173.ka_ref, bf16[1024,384]{1,0:T(8,128)(2,1)} %get-tuple-element.174.va_ref, ...), custom_call_target="tpu_custom_call" | custom-call | flops 805000000 | bytes 1048576 | tf_op jit(solution)/shard_map/attend/pallas_call | solution.py:115
  53.6 4.1 %turn_rows.1 = (bf16[768,1024]{1,0:T(8,128)(2,1)S(1)}, bf16[768,1024]{1,0:T(8,128)(2,1)}) custom-call(bf16[1024,768]{1,0:T(8,128)(2,1)} %get-tuple-element.182.a_ref, bf16[1024,768]{1,0:T(8,128)(2,1)} %get-tuple-element.183.b_ref), custom_call_target="tpu_custom_call" | custom-call | flops 172500000 | bytes 1048576 | tf_op jit(solution)/shard_map/turn_rows/pallas_call | solution.py:115
  58.8 11.3 %collective-permute-done.4.theirs_ref = bf16[512,768]{1,0:T(8,128)(2,1)S(1)} collective-permute-done((bf16[512,768]{1,0:T(8,128)(2,1)}, bf16[512,768]{1,0:T(8,128)(2,1)S(1)}, u32[]{:S(2)}, u32[]{:S(2)}) %collective-permute-start.4) | collective-permute-done | bytes 786464 | tf_op jit(solution)/shard_map/ppermute | solution.py:30
  71.1 4.8 %second.1 = (f32[512,768]{1,0:T(8,128)}, bf16[512,768]{1,0:T(8,128)(2,1)S(1)}, bf16[640,1664]{1,0:T(8,128)(2,1)}) custom-call(bf16[512,768]{1,0:T(8,128)(2,1)} %x_ref.3, bf16[512,768]{1,0:T(8,128)(2,1)} %get-tuple-element.180.mine_ref, bf16[512,768]{1,0:T(8,128)(2,1)} %copy-done.39, f32[1,768]{1,0:T(1,128)S(1)} %broadcast_in_dim.46.gain_ref, ...), custom_call_target="tpu_custom_call" | custom-call | flops 230000000 | bytes 1048576 | tf_op jit(solution)/shard_map/second/pallas_call | solution.py:115
  75.8 9.8 %all-to-all-start = ((bf16[16,40,1664]{2,1,0:T(8,128)(2,1)}), bf16[16,40,1664]{2,1,0:T(8,128)(2,1)}, u32[]{:S(2)}, u32[]{:S(2)}) async-start(bf16[16,40,1664]{2,1,0:T(8,128)(2,1)} %bitcast.44), calls=%async_computation | async-start | bytes 4259840 | tf_op jit(solution)/shard_map/all_to_all | solution.py:34
  88.1 11.2 %shared.1 = (bf16[512,1024]{1,0:T(8,128)(2,1)}, bf16[512,1024]{1,0:T(8,128)(2,1)}, bf16[512,1024]{1,0:T(8,128)(2,1)}, f32[512,768]{1,0:T(8,128)}, f32[512,768]{1,0:T(8,128)}, /*index=5*/f32[512,128]{1,0:T(8,128)S(1)}) custom-call(bf16[512,768]{1,0:T(8,128)(2,1)S(1)} %get-tuple-element.189.n_ref.n2_ref, bf16[512,768]{1,0:T(8,128)(2,1)} %cot_ref.7, ...), custom_call_target="tpu_custom_call" | custom-call | flops 690000000 | bytes 1048576 | tf_op jit(solution)/shard_map/shared/pallas_call | solution.py:115
  99.3 8.2 %shared_weights.1 = (bf16[384,3072]{1,0:T(8,128)(2,1)}, bf16[384,3072]{1,0:T(8,128)(2,1)}) custom-call(s32[1]{0:T(128)} %bitcast.core_ref, bf16[512,768]{1,0:T(8,128)(2,1)S(1)} %get-tuple-element.189.n_ref.n2_ref, bf16[512,768]{1,0:T(8,128)(2,1)S(1)} %copy-done, bf16[512,1024]{1,0:T(8,128)(2,1)} %get-tuple-element.193.gg_ref, ...), custom_call_target="tpu_custom_call" | custom-call | flops 345000000 | bytes 1048576 | tf_op jit(solution)/shard_map/shared_weights/pallas_call | solution.py:418
  107.5 8.5 %all-to-all-done = bf16[16,40,1664]{2,1,0:T(8,128)(2,1)} async-done(((bf16[16,40,1664]{2,1,0:T(8,128)(2,1)}), bf16[16,40,1664]{2,1,0:T(8,128)(2,1)}, u32[]{:S(2)}, u32[]{:S(2)}) %all-to-all-start) | async-done | bytes 2129952 | tf_op jit(solution)/shard_map/all_to_all | solution.py:34
  118.2 20.7 %expert_rows.1 = (bf16[8,640,256]{2,1,0:T(8,128)(2,1)}, bf16[8,640,512]{2,1,0:T(8,128)(2,1)}, bf16[640,896]{1,0:T(8,128)(2,1)}, bf16[640,768]{1,0:T(8,128)(2,1)S...) custom-call(s32[1]{0:T(128)} %bitcast.17.here_ref, bf16[640,1664]{1,0:T(8,128)(2,1)} %bitcast.19.sent_ref, ...), custom_call_target="tpu_custom_call" | custom-call | flops 1150000000 | bytes 1048576 | tf_op jit(solution)/shard_map/expert_rows/pallas_call | solution.py:115
  139.8 6.0 %all-to-all-start.1 = ((bf16[16,40,896]{2,1,0:T(8,128)(2,1)}), bf16[16,40,896]{2,1,0:T(8,128)(2,1)S(1)}, u32[]{:S(2)}, u32[]{:S(2)}) async-start(bf16[16,40,896]{2,1,0:T(8,128)(2,1)} %bitcast.46), calls=%async_computation.1 | async-start | bytes 2293760 | tf_op jit(solution)/shard_map/all_to_all | solution.py:34
  145.8 10.3 %expert_given.1 = (bf16[4,768,768]{2,1,0:T(8,128)(2,1)}, f32[640,768]{1,0:T(8,128)}, bf16[768,640]{1,0:T(8,128)(2,1)S(1)}, bf16[768,640]{1,0:T(8,128)(2,1)S(1)}) custom-call(bf16[640,768]{1,0:T(8,128)(2,1)} %copy-done.20, bf16[640,768]{1,0:T(8,128)(2,1)} %get-tuple-element.215.out_ref, bf16[8,640,256]{2,1,0:T(8,128)(2,1)} %get-tuple-element.216.hidden_ref, ...), custom_call_target="tpu_custom_call" | custom-call | flops 517500000 | bytes 1048576 | tf_op jit(solution)/shard_map/expert_given/pallas_call | solution.py:115
  158.1 4.0 %half_sum.1 = bf16[384,3072]{1,0:T(8,128)(2,1)} custom-call(bf16[384,3072]{1,0:T(8,128)(2,1)} %get-tuple-element.223.kept_ref, bf16[384,3072]{1,0:T(8,128)(2,1)} %collective-permute-done.11.taken_ref), custom_call_target="tpu_custom_call" | custom-call | flops 230000000 | bytes 1048576 | tf_op jit(solution)/shard_map/half_sum/pallas_call | solution.py:115
  166.5 3.6 combine.1
  171.2 11.2 %expert_kept.1 = (bf16[4,768,768]{2,1,0:T(8,128)(2,1)}, bf16[640,768]{1,0:T(8,128)(2,1)}) custom-call(bf16[768,640]{1,0:T(8,128)(2,1)} %copy-done.18, bf16[768,640]{1,0:T(8,128)(2,1)} %copy-done.19, f32[640,128]{1,0:T(8,128)S(1)} %get-tuple-element.232.share_ref, f32[640,768]{1,0:T(8,128)} %get-tuple-element.233.first_ref, ...), custom_call_target="tpu_custom_call" | custom-call | flops 517500000 | bytes 1048576 | tf_op jit(solution)/shard_map/expert_kept/pallas_call | solution.py:115
  182.4 6.7 %expert_sum.1 = (bf16[2,384,768]{2,1,0:T(8,128)(2,1)}, bf16[2,384,768]{2,1,0:T(8,128)(2,1)}, bf16[2,384,768]{2,1,0:T(8,128)(2,1)}, bf16[2,384,768]{2,1,0:T(8,128)(2,1)}) custom-call(bf16[4,768,768]{2,1,0:T(8,128)(2,1)} %get-tuple-element.234.kept_ref, bf16[4,768,768]{2,1,0:T(8,128)(2,1)} %collective-permute-done.13.taken_ref), custom_call_target="tpu_custom_call" | custom-call | flops 230000000 | bytes 1048576 | tf_op jit(solution)/shard_map/expert_sum/pallas_call | solution.py:115
  190.3 5.5 %reduce-scatter.3.cloned.1.call-done = bf16[96,3072]{1,0:T(8,128)(2,1)} async-done(((bf16[384,3072]{1,0:T(8,128)(2,1)}), bf16[96,3072]{1,0:T(8,128)(2,1)}) %reduce-scatter.3.cloned.1.call-update) | async-done | bytes 589840 | tf_op jit(solution)/shard_map/reduce_scatter | solution.py:898
  197.1 7.3 %all-to-all-start.2 = ((bf16[16,40,768]{2,1,0:T(8,128)(2,1)}), bf16[16,40,768]{2,1,0:T(8,128)(2,1)}, u32[]{:S(2)}, u32[]{:S(2)}) async-start(bf16[16,40,768]{2,1,0:T(8,128)(2,1)} %bitcast.22), calls=%async_computation.2 | async-start | bytes 1966080 | tf_op jit(solution)/shard_map/all_to_all | solution.py:34
  204.6 4.4 %back_two.1 = (f32[512,768]{1,0:T(8,128)}, bf16[512,768]{1,0:T(8,128)(2,1)S(1)}, bf16[512,384]{1,0:T(8,128)(2,1)S(1)}, f32[1,768]{1,0:T(1,128)S(1)}) custom-call(f32[512,768]{1,0:T(8,128)} %get-tuple-element.190.middle_ref, bf16[512,768]{1,0:T(8,128)(2,1)} %copy-done.21, bf16[512,768]{1,0:T(8,128)(2,1)} %copy-done.38, bf16[512,768]{1,0:T(8,128)(2,1)} %cot_ref.7, ...), custom_call_target="tpu_custom_call" | custom-call | flops 230000000 | bytes 1048576 | tf_op jit(solution)/shard_map/back_two/pallas_call | solution.py:115
  209.8 23.4 %attend_back.1 = (bf16[512,384]{1,0:T(8,128)(2,1)S(1)}, bf16[1024,384]{1,0:T(8,128)(2,1)}, bf16[1024,384]{1,0:T(8,128)(2,1)}, bf16[1024,384]{1,0:T(8,128)(2,1)}, bf16[1024,384]{1,0:T(8,128)(2,1)}) custom-call(f32[4]{0:T(128)S(1)} %add_select_fusion.hide_ref, bf16[512,384]{1,0:T(8,128)(2,1)S(1)} %copy-done.16, bf16[1024,384]{1,0:T(8,128)(2,1)} %get-tuple-element.173.ka_ref, ...), custom_call_target="tpu_custom_call" | custom-call | flops 1322499968 | bytes 1048576 | tf_op jit(solution)/shard_map/attend_back/pallas_call | solution.py:115
  236.6 10.4 %late_weights.1 = (bf16[384,1536]{1,0:T(8,128)(2,1)}, bf16[384,1536]{1,0:T(8,128)(2,1)}, bf16[384,128]{1,0:T(8,128)(2,1)S(1)}, bf16[384,128]{1,0:T(8,128)(2,1)S(1)}) custom-call(s32[1]{0:T(128)} %bitcast.core_ref, bf16[512,768]{1,0:T(8,128)(2,1)} %copy-done.4, bf16[512,768]{1,0:T(8,128)(2,1)} %copy-done.22, f32[1,768]{1,0:T(1,128)S(1)} %get-tuple-element.243.gain_ref, ...), custom_call_target="tpu_custom_call" | custom-call | flops 460000000 | bytes 1048576 | tf_op jit(solution)/shard_map/late_weights/pallas_call | solution.py:418
  259.8 6.0 %all-to-all-start.3 = ((bf16[16,24,1664]{2,1,0:T(8,128)(2,1)}), bf16[16,24,1664]{2,1,0:T(8,128)(2,1)}, u32[]{:S(2)}, u32[]{:S(2)}) async-start(bf16[16,24,1664]{2,1,0:T(8,128)(2,1)} %pad_maximum_fusion), calls=%async_computation.5 | async-start | bytes 2555904 | tf_op jit(solution)/shard_map/all_to_all | solution.py:34
  265.7 7.6 %normed_back.1 = (bf16[512,768]{1,0:T(8,128)(2,1)}, bf16[512,768]{1,0:T(8,128)(2,1)}, f32[512,768]{1,0:T(8,128)}, f32[512,768]{1,0:T(8,128)}) custom-call(bf16[512,384]{1,0:T(8,128)(2,1)S(1)} %get-tuple-element.284.dq_ref, bf16[1024,384]{1,0:T(8,128)(2,1)} %get-tuple-element.259.dka_ref, bf16[1024,384]{1,0:T(8,128)(2,1)} %get-tuple-element.261.dva_ref, ...), custom_call_target="tpu_custom_call" | custom-call | flops 460000000 | bytes 1048576 | tf_op jit(solution)/shard_map/normed_back/pallas_call | solution.py:115
  280.8 8.0 %collective-permute-done.20.fu_ref = bf16[384,768]{1,0:T(8,128)(2,1)S(1)} collective-permute-done((bf16[384,768]{1,0:T(8,128)(2,1)S(1)}, bf16[384,768]{1,0:T(8,128)(2,1)S(1)}, u32[]{:S(2)}, u32[]{:S(2)}) %collective-permute-start.20) | collective-permute-done | bytes 589856 | tf_op jit(solution)/shard_map/ppermute | solution.py:30
  294.3 11.5 %collective-permute-done.22 = bf16[512,768]{1,0:T(8,128)(2,1)} collective-permute-done((bf16[512,768]{1,0:T(8,128)(2,1)S(1)}, bf16[512,768]{1,0:T(8,128)(2,1)}, u32[]{:S(2)}, u32[]{:S(2)}) %collective-permute-start.22) | collective-permute-done | bytes 786464 | tf_op jit(solution)/shard_map/ppermute | solution.py:30
  311.6 7.1 %all-to-all-start.4 = ((bf16[16,24,1664]{2,1,0:T(8,128)(2,1)}), bf16[16,24,1664]{2,1,0:T(8,128)(2,1)S(1)}, u32[]{:S(2)}, u32[]{:S(2)}) async-start(bf16[16,24,1664]{2,1,0:T(8,128)(2,1)} %broadcast_in_dim.48), calls=%async_computation.6 | async-start | bytes 2555904 | tf_op jit(solution)/shard_map/all_to_all | solution.py:34
  322.1 6.8 %early_out.1 = (f32[768,1024]{1,0:T(8,128)}, f32[768,1024]{1,0:T(8,128)}, f32[1024,768]{1,0:T(8,128)}) custom-call(s32[1]{0:T(128)} %bitcast.core_ref, bf16[384,3072]{1,0:T(8,128)(2,1)} %all-gather.2.cloned.1.call-done.mine_ref, bf16[384,3072]{1,0:T(8,128)(2,1)} %collective-permute-done.28.theirs_ref), custom_call_target="tpu_custom_call" | custom-call | flops 287500000 | bytes 1048576 | tf_op jit(solution)/shard_map/early_out/pallas_call | solution.py:115
  328.9 8.9 %collective-permute-done.26.theirs_ref = bf16[512,768]{1,0:T(8,128)(2,1)} collective-permute-done((bf16[512,768]{1,0:T(8,128)(2,1)S(1)}, bf16[512,768]{1,0:T(8,128)(2,1)}, u32[]{:S(2)}, u32[]{:S(2)}) %collective-permute-start.26) | collective-permute-done | bytes 786464 | tf_op jit(solution)/shard_map/ppermute | solution.py:30
  345.1 3.8 %late_out.1 = (f32[768,384]{1,0:T(8,128)}, f32[768,384]{1,0:T(8,128)}, f32[768,384]{1,0:T(8,128)}, f32[384,768]{1,0:T(8,128)}, f32[768,128]{1,0:T(8,128)S(1)}) custom-call(s32[1]{0:T(128)} %bitcast.core_ref, bf16[384,1664]{1,0:T(8,128)(2,1)S(1)} %bitcast.32, bf16[384,1664]{1,0:T(8,128)(2,1)} %copy-done.36), custom_call_target="tpu_custom_call" | custom-call | flops 230000000 | bytes 1048576 | tf_op jit(solution)/shard_map/late_out/pallas_call | solution.py:115
  348.9 6.6 %collective-permute-done.30.fl_ref = bf16[384,768]{1,0:T(8,128)(2,1)} collective-permute-done((bf16[384,768]{1,0:T(8,128)(2,1)}, bf16[384,768]{1,0:T(8,128)(2,1)}, u32[]{:S(2)}, u32[]{:S(2)}) %collective-permute-start.30) | collective-permute-done | bytes 589856 | tf_op jit(solution)/shard_map/ppermute | solution.py:30
  (197 shorter events, 86.4 us)
Async XLA Ops:
  7.2 20.7 %collective-permute-start.1 = (bf16[512,768]{1,0:T(8,128)(2,1)}, bf16[512,768]{1,0:T(8,128)(2,1)}, u32[]{:S(2)}, u32[]{:S(2)}) collective-permute-start(bf16[512,768]{1,0:T(8,128)(2,1)} %x_ref.3), channel_id=1, source_target_pairs={{0,4},{4,0},{1,5},{5,1},{2,6},{6,2},{3,7},{7,3},{8,12},{12,8},{9,1... | collective-permute-start | bytes 2359304 | tf_op jit(solution)/shard_map/ppermute | solution.py:30
  9.4 11.1 %collective-permute-start = (bf16[512,768]{1,0:T(8,128)(2,1)}, bf16[512,768]{1,0:T(8,128)(2,1)}, u32[]{:S(2)}, u32[]{:S(2)}) collective-permute-start(bf16[512,768]{1,0:T(8,128)(2,1)} %x_ref.3), channel_id=1, source_target_pairs={{0,2},{2,0},{1,3},{3,1},{4,6},{6,4},{5,7},{7,5},{8,10},{10,8},{9,1... | collective-permute-start | bytes 2359304 | tf_op jit(solution)/shard_map/ppermute | solution.py:30
  13.9 36.5 %collective-permute-start.3 = (bf16[768,768]{1,0:T(8,128)(2,1)}, bf16[768,768]{1,0:T(8,128)(2,1)}, u32[]{:S(2)}, u32[]{:S(2)}) collective-permute-start(bf16[768,768]{1,0:T(8,128)(2,1)} %pad_maximum_fusion.2.refs_4_.refs_0_), channel_id=1, source_target_pairs={{0,1},{1,0},{2,3},{3,2},{4,5},{5,4},{6,7},{7,6},{8,9},{9,8},{10,11... | collective-permute-start | bytes 3538952 | tf_op jit(solution)/shard_map/ppermute | solution.py:30
  28.2 30.6 %collective-permute-start.5 = (bf16[768,768]{1,0:T(8,128)(2,1)}, bf16[768,768]{1,0:T(8,128)(2,1)}, u32[]{:S(2)}, u32[]{:S(2)}) collective-permute-start(bf16[768,768]{1,0:T(8,128)(2,1)} %pad_maximum_fusion.2.refs_4_.refs_0_), channel_id=1, source_target_pairs={{0,4},{4,0},{1,5},{5,1},{2,6},{6,2},{3,7},{7,3},{8,12},{12,8},{9,1... | collective-permute-start | bytes 3538952 | tf_op jit(solution)/shard_map/ppermute | solution.py:30
  50.4 19.8 %collective-permute-start.4 = (bf16[512,768]{1,0:T(8,128)(2,1)}, bf16[512,768]{1,0:T(8,128)(2,1)S(1)}, u32[]{:S(2)}, u32[]{:S(2)}) collective-permute-start(bf16[512,768]{1,0:T(8,128)(2,1)} %get-tuple-element.180.mine_ref), channel_id=1, source_target_pairs={{0,1},{1,0},{2,3},{3,2},{4,5},{5,4},{6,7},{7,6},{8,9},{9,8},{10,11... | collective-permute-start | bytes 2359304 | tf_op jit(solution)/shard_map/ppermute | solution.py:30
  52.3 35.3 %collective-permute-start.9 = (bf16[768,768]{1,0:T(8,128)(2,1)}, bf16[768,768]{1,0:T(8,128)(2,1)}, u32[]{:S(2)}, u32[]{:S(2)}) collective-permute-start(bf16[768,768]{1,0:T(8,128)(2,1)} %collective-permute-done.3.refs_5_.refs_1_), channel_id=1, source_target_pairs={{0,4},{4,0},{1,5},{5,1},{2,6},{6,2},{3,7},{7,3},{8,12},{12,8},{9,1... | collective-permute-start | bytes 3538952 | tf_op jit(solution)/shard_map/ppermute | solution.py:30
  75.8 40.2 %all-to-all-start = ((bf16[16,40,1664]{2,1,0:T(8,128)(2,1)}), bf16[16,40,1664]{2,1,0:T(8,128)(2,1)}, u32[]{:S(2)}, u32[]{:S(2)}) async-start(bf16[16,40,1664]{2,1,0:T(8,128)(2,1)} %bitcast.44), calls=%async_computation | async-start | bytes 4259840 | tf_op jit(solution)/shard_map/all_to_all | solution.py:34
  85.6 21.9 %collective-permute-start.7 = (bf16[768,768]{1,0:T(8,128)(2,1)}, bf16[768,768]{1,0:T(8,128)(2,1)}, u32[]{:S(2)}, u32[]{:S(2)}) collective-permute-start(bf16[768,768]{1,0:T(8,128)(2,1)} %collective-permute-done.3.refs_5_.refs_1_), channel_id=1, source_target_pairs={{0,2},{2,0},{1,3},{3,1},{4,6},{6,4},{5,7},{7,5},{8,10},{10,8},{9,1... | collective-permute-start | bytes 3538952 | tf_op jit(solution)/shard_map/ppermute | solution.py:30
  87.1 20.4 %collective-permute-start.6 = (bf16[768,768]{1,0:T(8,128)(2,1)}, bf16[768,768]{1,0:T(8,128)(2,1)}, u32[]{:S(2)}, u32[]{:S(2)}) collective-permute-start(bf16[768,768]{1,0:T(8,128)(2,1)} %pad_maximum_fusion.2.refs_4_.refs_0_), channel_id=1, source_target_pairs={{0,2},{2,0},{1,3},{3,1},{4,6},{6,4},{5,7},{7,5},{8,10},{10,8},{9,1... | collective-permute-start | bytes 3538952 | tf_op jit(solution)/shard_map/ppermute | solution.py:30
  87.2 20.3 %collective-permute-start.8 = (bf16[768,768]{1,0:T(8,128)(2,1)}, bf16[768,768]{1,0:T(8,128)(2,1)}, u32[]{:S(2)}, u32[]{:S(2)}) collective-permute-start(bf16[768,768]{1,0:T(8,128)(2,1)} %collective-permute-done.5.refs_6_.refs_2_), channel_id=1, source_target_pairs={{0,2},{2,0},{1,3},{3,1},{4,6},{6,4},{5,7},{7,5},{8,10},{10,8},{9,1... | collective-permute-start | bytes 3538952 | tf_op jit(solution)/shard_map/ppermute | solution.py:30
  87.6 19.9 %collective-permute-start.10 = (bf16[768,768]{1,0:T(8,128)(2,1)}, bf16[768,768]{1,0:T(8,128)(2,1)}, u32[]{:S(2)}, u32[]{:S(2)}) collective-permute-start(bf16[768,768]{1,0:T(8,128)(2,1)} %collective-permute-done.9.refs_7_.refs_3_), channel_id=1, source_target_pairs={{0,2},{2,0},{1,3},{3,1},{4,6},{6,4},{5,7},{7,5},{8,10},{10,8},{9,1... | collective-permute-start | bytes 3538952 | tf_op jit(solution)/shard_map/ppermute | solution.py:30
  116.0 42.0 %collective-permute-start.11 = (bf16[384,3072]{1,0:T(8,128)(2,1)}, bf16[384,3072]{1,0:T(8,128)(2,1)}, u32[]{:S(2)}, u32[]{:S(2)}) collective-permute-start(bf16[384,3072]{1,0:T(8,128)(2,1)} %get-tuple-element.224), channel_id=1, source_target_pairs={{0,2},{2,0},{1,3},{3,1},{4,6},{6,4},{5,7},{7,5},{8,10},{10,8},{9,1... | collective-permute-start | bytes 7077896 | tf_op jit(solution)/shard_map/ppermute | solution.py:30
  139.8 25.6 %all-to-all-start.1 = ((bf16[16,40,896]{2,1,0:T(8,128)(2,1)}), bf16[16,40,896]{2,1,0:T(8,128)(2,1)S(1)}, u32[]{:S(2)}, u32[]{:S(2)}) async-start(bf16[16,40,896]{2,1,0:T(8,128)(2,1)} %bitcast.46), calls=%async_computation.1 | async-start | bytes 2293760 | tf_op jit(solution)/shard_map/all_to_all | solution.py:34
  145.8 50.0 %reduce-scatter.3.cloned.1.call-start = ((), (), s32[]{:S(2)}) async-start(), calls=%async_computation.7 | async-start | bytes 2949120 | tf_op jit(solution)/shard_map/reduce_scatter | solution.py:898
  165.4 17.0 %collective-permute-start.13 = (bf16[4,768,768]{2,1,0:T(8,128)(2,1)}, bf16[4,768,768]{2,1,0:T(8,128)(2,1)}, u32[]{:S(2)}, u32[]{:S(2)}) collective-permute-start(bf16[4,768,768]{2,1,0:T(8,128)(2,1)} %get-tuple-element.235), channel_id=1, source_target_pairs={{0,2},{2,0},{1,3},{3,1},{4,6},{6,4},{5,7},{7,5},{8,10},{10,8},{9,1... | collective-permute-start | bytes 14155784 | tf_op jit(solution)/shard_map/ppermute | solution.py:30
  166.5 69.5 %reduce-scatter.5.cloned.1.call-start = ((), (), s32[]{:S(2)}) async-start(), calls=%async_computation.8 | async-start | bytes 737280 | tf_op jit(solution)/shard_map/reduce_scatter | solution.py:899
  170.1 18.9 %collective-permute-start.12 = (bf16[512,768]{1,0:T(8,128)(2,1)S(1)}, bf16[512,768]{1,0:T(8,128)(2,1)S(1)}, u32[]{:S(2)}, u32[]{:S(2)}) collective-permute-start(bf16[512,768]{1,0:T(8,128)(2,1)S(1)} %get-tuple-element.228.mine_ref), channel_id=1, source_target_pairs={{0,1},{1,0},{2,3},{3,2},{4,5},{5,4},{6,7},{7,6},{8,9},{9,8},{10,11... | collective-permute-start | bytes 2359304 | tf_op jit(solution)/shard_map/ppermute | solution.py:30
  189.9 46.0 %collective-permute-start.14 = (bf16[2,384,768]{2,1,0:T(8,128)(2,1)}, bf16[2,384,768]{2,1,0:T(8,128)(2,1)}, u32[]{:S(2)}, u32[]{:S(2)}) collective-permute-start(bf16[2,384,768]{2,1,0:T(8,128)(2,1)} %get-tuple-element.255), channel_id=1, source_target_pairs={{0,4},{4,0},{1,5},{5,1},{2,6},{6,2},{3,7},{7,3},{8,12},{12,8},{9,1... | collective-permute-start | bytes 3538952 | tf_op jit(solution)/shard_map/ppermute | solution.py:30
  195.8 40.1 %collective-permute-start.15 = (bf16[2,384,768]{2,1,0:T(8,128)(2,1)}, bf16[2,384,768]{2,1,0:T(8,128)(2,1)}, u32[]{:S(2)}, u32[]{:S(2)}) collective-permute-start(bf16[2,384,768]{2,1,0:T(8,128)(2,1)} %get-tuple-element.256), channel_id=1, source_target_pairs={{0,1},{1,0},{2,3},{3,2},{4,5},{5,4},{6,7},{7,6},{8,9},{9,8},{10,11... | collective-permute-start | bytes 3538952 | tf_op jit(solution)/shard_map/ppermute | solution.py:30
  197.1 38.8 %all-to-all-start.2 = ((bf16[16,40,768]{2,1,0:T(8,128)(2,1)}), bf16[16,40,768]{2,1,0:T(8,128)(2,1)}, u32[]{:S(2)}, u32[]{:S(2)}) async-start(bf16[16,40,768]{2,1,0:T(8,128)(2,1)} %bitcast.22), calls=%async_computation.2 | async-start | bytes 1966080 | tf_op jit(solution)/shard_map/all_to_all | solution.py:34
  204.5 105.3 %all-gather.2.cloned.1.call-start = ((), (), s32[]{:S(2)}) async-start(), calls=%async_computation.9 | async-start | bytes 2506752 | tf_op jit(solution)/shard_map/all_gather | solution.py:925
  235.9 13.6 %collective-permute-start.27 = (bf16[24,3072]{1,0:T(8,128)(2,1)}, bf16[24,3072]{1,0:T(8,128)(2,1)S(1)}, u32[]{:S(2)}, u32[]{:S(2)}) collective-permute-start(bf16[24,3072]{1,0:T(8,128)(2,1)} %reduce-scatter.5.cloned.1.call-done), channel_id=1, source_target_pairs={{0,64},{64,0},{1,65},{65,1},{2,66},{66,2},{3,67},{67,3},{4,68},{68... | collective-permute-start | bytes 442376 | tf_op jit(solution)/shard_map/ppermute | solution.py:30
  259.8 29.9 %all-to-all-start.3 = ((bf16[16,24,1664]{2,1,0:T(8,128)(2,1)}), bf16[16,24,1664]{2,1,0:T(8,128)(2,1)}, u32[]{:S(2)}, u32[]{:S(2)}) async-start(bf16[16,24,1664]{2,1,0:T(8,128)(2,1)} %pad_maximum_fusion), calls=%async_computation.5 | async-start | bytes 2555904 | tf_op jit(solution)/shard_map/all_to_all | solution.py:34
  273.9 14.9 %collective-permute-start.20 = (bf16[384,768]{1,0:T(8,128)(2,1)S(1)}, bf16[384,768]{1,0:T(8,128)(2,1)S(1)}, u32[]{:S(2)}, u32[]{:S(2)}) collective-permute-start(bf16[384,768]{1,0:T(8,128)(2,1)S(1)} %copy-done.32), channel_id=1, source_target_pairs={{0,1},{1,0},{2,3},{3,2},{4,5},{5,4},{6,7},{7,6},{8,9},{9,8},{10,11... | collective-permute-start | bytes 1769480 | tf_op jit(solution)/shard_map/ppermute | solution.py:30
  274.0 18.5 %collective-permute-start.23 = (bf16[512,768]{1,0:T(8,128)(2,1)}, bf16[512,768]{1,0:T(8,128)(2,1)}, u32[]{:S(2)}, u32[]{:S(2)}) collective-permute-start(bf16[512,768]{1,0:T(8,128)(2,1)} %get-tuple-element.286), channel_id=1, source_target_pairs={{0,2},{2,0},{1,3},{3,1},{4,6},{6,4},{5,7},{7,5},{8,10},{10,8},{9,1... | collective-permute-start | bytes 2359304 | tf_op jit(solution)/shard_map/ppermute | solution.py:30
  276.7 29.1 %collective-permute-start.22 = (bf16[512,768]{1,0:T(8,128)(2,1)S(1)}, bf16[512,768]{1,0:T(8,128)(2,1)}, u32[]{:S(2)}, u32[]{:S(2)}) collective-permute-start(bf16[512,768]{1,0:T(8,128)(2,1)S(1)} %add_convert_fusion.4), channel_id=1, source_target_pairs={{0,1},{1,0},{2,3},{3,2},{4,5},{5,4},{6,7},{7,6},{8,9},{9,8},{10,11... | collective-permute-start | bytes 2359304 | tf_op jit(solution)/shard_map/ppermute | solution.py:30
  279.2 30.3 %collective-permute-start.25 = (bf16[512,768]{1,0:T(8,128)(2,1)}, bf16[512,768]{1,0:T(8,128)(2,1)S(1)}, u32[]{:S(2)}, u32[]{:S(2)}) collective-permute-start(bf16[512,768]{1,0:T(8,128)(2,1)} %add_convert_fusion.3), channel_id=1, source_target_pairs={{0,4},{4,0},{1,5},{5,1},{2,6},{6,2},{3,7},{7,3},{8,12},{12,8},{9,1... | collective-permute-start | bytes 2359304 | tf_op jit(solution)/shard_map/ppermute | solution.py:30
  291.2 16.6 %collective-permute-start.21 = (bf16[24,1664]{1,0:T(8,128)(2,1)S(1)}, bf16[24,1664]{1,0:T(8,128)(2,1)S(1)}, u32[]{:S(2)}, u32[]{:S(2)}) collective-permute-start(bf16[24,1664]{1,0:T(8,128)(2,1)S(1)} %reduce_sum.12), channel_id=1, source_target_pairs={{0,64},{64,0},{1,65},{65,1},{2,66},{66,2},{3,67},{67,3},{4,68},{68... | collective-permute-start | bytes 239624 | tf_op jit(solution)/shard_map/ppermute | solution.py:30
  309.8 12.3 %collective-permute-start.28 = (bf16[384,3072]{1,0:T(8,128)(2,1)}, bf16[384,3072]{1,0:T(8,128)(2,1)}, u32[]{:S(2)}, u32[]{:S(2)}) collective-permute-start(bf16[384,3072]{1,0:T(8,128)(2,1)} %all-gather.2.cloned.1.call-done.mine_ref), channel_id=1, source_target_pairs={{0,2},{2,0},{1,3},{3,1},{4,6},{6,4},{5,7},{7,5},{8,10},{10,8},{9,1... | collective-permute-start | bytes 7077896 | tf_op jit(solution)/shard_map/ppermute | solution.py:30
  311.6 26.5 %all-to-all-start.4 = ((bf16[16,24,1664]{2,1,0:T(8,128)(2,1)}), bf16[16,24,1664]{2,1,0:T(8,128)(2,1)S(1)}, u32[]{:S(2)}, u32[]{:S(2)}) async-start(bf16[16,24,1664]{2,1,0:T(8,128)(2,1)} %broadcast_in_dim.48), calls=%async_computation.6 | async-start | bytes 2555904 | tf_op jit(solution)/shard_map/all_to_all | solution.py:34
  318.7 19.0 %collective-permute-start.26 = (bf16[512,768]{1,0:T(8,128)(2,1)S(1)}, bf16[512,768]{1,0:T(8,128)(2,1)}, u32[]{:S(2)}, u32[]{:S(2)}) collective-permute-start(bf16[512,768]{1,0:T(8,128)(2,1)S(1)} %add_convert_fusion.2.mine_ref), channel_id=1, source_target_pairs={{0,1},{1,0},{2,3},{3,2},{4,5},{5,4},{6,7},{7,6},{8,9},{9,8},{10,11... | collective-permute-start | bytes 2359304 | tf_op jit(solution)/shard_map/ppermute | solution.py:30
  340.2 15.3 %collective-permute-start.30 = (bf16[384,768]{1,0:T(8,128)(2,1)}, bf16[384,768]{1,0:T(8,128)(2,1)}, u32[]{:S(2)}, u32[]{:S(2)}) collective-permute-start(bf16[384,768]{1,0:T(8,128)(2,1)} %copy-done.30), channel_id=1, source_target_pairs={{0,4},{4,0},{1,5},{5,1},{2,6},{6,2},{3,7},{7,3},{8,12},{12,8},{9,1... | collective-permute-start | bytes 1769480 | tf_op jit(solution)/shard_map/ppermute | solution.py:30
  (56 other events, 386.2 us)
Sparse Core Ops, SparseCore 0:
  166.6 29.1 reduce-scatter.2
  198.2 29.1 reduce-scatter.4
  250.4 58.7 all-gather.1

commit v3 on v2

--- a/solution.py
+++ b/solution.py
@@ -621,7 +621,7 @@
 
 def expert_sum_kernel(kept_ref, taken_ref, high_ref, tensor_ref, keep_high_ref, keep_tensor_ref):
     shard = pl.program_id(0)
-    half = kept_ref.shape[1] // 2
+    half = high_ref.shape[1]
     total = kept_ref[0] + taken_ref[0]
     for ref, at, here in (
         (keep_high_ref, 0, shard < 2),
@@ -631,7 +631,7 @@
     ):
         @pl.when(here)
         def _(ref=ref, at=at):
-            ref[0] = total[at : at + half]
+            ref[0] = total[at : at + ref.shape[1]]
 
 
 def expert_sums_kernel(kh_ref, fh_ref, kt_ref, ft_ref, to_t_ref, to_y_ref, kept_u_ref, kept_l_ref):
@@ -646,9 +646,10 @@
     part = gate_ref.shape[2]
     for at, (kept_ref, from_ref) in ((0, (ku_ref, fu_ref)), (half, (kl_ref, fl_ref))):
         total = kept_ref[...].astype(f32) + from_ref[...].astype(f32)
-        gate_ref[0, at : at + half, :] = total[:, :part]
-        up_ref[0, at : at + half, :] = total[:, part : 2 * part]
-        down_ref[0, :, at : at + half] = total[:, 2 * part :].T
+        rows = slice(at, at + kept_ref.shape[0])
+        gate_ref[0, rows, :] = total[:, :part]
+        up_ref[0, rows, :] = total[:, part : 2 * part]
+        down_ref[0, :, rows] = total[:, 2 * part :].T
 
 
 def combine_kernel(placer_ref, back_ref, share_ref, router_ref, shared_ref, part_ref, lg_ref, *, experts):
@@ -864,19 +865,19 @@
         [((seats, width), bf16)],
     )
     of_shard = pl.BlockSpec((1, width, 3 * part), lambda k: (k, 0, 0))
-    half_shard = (1, width // 2, 3 * part)
+    upper, lower = (2 * width // 3, 3 * part), (width // 3, 3 * part)
     to_high, to_tensor, keep_high, keep_tensor = call(
         expert_sum_kernel,
         "expert_sum",
         (kept, swap(given, "c")),
-        [((2, width // 2, 3 * part), bf16)] * 4,
+        [((2, *upper), bf16), ((2, *lower), bf16)] * 2,
         grid=(4,),
         in_specs={0: of_shard, 1: of_shard},
         out_specs={
-            0: pl.BlockSpec(half_shard, lambda k: (jnp.maximum(k - 2, 0), 0, 0)),
-            1: pl.BlockSpec(half_shard, lambda k: (k // 2, 0, 0)),
-            2: pl.BlockSpec(half_shard, lambda k: (jnp.minimum(k, 1), 0, 0)),
-            3: pl.BlockSpec(half_shard, lambda k: (k // 2, 0, 0)),
+            0: pl.BlockSpec((1, *upper), lambda k: (jnp.maximum(k - 2, 0), 0, 0)),
+            1: pl.BlockSpec((1, *lower), lambda k: (k // 2, 0, 0)),
+            2: pl.BlockSpec((1, *upper), lambda k: (jnp.minimum(k, 1), 0, 0)),
+            3: pl.BlockSpec((1, *lower), lambda k: (k // 2, 0, 0)),
         },
     )
     theirs, to_high, to_tensor, keep_high, keep_tensor, picked = lax.optimization_barrier(
@@ -919,7 +920,7 @@
         expert_sums_kernel,
         "expert_sums",
         (keep_high, after(from_high, late_given), keep_tensor, from_tensor),
-        [((width // 2, 3 * part), bf16)] * 4,
+        [(upper, bf16), (lower, bf16)] * 2,
     )
     early = early.astype(f32) + after(early_zh, late_given).astype(f32)
     early = lax.all_gather(early.astype(bf16), PLANE, axis=0, tiled=True)

time: 374 us -> 381 us (1.019)
  waiting for transfers between devices: 72.1 us -> 79.2 us
    all_to_all x5, waiting for transfers between devices: 14.9 us -> 23.5 us  [exchange(): return lax.all_to_all(x, axis, split_axis=0, concat_axis=0, tiled=True)]
    unnamed x102 -> x104, local copies, waits for them, and re-layouts: 14.1 us -> 15.2 us
  transfers between devices with their start and end apart: 39 -> 39, of which waited for: 14 -> 13; matrix products, arithmetic and copies ran while one was open for 5% -> 5% of each run, Pallas kernels for 48% -> 47%
where the time goes in v3:
time: 381 us; the launch traced here: 374 us
  Pallas kernels  180 us (47%)
  waiting for transfers between devices  79.2 us (21%)
  starting transfers between devices  67.2 us (18%)
  local copies, waits for them, and re-layouts  17.6 us (5%)
  between operations  14.4 us (4%)
  other arithmetic  13.7 us (4%)
    pallas_call x21, Pallas kernels, call(): pl.pallas_call(kernel, **{} if grid is None else {'grid': grid}, in_specs...  161 us
    ppermute x30, waiting for transfers between devices, swap(): return lax.ppermute(x, axis, [(0, 1), (1, 0)])  49.2 us
    all_to_all x5, starting transfers between devices, exchange(): return lax.all_to_all(x, axis, split_axis=0, concat_axis=0, tiled=True)  35 us
    ppermute x30, starting transfers between devices, swap(): return lax.ppermute(x, axis, [(0, 1), (1, 0)])  30.9 us
    all_to_all x5, waiting for transfers between devices, exchange(): return lax.all_to_all(x, axis, split_axis=0, concat_axis=0, tiled=True)  23.5 us
    pallas_call x2, Pallas kernels, half_call(): pl.pallas_call(kernel, grid_spec=pltpu.PrefetchScalarGridSpec(num_scalar_...  18.6 us
    unnamed x104, local copies, waits for them, and re-layouts  15.2 us
  transfers between devices with their start and end apart: 39, of which 13 were waited for; matrix products, arithmetic and copies ran while one was open for 5% of the time, Pallas kernels for 47%

profile of v3, /device:TPU:1, one launch (start us, length us, event | category | flops | bytes accessed | tf_op | source)
XLA Modules:
  0.0 374.3 jit_solution(10084035778579769721)
XLA Ops:
  15.7 3.7 route.1
  20.6 6.6 %project.2 = (bf16[1024,768]{1,0:T(8,128)(2,1)}, bf16[1024,384]{1,0:T(8,128)(2,1)}, bf16[1024,384]{1,0:T(8,128)(2,1)}, bf16[512,384]{1,0:T(8,128)(2,1)S(1)}) custom-call(bf16[512,768]{1,0:T(8,128)(2,1)} %x_ref.3, bf16[512,768]{1,0:T(8,128)(2,1)} %collective-permute-done.x1_ref, f32[1,768]{1,0:T(1,128)S(1)} %broadcast_in_dim.23.gain_ref.scale_ref, ...), custom_call_target="tpu_custom_call" | custom-call | flops 287500000 | bytes 1048576 | tf_op jit(solution)/shard_map/project/pallas_call | solution.py:115
  31.3 5.1 %project.3 = (bf16[1024,768]{1,0:T(8,128)(2,1)}, bf16[1024,384]{1,0:T(8,128)(2,1)}, bf16[1024,384]{1,0:T(8,128)(2,1)}) custom-call(bf16[512,768]{1,0:T(8,128)(2,1)} %collective-permute-done.1.x0_ref, bf16[512,768]{1,0:T(8,128)(2,1)} %copy-done.41, f32[1,768]{1,0:T(1,128)S(1)} %broadcast_in_dim.23.gain_ref.scale_ref, bf16[768,384]{1,0:T(8,128)(2,1)S(1)} %copy-done.1, ...), custom_call_target="tpu_custom_call" | custom-call | flops 287500000 | bytes 1048576 | tf_op jit(solution)/shard_map/project/pallas_call | solution.py:115
  36.4 14.0 %attend.1 = (bf16[512,384]{1,0:T(8,128)(2,1)S(1)}, f32[512,384]{1,0:T(8,128)}, bf16[512,768]{1,0:T(8,128)(2,1)}) custom-call(f32[4]{0:T(128)S(1)} %add_select_fusion.hide_ref, bf16[512,384]{1,0:T(8,128)(2,1)S(1)} %copy-done.15, bf16[1024,384]{1,0:T(8,128)(2,1)} %get-tuple-element.173.ka_ref, bf16[1024,384]{1,0:T(8,128)(2,1)} %get-tuple-element.174.va_ref, ...), custom_call_target="tpu_custom_call" | custom-call | flops 805000000 | bytes 1048576 | tf_op jit(solution)/shard_map/attend/pallas_call | solution.py:115
  53.6 4.1 %turn_rows.1 = (bf16[768,1024]{1,0:T(8,128)(2,1)S(1)}, bf16[768,1024]{1,0:T(8,128)(2,1)}) custom-call(bf16[1024,768]{1,0:T(8,128)(2,1)} %get-tuple-element.182.a_ref, bf16[1024,768]{1,0:T(8,128)(2,1)} %get-tuple-element.183.b_ref), custom_call_target="tpu_custom_call" | custom-call | flops 172500000 | bytes 1048576 | tf_op jit(solution)/shard_map/turn_rows/pallas_call | solution.py:115
  58.9 11.3 %collective-permute-done.4.theirs_ref = bf16[512,768]{1,0:T(8,128)(2,1)S(1)} collective-permute-done((bf16[512,768]{1,0:T(8,128)(2,1)}, bf16[512,768]{1,0:T(8,128)(2,1)S(1)}, u32[]{:S(2)}, u32[]{:S(2)}) %collective-permute-start.4) | collective-permute-done | bytes 786464 | tf_op jit(solution)/shard_map/ppermute | solution.py:30
  71.0 4.8 %second.1 = (f32[512,768]{1,0:T(8,128)}, bf16[512,768]{1,0:T(8,128)(2,1)S(1)}, bf16[640,1664]{1,0:T(8,128)(2,1)}) custom-call(bf16[512,768]{1,0:T(8,128)(2,1)} %x_ref.3, bf16[512,768]{1,0:T(8,128)(2,1)} %get-tuple-element.180.mine_ref, bf16[512,768]{1,0:T(8,128)(2,1)} %copy-done.40, f32[1,768]{1,0:T(1,128)S(1)} %broadcast_in_dim.46.gain_ref, ...), custom_call_target="tpu_custom_call" | custom-call | flops 230000000 | bytes 1048576 | tf_op jit(solution)/shard_map/second/pallas_call | solution.py:115
  75.8 9.8 %all-to-all-start = ((bf16[16,40,1664]{2,1,0:T(8,128)(2,1)}), bf16[16,40,1664]{2,1,0:T(8,128)(2,1)}, u32[]{:S(2)}, u32[]{:S(2)}) async-start(bf16[16,40,1664]{2,1,0:T(8,128)(2,1)} %bitcast.44), calls=%async_computation | async-start | bytes 4259840 | tf_op jit(solution)/shard_map/all_to_all | solution.py:34
  88.1 11.2 %shared.1 = (bf16[512,1024]{1,0:T(8,128)(2,1)}, bf16[512,1024]{1,0:T(8,128)(2,1)}, bf16[512,1024]{1,0:T(8,128)(2,1)}, f32[512,768]{1,0:T(8,128)}, f32[512,768]{1,0:T(8,128)}, /*index=5*/f32[512,128]{1,0:T(8,128)S(1)}) custom-call(bf16[512,768]{1,0:T(8,128)(2,1)S(1)} %get-tuple-element.189.n_ref.n2_ref, bf16[512,768]{1,0:T(8,128)(2,1)} %cot_ref.7, ...), custom_call_target="tpu_custom_call" | custom-call | flops 690000000 | bytes 1048576 | tf_op jit(solution)/shard_map/shared/pallas_call | solution.py:115
  99.3 8.2 %shared_weights.1 = (bf16[384,3072]{1,0:T(8,128)(2,1)}, bf16[384,3072]{1,0:T(8,128)(2,1)}) custom-call(s32[1]{0:T(128)} %bitcast.core_ref, bf16[512,768]{1,0:T(8,128)(2,1)S(1)} %get-tuple-element.189.n_ref.n2_ref, bf16[512,768]{1,0:T(8,128)(2,1)S(1)} %copy-done, bf16[512,1024]{1,0:T(8,128)(2,1)} %get-tuple-element.193.gg_ref, ...), custom_call_target="tpu_custom_call" | custom-call | flops 345000000 | bytes 1048576 | tf_op jit(solution)/shard_map/shared_weights/pallas_call | solution.py:418
  107.5 8.5 %all-to-all-done = bf16[16,40,1664]{2,1,0:T(8,128)(2,1)} async-done(((bf16[16,40,1664]{2,1,0:T(8,128)(2,1)}), bf16[16,40,1664]{2,1,0:T(8,128)(2,1)}, u32[]{:S(2)}, u32[]{:S(2)}) %all-to-all-start) | async-done | bytes 2129952 | tf_op jit(solution)/shard_map/all_to_all | solution.py:34
  118.2 20.7 %expert_rows.1 = (bf16[8,640,256]{2,1,0:T(8,128)(2,1)}, bf16[8,640,512]{2,1,0:T(8,128)(2,1)}, bf16[640,896]{1,0:T(8,128)(2,1)}, bf16[640,768]{1,0:T(8,128)(2,1)S...) custom-call(s32[1]{0:T(128)} %bitcast.17.here_ref, bf16[640,1664]{1,0:T(8,128)(2,1)} %bitcast.19.sent_ref, ...), custom_call_target="tpu_custom_call" | custom-call | flops 1150000000 | bytes 1048576 | tf_op jit(solution)/shard_map/expert_rows/pallas_call | solution.py:115
  139.8 6.0 %all-to-all-start.1 = ((bf16[16,40,896]{2,1,0:T(8,128)(2,1)}), bf16[16,40,896]{2,1,0:T(8,128)(2,1)S(1)}, u32[]{:S(2)}, u32[]{:S(2)}) async-start(bf16[16,40,896]{2,1,0:T(8,128)(2,1)} %bitcast.46), calls=%async_computation.1 | async-start | bytes 2293760 | tf_op jit(solution)/shard_map/all_to_all | solution.py:34
  145.8 10.3 %expert_given.1 = (bf16[4,768,768]{2,1,0:T(8,128)(2,1)}, f32[640,768]{1,0:T(8,128)}, bf16[768,640]{1,0:T(8,128)(2,1)S(1)}, bf16[768,640]{1,0:T(8,128)(2,1)S(1)}) custom-call(bf16[640,768]{1,0:T(8,128)(2,1)} %copy-done.20, bf16[640,768]{1,0:T(8,128)(2,1)} %get-tuple-element.215.out_ref, bf16[8,640,256]{2,1,0:T(8,128)(2,1)} %get-tuple-element.216.hidden_ref, ...), custom_call_target="tpu_custom_call" | custom-call | flops 517500000 | bytes 1048576 | tf_op jit(solution)/shard_map/expert_given/pallas_call | solution.py:115
  158.1 4.0 %half_sum.1 = bf16[384,3072]{1,0:T(8,128)(2,1)} custom-call(bf16[384,3072]{1,0:T(8,128)(2,1)} %get-tuple-element.223.kept_ref, bf16[384,3072]{1,0:T(8,128)(2,1)} %collective-permute-done.11.taken_ref), custom_call_target="tpu_custom_call" | custom-call | flops 230000000 | bytes 1048576 | tf_op jit(solution)/shard_map/half_sum/pallas_call | solution.py:115
  166.5 3.6 combine.1
  171.2 11.2 %expert_kept.1 = (bf16[4,768,768]{2,1,0:T(8,128)(2,1)}, bf16[640,768]{1,0:T(8,128)(2,1)}) custom-call(bf16[768,640]{1,0:T(8,128)(2,1)} %copy-done.18, bf16[768,640]{1,0:T(8,128)(2,1)} %copy-done.19, f32[640,128]{1,0:T(8,128)S(1)} %get-tuple-element.232.share_ref, f32[640,768]{1,0:T(8,128)} %get-tuple-element.233.first_ref, ...), custom_call_target="tpu_custom_call" | custom-call | flops 517500000 | bytes 1048576 | tf_op jit(solution)/shard_map/expert_kept/pallas_call | solution.py:115
  182.4 6.3 %expert_sum.1 = (bf16[2,512,768]{2,1,0:T(8,128)(2,1)}, bf16[2,256,768]{2,1,0:T(8,128)(2,1)}, bf16[2,512,768]{2,1,0:T(8,128)(2,1)}, bf16[2,256,768]{2,1,0:T(8,128)(2,1)S(1)}) custom-call(bf16[4,768,768]{2,1,0:T(8,128)(2,1)} %get-tuple-element.234.kept_ref, bf16[4,768,768]{2,1,0:T(8,128)(2,1)} %collective-permute-done.13.taken_ref), custom_call_target="tpu_custom_call" | custom-call | flops 230000000 | bytes 1048576 | tf_op jit(solution)/shard_map/expert_sum/pallas_call | solution.py:115
  190.8 5.0 %reduce-scatter.3.cloned.1.call-done = bf16[96,3072]{1,0:T(8,128)(2,1)} async-done(((bf16[384,3072]{1,0:T(8,128)(2,1)}), bf16[96,3072]{1,0:T(8,128)(2,1)}) %reduce-scatter.3.cloned.1.call-update) | async-done | bytes 589840 | tf_op jit(solution)/shard_map/reduce_scatter | solution.py:899
  195.8 7.6 %all-to-all-start.2 = ((bf16[16,40,768]{2,1,0:T(8,128)(2,1)}), bf16[16,40,768]{2,1,0:T(8,128)(2,1)}, u32[]{:S(2)}, u32[]{:S(2)}) async-start(bf16[16,40,768]{2,1,0:T(8,128)(2,1)} %bitcast.22), calls=%async_computation.2 | async-start | bytes 1966080 | tf_op jit(solution)/shard_map/all_to_all | solution.py:34
  204.0 4.4 %back_two.1 = (f32[512,768]{1,0:T(8,128)}, bf16[512,768]{1,0:T(8,128)(2,1)S(1)}, bf16[512,384]{1,0:T(8,128)(2,1)S(1)}, f32[1,768]{1,0:T(1,128)S(1)}) custom-call(f32[512,768]{1,0:T(8,128)} %get-tuple-element.190.middle_ref, bf16[512,768]{1,0:T(8,128)(2,1)} %copy-done.22, bf16[512,768]{1,0:T(8,128)(2,1)} %copy-done.39, bf16[512,768]{1,0:T(8,128)(2,1)} %cot_ref.7, ...), custom_call_target="tpu_custom_call" | custom-call | flops 230000000 | bytes 1048576 | tf_op jit(solution)/shard_map/back_two/pallas_call | solution.py:115
  209.2 23.4 %attend_back.1 = (bf16[512,384]{1,0:T(8,128)(2,1)S(1)}, bf16[1024,384]{1,0:T(8,128)(2,1)}, bf16[1024,384]{1,0:T(8,128)(2,1)}, bf16[1024,384]{1,0:T(8,128)(2,1)}, bf16[1024,384]{1,0:T(8,128)(2,1)}) custom-call(f32[4]{0:T(128)S(1)} %add_select_fusion.hide_ref, bf16[512,384]{1,0:T(8,128)(2,1)S(1)} %copy-done.16, bf16[1024,384]{1,0:T(8,128)(2,1)} %get-tuple-element.173.ka_ref, ...), custom_call_target="tpu_custom_call" | custom-call | flops 1322499968 | bytes 1048576 | tf_op jit(solution)/shard_map/attend_back/pallas_call | solution.py:115
  232.6 10.7 %all-to-all-done.2 = bf16[16,40,768]{2,1,0:T(8,128)(2,1)} async-done(((bf16[16,40,768]{2,1,0:T(8,128)(2,1)}), bf16[16,40,768]{2,1,0:T(8,128)(2,1)}, u32[]{:S(2)}, u32[]{:S(2)}) %all-to-all-start.2) | async-done | bytes 983072 | tf_op jit(solution)/shard_map/all_to_all | solution.py:34
  244.9 10.4 %late_weights.1 = (bf16[384,1536]{1,0:T(8,128)(2,1)}, bf16[384,1536]{1,0:T(8,128)(2,1)}, bf16[384,128]{1,0:T(8,128)(2,1)S(1)}, bf16[384,128]{1,0:T(8,128)(2,1)S(1)}) custom-call(s32[1]{0:T(128)} %bitcast.core_ref, bf16[512,768]{1,0:T(8,128)(2,1)} %copy-done.4, bf16[512,768]{1,0:T(8,128)(2,1)} %copy-done.24, f32[1,768]{1,0:T(1,128)S(1)} %get-tuple-element.243.gain_ref, ...), custom_call_target="tpu_custom_call" | custom-call | flops 460000000 | bytes 1048576 | tf_op jit(solution)/shard_map/late_weights/pallas_call | solution.py:418
  268.7 4.8 %all-to-all-start.3 = ((bf16[16,24,1664]{2,1,0:T(8,128)(2,1)}), bf16[16,24,1664]{2,1,0:T(8,128)(2,1)}, u32[]{:S(2)}, u32[]{:S(2)}) async-start(bf16[16,24,1664]{2,1,0:T(8,128)(2,1)} %pad_maximum_fusion), calls=%async_computation.5 | async-start | bytes 2555904 | tf_op jit(solution)/shard_map/all_to_all | solution.py:34
  273.5 7.7 %normed_back.1 = (bf16[512,768]{1,0:T(8,128)(2,1)}, bf16[512,768]{1,0:T(8,128)(2,1)}, f32[512,768]{1,0:T(8,128)}, f32[512,768]{1,0:T(8,128)}) custom-call(bf16[512,384]{1,0:T(8,128)(2,1)S(1)} %get-tuple-element.284.dq_ref, bf16[1024,384]{1,0:T(8,128)(2,1)} %get-tuple-element.259.dka_ref, bf16[1024,384]{1,0:T(8,128)(2,1)} %get-tuple-element.261.dva_ref, ...), custom_call_target="tpu_custom_call" | custom-call | flops 460000000 | bytes 1048576 | tf_op jit(solution)/shard_map/normed_back/pallas_call | solution.py:115
  288.9 12.0 %collective-permute-done.20.fu_ref = bf16[512,768]{1,0:T(8,128)(2,1)} collective-permute-done((bf16[512,768]{1,0:T(8,128)(2,1)S(1)}, bf16[512,768]{1,0:T(8,128)(2,1)}, u32[]{:S(2)}, u32[]{:S(2)}) %collective-permute-start.20) | collective-permute-done | bytes 786464 | tf_op jit(solution)/shard_map/ppermute | solution.py:30
  304.9 12.8 %collective-permute-done.22 = bf16[512,768]{1,0:T(8,128)(2,1)} collective-permute-done((bf16[512,768]{1,0:T(8,128)(2,1)S(1)}, bf16[512,768]{1,0:T(8,128)(2,1)}, u32[]{:S(2)}, u32[]{:S(2)}) %collective-permute-start.22) | collective-permute-done | bytes 786464 | tf_op jit(solution)/shard_map/ppermute | solution.py:30
  321.8 6.8 %all-to-all-start.4 = ((bf16[16,24,1664]{2,1,0:T(8,128)(2,1)}), bf16[16,24,1664]{2,1,0:T(8,128)(2,1)S(1)}, u32[]{:S(2)}, u32[]{:S(2)}) async-start(bf16[16,24,1664]{2,1,0:T(8,128)(2,1)} %broadcast_in_dim.48), calls=%async_computation.6 | async-start | bytes 2555904 | tf_op jit(solution)/shard_map/all_to_all | solution.py:34
  331.8 6.8 %early_out.1 = (f32[768,1024]{1,0:T(8,128)}, f32[768,1024]{1,0:T(8,128)}, f32[1024,768]{1,0:T(8,128)}) custom-call(s32[1]{0:T(128)} %bitcast.core_ref, bf16[384,3072]{1,0:T(8,128)(2,1)} %all-gather.2.cloned.1.call-done.mine_ref, bf16[384,3072]{1,0:T(8,128)(2,1)} %collective-permute-done.28.theirs_ref), custom_call_target="tpu_custom_call" | custom-call | flops 287500000 | bytes 1048576 | tf_op jit(solution)/shard_map/early_out/pallas_call | solution.py:115
  338.6 9.2 %collective-permute-done.26.theirs_ref = bf16[512,768]{1,0:T(8,128)(2,1)} collective-permute-done((bf16[512,768]{1,0:T(8,128)(2,1)S(1)}, bf16[512,768]{1,0:T(8,128)(2,1)}, u32[]{:S(2)}, u32[]{:S(2)}) %collective-permute-start.26) | collective-permute-done | bytes 786464 | tf_op jit(solution)/shard_map/ppermute | solution.py:30
  355.1 3.8 %late_out.1 = (f32[768,384]{1,0:T(8,128)}, f32[768,384]{1,0:T(8,128)}, f32[768,384]{1,0:T(8,128)}, f32[384,768]{1,0:T(8,128)}, f32[768,128]{1,0:T(8,128)S(1)}) custom-call(s32[1]{0:T(128)} %bitcast.core_ref, bf16[384,1664]{1,0:T(8,128)(2,1)S(1)} %bitcast.32, bf16[384,1664]{1,0:T(8,128)(2,1)} %copy-done.37), custom_call_target="tpu_custom_call" | custom-call | flops 230000000 | bytes 1048576 | tf_op jit(solution)/shard_map/late_out/pallas_call | solution.py:115
  (199 shorter events, 85.0 us)
Async XLA Ops:
  7.2 20.7 %collective-permute-start.1 = (bf16[512,768]{1,0:T(8,128)(2,1)}, bf16[512,768]{1,0:T(8,128)(2,1)}, u32[]{:S(2)}, u32[]{:S(2)}) collective-permute-start(bf16[512,768]{1,0:T(8,128)(2,1)} %x_ref.3), channel_id=1, source_target_pairs={{0,4},{4,0},{1,5},{5,1},{2,6},{6,2},{3,7},{7,3},{8,12},{12,8},{9,1... | collective-permute-start | bytes 2359304 | tf_op jit(solution)/shard_map/ppermute | solution.py:30
  9.4 11.1 %collective-permute-start = (bf16[512,768]{1,0:T(8,128)(2,1)}, bf16[512,768]{1,0:T(8,128)(2,1)}, u32[]{:S(2)}, u32[]{:S(2)}) collective-permute-start(bf16[512,768]{1,0:T(8,128)(2,1)} %x_ref.3), channel_id=1, source_target_pairs={{0,2},{2,0},{1,3},{3,1},{4,6},{6,4},{5,7},{7,5},{8,10},{10,8},{9,1... | collective-permute-start | bytes 2359304 | tf_op jit(solution)/shard_map/ppermute | solution.py:30
  13.9 36.5 %collective-permute-start.3 = (bf16[768,768]{1,0:T(8,128)(2,1)}, bf16[768,768]{1,0:T(8,128)(2,1)}, u32[]{:S(2)}, u32[]{:S(2)}) collective-permute-start(bf16[768,768]{1,0:T(8,128)(2,1)} %pad_maximum_fusion.2.refs_4_.refs_0_), channel_id=1, source_target_pairs={{0,1},{1,0},{2,3},{3,2},{4,5},{5,4},{6,7},{7,6},{8,9},{9,8},{10,11... | collective-permute-start | bytes 3538952 | tf_op jit(solution)/shard_map/ppermute | solution.py:30
  28.2 30.6 %collective-permute-start.5 = (bf16[768,768]{1,0:T(8,128)(2,1)}, bf16[768,768]{1,0:T(8,128)(2,1)}, u32[]{:S(2)}, u32[]{:S(2)}) collective-permute-start(bf16[768,768]{1,0:T(8,128)(2,1)} %pad_maximum_fusion.2.refs_4_.refs_0_), channel_id=1, source_target_pairs={{0,4},{4,0},{1,5},{5,1},{2,6},{6,2},{3,7},{7,3},{8,12},{12,8},{9,1... | collective-permute-start | bytes 3538952 | tf_op jit(solution)/shard_map/ppermute | solution.py:30
  50.4 19.8 %collective-permute-start.4 = (bf16[512,768]{1,0:T(8,128)(2,1)}, bf16[512,768]{1,0:T(8,128)(2,1)S(1)}, u32[]{:S(2)}, u32[]{:S(2)}) collective-permute-start(bf16[512,768]{1,0:T(8,128)(2,1)} %get-tuple-element.180.mine_ref), channel_id=1, source_target_pairs={{0,1},{1,0},{2,3},{3,2},{4,5},{5,4},{6,7},{7,6},{8,9},{9,8},{10,11... | collective-permute-start | bytes 2359304 | tf_op jit(solution)/shard_map/ppermute | solution.py:30
  52.3 35.3 %collective-permute-start.9 = (bf16[768,768]{1,0:T(8,128)(2,1)}, bf16[768,768]{1,0:T(8,128)(2,1)}, u32[]{:S(2)}, u32[]{:S(2)}) collective-permute-start(bf16[768,768]{1,0:T(8,128)(2,1)} %collective-permute-done.3.refs_5_.refs_1_), channel_id=1, source_target_pairs={{0,4},{4,0},{1,5},{5,1},{2,6},{6,2},{3,7},{7,3},{8,12},{12,8},{9,1... | collective-permute-start | bytes 3538952 | tf_op jit(solution)/shard_map/ppermute | solution.py:30
  75.8 40.2 %all-to-all-start = ((bf16[16,40,1664]{2,1,0:T(8,128)(2,1)}), bf16[16,40,1664]{2,1,0:T(8,128)(2,1)}, u32[]{:S(2)}, u32[]{:S(2)}) async-start(bf16[16,40,1664]{2,1,0:T(8,128)(2,1)} %bitcast.44), calls=%async_computation | async-start | bytes 4259840 | tf_op jit(solution)/shard_map/all_to_all | solution.py:34
  85.6 21.9 %collective-permute-start.7 = (bf16[768,768]{1,0:T(8,128)(2,1)}, bf16[768,768]{1,0:T(8,128)(2,1)}, u32[]{:S(2)}, u32[]{:S(2)}) collective-permute-start(bf16[768,768]{1,0:T(8,128)(2,1)} %collective-permute-done.3.refs_5_.refs_1_), channel_id=1, source_target_pairs={{0,2},{2,0},{1,3},{3,1},{4,6},{6,4},{5,7},{7,5},{8,10},{10,8},{9,1... | collective-permute-start | bytes 3538952 | tf_op jit(solution)/shard_map/ppermute | solution.py:30
  87.1 20.4 %collective-permute-start.6 = (bf16[768,768]{1,0:T(8,128)(2,1)}, bf16[768,768]{1,0:T(8,128)(2,1)}, u32[]{:S(2)}, u32[]{:S(2)}) collective-permute-start(bf16[768,768]{1,0:T(8,128)(2,1)} %pad_maximum_fusion.2.refs_4_.refs_0_), channel_id=1, source_target_pairs={{0,2},{2,0},{1,3},{3,1},{4,6},{6,4},{5,7},{7,5},{8,10},{10,8},{9,1... | collective-permute-start | bytes 3538952 | tf_op jit(solution)/shard_map/ppermute | solution.py:30
  87.2 20.3 %collective-permute-start.8 = (bf16[768,768]{1,0:T(8,128)(2,1)}, bf16[768,768]{1,0:T(8,128)(2,1)}, u32[]{:S(2)}, u32[]{:S(2)}) collective-permute-start(bf16[768,768]{1,0:T(8,128)(2,1)} %collective-permute-done.5.refs_6_.refs_2_), channel_id=1, source_target_pairs={{0,2},{2,0},{1,3},{3,1},{4,6},{6,4},{5,7},{7,5},{8,10},{10,8},{9,1... | collective-permute-start | bytes 3538952 | tf_op jit(solution)/shard_map/ppermute | solution.py:30
  87.6 19.9 %collective-permute-start.10 = (bf16[768,768]{1,0:T(8,128)(2,1)}, bf16[768,768]{1,0:T(8,128)(2,1)}, u32[]{:S(2)}, u32[]{:S(2)}) collective-permute-start(bf16[768,768]{1,0:T(8,128)(2,1)} %collective-permute-done.9.refs_7_.refs_3_), channel_id=1, source_target_pairs={{0,2},{2,0},{1,3},{3,1},{4,6},{6,4},{5,7},{7,5},{8,10},{10,8},{9,1... | collective-permute-start | bytes 3538952 | tf_op jit(solution)/shard_map/ppermute | solution.py:30
  116.0 42.0 %collective-permute-start.11 = (bf16[384,3072]{1,0:T(8,128)(2,1)}, bf16[384,3072]{1,0:T(8,128)(2,1)}, u32[]{:S(2)}, u32[]{:S(2)}) collective-permute-start(bf16[384,3072]{1,0:T(8,128)(2,1)} %get-tuple-element.224), channel_id=1, source_target_pairs={{0,2},{2,0},{1,3},{3,1},{4,6},{6,4},{5,7},{7,5},{8,10},{10,8},{9,1... | collective-permute-start | bytes 7077896 | tf_op jit(solution)/shard_map/ppermute | solution.py:30
  139.8 25.6 %all-to-all-start.1 = ((bf16[16,40,896]{2,1,0:T(8,128)(2,1)}), bf16[16,40,896]{2,1,0:T(8,128)(2,1)S(1)}, u32[]{:S(2)}, u32[]{:S(2)}) async-start(bf16[16,40,896]{2,1,0:T(8,128)(2,1)} %bitcast.46), calls=%async_computation.1 | async-start | bytes 2293760 | tf_op jit(solution)/shard_map/all_to_all | solution.py:34
  145.8 50.0 %reduce-scatter.3.cloned.1.call-start = ((), (), s32[]{:S(2)}) async-start(), calls=%async_computation.7 | async-start | bytes 2949120 | tf_op jit(solution)/shard_map/reduce_scatter | solution.py:899
  165.4 17.0 %collective-permute-start.13 = (bf16[4,768,768]{2,1,0:T(8,128)(2,1)}, bf16[4,768,768]{2,1,0:T(8,128)(2,1)}, u32[]{:S(2)}, u32[]{:S(2)}) collective-permute-start(bf16[4,768,768]{2,1,0:T(8,128)(2,1)} %get-tuple-element.235), channel_id=1, source_target_pairs={{0,2},{2,0},{1,3},{3,1},{4,6},{6,4},{5,7},{7,5},{8,10},{10,8},{9,1... | collective-permute-start | bytes 14155784 | tf_op jit(solution)/shard_map/ppermute | solution.py:30
  166.5 76.9 %reduce-scatter.5.cloned.1.call-start = ((), (), s32[]{:S(2)}) async-start(), calls=%async_computation.8 | async-start | bytes 737280 | tf_op jit(solution)/shard_map/reduce_scatter | solution.py:900
  170.1 19.5 %collective-permute-start.12 = (bf16[512,768]{1,0:T(8,128)(2,1)S(1)}, bf16[512,768]{1,0:T(8,128)(2,1)S(1)}, u32[]{:S(2)}, u32[]{:S(2)}) collective-permute-start(bf16[512,768]{1,0:T(8,128)(2,1)S(1)} %get-tuple-element.228.mine_ref), channel_id=1, source_target_pairs={{0,1},{1,0},{2,3},{3,2},{4,5},{5,4},{6,7},{7,6},{8,9},{9,8},{10,11... | collective-permute-start | bytes 2359304 | tf_op jit(solution)/shard_map/ppermute | solution.py:30
  190.5 52.9 %collective-permute-start.14 = (bf16[2,512,768]{2,1,0:T(8,128)(2,1)}, bf16[2,512,768]{2,1,0:T(8,128)(2,1)}, u32[]{:S(2)}, u32[]{:S(2)}) collective-permute-start(bf16[2,512,768]{2,1,0:T(8,128)(2,1)} %get-tuple-element.255), channel_id=1, source_target_pairs={{0,4},{4,0},{1,5},{5,1},{2,6},{6,2},{3,7},{7,3},{8,12},{12,8},{9,1... | collective-permute-start | bytes 4718600 | tf_op jit(solution)/shard_map/ppermute | solution.py:30
  195.8 47.6 %all-to-all-start.2 = ((bf16[16,40,768]{2,1,0:T(8,128)(2,1)}), bf16[16,40,768]{2,1,0:T(8,128)(2,1)}, u32[]{:S(2)}, u32[]{:S(2)}) async-start(bf16[16,40,768]{2,1,0:T(8,128)(2,1)} %bitcast.22), calls=%async_computation.2 | async-start | bytes 1966080 | tf_op jit(solution)/shard_map/all_to_all | solution.py:34
  203.4 116.0 %all-gather.2.cloned.1.call-start = ((), (), s32[]{:S(2)}) async-start(), calls=%async_computation.9 | async-start | bytes 2506752 | tf_op jit(solution)/shard_map/all_gather | solution.py:926
  203.5 29.2 %collective-permute-start.15 = (bf16[2,256,768]{2,1,0:T(8,128)(2,1)}, bf16[2,256,768]{2,1,0:T(8,128)(2,1)}, u32[]{:S(2)}, u32[]{:S(2)}) collective-permute-start(bf16[2,256,768]{2,1,0:T(8,128)(2,1)} %get-tuple-element.256), channel_id=1, source_target_pairs={{0,1},{1,0},{2,3},{3,2},{4,5},{5,4},{6,7},{7,6},{8,9},{9,8},{10,11... | collective-permute-start | bytes 2359304 | tf_op jit(solution)/shard_map/ppermute | solution.py:30
  243.4 15.0 %collective-permute-start.27 = (bf16[24,3072]{1,0:T(8,128)(2,1)}, bf16[24,3072]{1,0:T(8,128)(2,1)S(1)}, u32[]{:S(2)}, u32[]{:S(2)}) collective-permute-start(bf16[24,3072]{1,0:T(8,128)(2,1)} %reduce-scatter.5.cloned.1.call-done), channel_id=1, source_target_pairs={{0,64},{64,0},{1,65},{65,1},{2,66},{66,2},{3,67},{67,3},{4,68},{68... | collective-permute-start | bytes 442376 | tf_op jit(solution)/shard_map/ppermute | solution.py:30
  268.7 32.2 %all-to-all-start.3 = ((bf16[16,24,1664]{2,1,0:T(8,128)(2,1)}), bf16[16,24,1664]{2,1,0:T(8,128)(2,1)}, u32[]{:S(2)}, u32[]{:S(2)}) async-start(bf16[16,24,1664]{2,1,0:T(8,128)(2,1)} %pad_maximum_fusion), calls=%async_computation.5 | async-start | bytes 2555904 | tf_op jit(solution)/shard_map/all_to_all | solution.py:34
  281.7 19.2 %collective-permute-start.20 = (bf16[512,768]{1,0:T(8,128)(2,1)S(1)}, bf16[512,768]{1,0:T(8,128)(2,1)}, u32[]{:S(2)}, u32[]{:S(2)}) collective-permute-start(bf16[512,768]{1,0:T(8,128)(2,1)S(1)} %copy-done.32), channel_id=1, source_target_pairs={{0,1},{1,0},{2,3},{3,2},{4,5},{5,4},{6,7},{7,6},{8,9},{9,8},{10,11... | collective-permute-start | bytes 2359304 | tf_op jit(solution)/shard_map/ppermute | solution.py:30
  282.4 20.8 %collective-permute-start.23 = (bf16[512,768]{1,0:T(8,128)(2,1)}, bf16[512,768]{1,0:T(8,128)(2,1)}, u32[]{:S(2)}, u32[]{:S(2)}) collective-permute-start(bf16[512,768]{1,0:T(8,128)(2,1)} %get-tuple-element.286), channel_id=1, source_target_pairs={{0,2},{2,0},{1,3},{3,1},{4,6},{6,4},{5,7},{7,5},{8,10},{10,8},{9,1... | collective-permute-start | bytes 2359304 | tf_op jit(solution)/shard_map/ppermute | solution.py:30
  285.0 32.7 %collective-permute-start.22 = (bf16[512,768]{1,0:T(8,128)(2,1)S(1)}, bf16[512,768]{1,0:T(8,128)(2,1)}, u32[]{:S(2)}, u32[]{:S(2)}) collective-permute-start(bf16[512,768]{1,0:T(8,128)(2,1)S(1)} %add_convert_fusion.4), channel_id=1, source_target_pairs={{0,1},{1,0},{2,3},{3,2},{4,5},{5,4},{6,7},{7,6},{8,9},{9,8},{10,11... | collective-permute-start | bytes 2359304 | tf_op jit(solution)/shard_map/ppermute | solution.py:30
  287.3 31.9 %collective-permute-start.25 = (bf16[512,768]{1,0:T(8,128)(2,1)}, bf16[512,768]{1,0:T(8,128)(2,1)S(1)}, u32[]{:S(2)}, u32[]{:S(2)}) collective-permute-start(bf16[512,768]{1,0:T(8,128)(2,1)} %add_convert_fusion.3), channel_id=1, source_target_pairs={{0,4},{4,0},{1,5},{5,1},{2,6},{6,2},{3,7},{7,3},{8,12},{12,8},{9,1... | collective-permute-start | bytes 2359304 | tf_op jit(solution)/shard_map/ppermute | solution.py:30
  302.3 16.8 %collective-permute-start.21 = (bf16[24,1664]{1,0:T(8,128)(2,1)S(1)}, bf16[24,1664]{1,0:T(8,128)(2,1)S(1)}, u32[]{:S(2)}, u32[]{:S(2)}) collective-permute-start(bf16[24,1664]{1,0:T(8,128)(2,1)S(1)} %reduce_sum.12), channel_id=1, source_target_pairs={{0,64},{64,0},{1,65},{65,1},{2,66},{66,2},{3,67},{67,3},{4,68},{68... | collective-permute-start | bytes 239624 | tf_op jit(solution)/shard_map/ppermute | solution.py:30
  319.4 12.3 %collective-permute-start.28 = (bf16[384,3072]{1,0:T(8,128)(2,1)}, bf16[384,3072]{1,0:T(8,128)(2,1)}, u32[]{:S(2)}, u32[]{:S(2)}) collective-permute-start(bf16[384,3072]{1,0:T(8,128)(2,1)} %all-gather.2.cloned.1.call-done.mine_ref), channel_id=1, source_target_pairs={{0,2},{2,0},{1,3},{3,1},{4,6},{6,4},{5,7},{7,5},{8,10},{10,8},{9,1... | collective-permute-start | bytes 7077896 | tf_op jit(solution)/shard_map/ppermute | solution.py:30
  321.8 26.9 %all-to-all-start.4 = ((bf16[16,24,1664]{2,1,0:T(8,128)(2,1)}), bf16[16,24,1664]{2,1,0:T(8,128)(2,1)S(1)}, u32[]{:S(2)}, u32[]{:S(2)}) async-start(bf16[16,24,1664]{2,1,0:T(8,128)(2,1)} %broadcast_in_dim.48), calls=%async_computation.6 | async-start | bytes 2555904 | tf_op jit(solution)/shard_map/all_to_all | solution.py:34
  328.6 19.2 %collective-permute-start.26 = (bf16[512,768]{1,0:T(8,128)(2,1)S(1)}, bf16[512,768]{1,0:T(8,128)(2,1)}, u32[]{:S(2)}, u32[]{:S(2)}) collective-permute-start(bf16[512,768]{1,0:T(8,128)(2,1)S(1)} %add_convert_fusion.2.mine_ref), channel_id=1, source_target_pairs={{0,1},{1,0},{2,3},{3,2},{4,5},{5,4},{6,7},{7,6},{8,9},{9,8},{10,11... | collective-permute-start | bytes 2359304 | tf_op jit(solution)/shard_map/ppermute | solution.py:30
  350.2 11.0 %collective-permute-start.30 = (bf16[256,768]{1,0:T(8,128)(2,1)}, bf16[256,768]{1,0:T(8,128)(2,1)S(1)}, u32[]{:S(2)}, u32[]{:S(2)}) collective-permute-start(bf16[256,768]{1,0:T(8,128)(2,1)} %copy-done.33), channel_id=1, source_target_pairs={{0,4},{4,0},{1,5},{5,1},{2,6},{6,2},{3,7},{7,3},{8,12},{12,8},{9,1... | collective-permute-start | bytes 1179656 | tf_op jit(solution)/shard_map/ppermute | solution.py:30
  (57 other events, 404.4 us)
Sparse Core Ops, SparseCore 0:
  166.6 29.1 reduce-scatter.2
  198.2 29.0 reduce-scatter.4
  259.3 56.9 all-gather.1
